TPU v7x, 32 devices: a whole 2x2x4 slice. The times are simulated.
32 devices in a mesh: groups: 2 (over y), replay: 4 (over z), module: 2 (over x), half: 2 (over core).
Axes of the slice: x: 2, y: 2, z: 4, core: 2. Of those that a mesh axis runs over, the one named last changes fastest.
Arguments:
- new_factors: bfloat16 [128, 2, 64, 128], P(('groups', 'replay', 'module')), parts along dimension 0, may hold values from -0.5 to 0.5
- new_counts: int32 [128], P(('groups', 'replay', 'module')), parts along dimension 0, may hold values from 32 to 64
- new_ids: int32 [128], P(('groups', 'module', 'half')), parts along dimension 0, may hold values from 0 to 3071
- replay_grads: bfloat16 [6144, 2, 4096], P(('groups', 'replay'), 'module', 'half'), parts along dimension 0, may hold values from -0.75 to 0.75
- replay_ids: int32 [6144], P(('groups', 'replay')), parts along dimension 0, may hold values from 0 to 3071
- slot_module: int32 [2], replicated, may hold values from 0 to 1, each once
- output_inverse: float32 [2, 64, 64], replicated, as said below
- input_inverse: float32 [2, 64, 64], replicated, as said below
Outputs:
- scores: float32 [128, 3072], P(('groups', 'module', 'half'), 'replay'), parts along dimension 0
There are 2 independent parts, one for each index of `groups`. A program takes and returns all parts, laid end to end along the dimension named above; an argument that names none is the same for every part. Nothing has to cross between parts.
Inputs may be any that keep to these rules, and one draw needn't show every extreme that they name: `new_counts`: each new example has at least half of its token slots live, the live ones first. `slot_module`: each module sits in exactly one slot. `output_inverse`: symmetric with a positive diagonal. `input_inverse`: symmetric with a positive diagonal.
All inputs are finite; a program needn't handle non-finite values.
Results may differ from a plain program's by a relative error of at most 0.0029.
Values may be sent and summed in bfloat16 or wider, within the bound.
No kernel may reach another device: no remote copies, remote signals or barrier semaphores. Data moves between devices by JAX's collectives and lax.ppermute only.
A program may use at most 64 MiB of HBM per device.

v0:
```python
import functools

import jax
import jax.numpy as jnp
from jax import lax
from jax.experimental import pallas as pl
from jax.experimental.pallas import tpu as pltpu
from jax.sharding import PartitionSpec as P

LANES = 128


def partner(place, step, count):
    if count & (count - 1) == 0:
        return place ^ step
    return lax.rem(place + step, count) if isinstance(place, jax.Array) else (place + step) % count


def origin(place, step, count):
    return partner(place, step if count & (count - 1) == 0 else (count - step) % count, count)


def exchange(value, names, counts, steps):
    pairs = [
        (a * counts[1] + b, partner(a, steps[0], counts[0]) * counts[1] + partner(b, steps[1], counts[1]))
        for a in range(counts[0])
        for b in range(counts[1])
    ]
    return lax.ppermute(value, names, pairs)


def split(value):
    high = value.astype(jnp.bfloat16)
    return high, (value - high.astype(jnp.float32)).astype(jnp.bfloat16)


def precondition_kernel(
    counts_in,
    slots_in,
    factors_in,
    output_inverse_in,
    input_inverse_in,
    replay_in,
    replay_rows,
    *rest,
):
    counts, slots, factors, output_inverse, input_inverse, arrived = rest[-6:]
    rows = rest[:-6]
    copies_in = [
        pltpu.make_async_copy(source, target, arrived.at[number])
        for number, (source, target) in enumerate(
            (
                (slots_in, slots),
                (counts_in, counts),
                (input_inverse_in, input_inverse),
                (output_inverse_in, output_inverse),
                (factors_in, factors),
                (replay_in, replay_rows),
            )
        )
    ]
    for copy_in in copies_in:
        copy_in.start()

    examples, modules, tokens, width = factors.shape
    features = width // 2
    share = rows[0].shape[1] // features
    pack = LANES // features
    groups = share // pack
    module_place = lax.axis_index("module")
    first_row = pl.multiple_of(lax.axis_index("half") * share, 8)
    for copy_in in copies_in[:-1]:
        copy_in.wait()

    place = (examples, examples * tokens)
    example = lax.broadcasted_iota(jnp.int32, place, 0)
    column = lax.broadcasted_iota(jnp.int32, place, 1)
    kept = jnp.zeros(place, jnp.bool_)
    for e in range(examples):
        kept |= (example == e) & (column >= e * tokens) & (column < e * tokens + counts[e])
    lane = lax.broadcasted_iota(jnp.int32, (examples * tokens, LANES), 1)

    for step in reversed(range(modules)):
        module = slots[partner(module_place, step, modules)]
        tokens_in = factors[:, pl.ds(module, 1)].reshape(examples * tokens, width)
        twice = jnp.concatenate([tokens_in, tokens_in], axis=1)

        right = input_inverse[module]
        right = jnp.concatenate([right] * pack, axis=1)
        right = jnp.concatenate([right, jnp.zeros((features, LANES), jnp.float32)], axis=0)
        right = jnp.concatenate(split(right), axis=0)
        inner = jnp.dot(twice, right, preferred_element_type=jnp.float32)

        left = output_inverse[module, pl.ds(first_row, share)]
        left = jnp.concatenate([jnp.zeros((share, features), jnp.float32), left], axis=1)
        left = jnp.concatenate(
            [
                jnp.broadcast_to(left[pack * q + p : pack * q + p + 1], (examples, width))
                for p in range(pack)
                for q in range(groups)
            ],
            axis=0,
        )
        left = jnp.concatenate(split(left), axis=1)
        outer = lax.dot_general(
            left, twice, (((1,), (1,)), ((), ())), preferred_element_type=jnp.float32
        )
        outer = outer.reshape(pack * groups, examples, examples * tokens)
        outer = jnp.where(kept[None], outer, 0.0).reshape(pack * groups * examples, -1)

        total = jnp.zeros((groups * examples, LANES), jnp.float32)
        for p in range(pack):
            outer_high, outer_low = split(outer[p * groups * examples : (p + 1) * groups * examples])
            mine = (lane >= p * features) & (lane < (p + 1) * features)
            inner_high, inner_low = split(jnp.where(mine, inner, 0.0))
            for one, other in (
                (outer_high, inner_high),
                (outer_high, inner_low),
                (outer_low, inner_high),
            ):
                total += jnp.dot(one, other, preferred_element_type=jnp.float32)
        total = total.astype(jnp.bfloat16)
        for q in range(groups):
            rows[step][:, q * LANES : (q + 1) * LANES] = total[q * examples : (q + 1) * examples]
    copies_in[-1].wait()


def score_kernel(replay_count, module_count, half_count, *refs):
    block_count = replay_count * module_count
    blocks, replay_rows = refs[:block_count], refs[block_count]
    chunks, (joined, partials) = refs[block_count + 1 : -2], refs[-2:]
    examples = blocks[0].shape[0]
    replay_place = lax.axis_index("replay")
    module_place = lax.axis_index("module")
    half_place = lax.axis_index("half")

    per_group = joined.shape[1] // examples
    for group in range(joined.shape[0]):
        joined[group] = jnp.concatenate(
            [
                block[...].astype(jnp.float32)
                for block in blocks[group * per_group : (group + 1) * per_group]
            ],
            axis=0,
        ).astype(jnp.bfloat16)

    def one_group(group, carry):
        product = lax.dot_general(
            joined[group],
            replay_rows[...],
            (((1,), (1,)), ((), ())),
            preferred_element_type=jnp.float32,
        )
        for number in range(per_group):
            step = group * per_group + number
            source = origin(replay_place, step // module_count, replay_count) * module_count + origin(
                module_place, step % module_count, module_count
            )
            partials[source] = product[number * examples : (number + 1) * examples]
        return carry

    if joined.shape[0] == 1:
        one_group(0, 0)
    else:
        lax.fori_loop(0, joined.shape[0], one_group, 0)

    share = block_count // (module_count * half_count)
    for step, chunk in enumerate(chunks):
        target = partner(module_place, step // half_count, module_count) * half_count + partner(
            half_place, step % half_count, half_count
        )
        value = partials[pl.ds(target * share, share)]
        chunk[...] = value.reshape(chunk.shape).astype(chunk.dtype)


def body(
    new_factors,
    new_counts,
    new_ids,
    replay_grads,
    replay_ids,
    slot_module,
    output_inverse,
    input_inverse,
):
    examples, module_count = new_factors.shape[:2]
    replay_total, _, depth = replay_grads.shape
    replay_count = lax.axis_size("replay")
    half_count = lax.axis_size("half")
    holders = module_count * half_count
    blocks = replay_count * module_count
    vmem = pl.BlockSpec(memory_space=pltpu.VMEM)
    hbm = pl.BlockSpec(memory_space=pltpu.HBM)

    operands = (
        new_counts,
        slot_module,
        new_factors,
        output_inverse,
        input_inverse,
        replay_grads.reshape(replay_total, depth),
    )
    replay_rows, *outgoing = pl.pallas_call(
        precondition_kernel,
        out_shape=[pltpu.VMEM((replay_total, depth), jnp.bfloat16)]
        + [pltpu.VMEM((examples, depth), jnp.bfloat16)] * module_count,
        in_specs=[hbm] * len(operands),
        out_specs=[vmem] * (1 + module_count),
        scratch_shapes=[
            pltpu.SMEM(new_counts.shape, jnp.int32),
            pltpu.SMEM(slot_module.shape, jnp.int32),
            pltpu.VMEM(new_factors.shape, jnp.bfloat16),
            pltpu.VMEM(output_inverse.shape, jnp.float32),
            pltpu.VMEM(input_inverse.shape, jnp.float32),
            pltpu.SemaphoreType.DMA((len(operands),)),
        ],
        compiler_params=pltpu.CompilerParams(vmem_limit_bytes=16 * 2**20),
    )(*[pltpu.with_memory_space_constraint(operand, pltpu.HBM) for operand in operands])

    gathered = [None] * blocks
    gathered[0] = outgoing[0]
    for step in range(blocks - 1, 0, -1):
        steps = step // module_count, step % module_count
        gathered[step] = exchange(
            outgoing[steps[1]], ("replay", "module"), (replay_count, module_count), steps
        )

    rows = blocks * examples
    group_rows = min(rows, 64)
    shape = (rows // holders, replay_total)
    chunks = pl.pallas_call(
        functools.partial(score_kernel, replay_count, module_count, half_count),
        out_shape=[pltpu.VMEM(shape, jnp.float32)]
        + [pltpu.VMEM(shape, jnp.bfloat16)] * (holders - 1),
        in_specs=[vmem] * (blocks + 1),
        out_specs=[vmem] * holders,
        scratch_shapes=[
            pltpu.VMEM((rows // group_rows, group_rows, depth), jnp.bfloat16),
            pltpu.VMEM((blocks, examples, replay_total), jnp.float32),
        ],
        compiler_params=pltpu.CompilerParams(vmem_limit_bytes=24 * 2**20),
        cost_estimate=pl.CostEstimate(
            flops=2 * rows * replay_total * depth,
            bytes_accessed=2 * (rows + replay_total) * depth + 4 * rows * replay_total,
            transcendentals=0,
        ),
    )(*gathered, replay_rows)

    summed_scores = chunks[0]
    for step in range(holders - 1, 0, -1):
        steps = step // half_count, step % half_count
        term = exchange(chunks[step], ("module", "half"), (module_count, half_count), steps)
        summed_scores = summed_scores + term.astype(jnp.float32)
    self_pairs = new_ids[:, None] == replay_ids[None, :]
    return jnp.where(self_pairs, jnp.zeros((), jnp.float32), summed_scores)


def solution(mesh):
    in_specs = (
        P(("groups", "replay", "module"), None, None, None),
        P(("groups", "replay", "module")),
        P(("groups", "module", "half")),
        P(("groups", "replay"), "module", "half"),
        P(("groups", "replay")),
        P(),
        P(),
        P(),
    )
    out_specs = P(("groups", "module", "half"), "replay")
    return jax.shard_map(body, mesh=mesh, in_specs=in_specs, out_specs=out_specs, check_vma=False)
```

profile of v0, /device:TPU:0, one launch (start us, length us, event | category | flops | bytes accessed | tf_op | source)
XLA Modules:
  0.0 24.4 jit_solution(9014821273545708330)
XLA Ops:
  0.0 0.0 copy-start
  0.0 0.0 copy-start.1
  0.0 2.3 %shard_map.82 = (bf16[768,2048]{1,0:T(8,128)(2,1)S(1)}, bf16[8,2048]{1,0:T(8,128)(2,1)S(1)}, bf16[8,2048]{1,0:T(8,128)(2,1)S(1)}) custom-call(s32[8]{0:T(128)} %counts_in.1, s32[2]{0:T(128)} %slots_in.1, bf16[8,2,64,128]{3,2,1,0:T(8,128)(2,1)} %factors_in.1, f32[2,64,64]{2,1,0:T(8,128)} %output_inverse_in.1, f32[2,64,64]{2,1,0:T(8,128)} %input_inverse_in.1, ...), custom_call_target="tpu_custom_call" | custom-call | tf_op jit(solution)/shard_map/pallas_call | solution.py:203
  2.3 5.1 %collective-permute-start.5 = (bf16[8,2048]{1,0:T(8,128)(2,1)S(1)}, bf16[8,2048]{1,0:T(8,128)(2,1)S(1)}, u32[]{:S(2)}, u32[]{:S(2)}) collective-permute-start(bf16[8,2048]{1,0:T(8,128)(2,1)S(1)} %get-tuple-element.12.refs_0_), channel_id=1, source_target_pairs={{0,12},{2,14},{4,8},{6,10},{8,4},{10,6},{12,0},{14,2},{1,13},{3,15... | collective-permute-start | bytes 98312 | tf_op jit(solution)/shard_map/ppermute | solution.py:29
  7.4 0.0 collective-permute-start.3
  7.4 0.6 %collective-permute-start.1 = (bf16[8,2048]{1,0:T(8,128)(2,1)S(1)}, bf16[8,2048]{1,0:T(8,128)(2,1)S(1)}, u32[]{:S(2)}, u32[]{:S(2)}) collective-permute-start(bf16[8,2048]{1,0:T(8,128)(2,1)S(1)} %get-tuple-element.12.refs_0_), channel_id=1, source_target_pairs={{0,4},{2,6},{4,0},{6,2},{8,12},{10,14},{12,8},{14,10},{1,5},{3,7},... | collective-permute-start | bytes 98312 | tf_op jit(solution)/shard_map/ppermute | solution.py:29
  8.0 4.7 %collective-permute-start.6 = (bf16[8,2048]{1,0:T(8,128)(2,1)S(1)}, bf16[8,2048]{1,0:T(8,128)(2,1)S(1)}, u32[]{:S(2)}, u32[]{:S(2)}) collective-permute-start(bf16[8,2048]{1,0:T(8,128)(2,1)S(1)} %get-tuple-element.13), channel_id=1, source_target_pairs={{0,14},{2,12},{4,10},{6,8},{8,6},{10,4},{12,2},{14,0},{1,15},{3,13... | collective-permute-start | bytes 98312 | tf_op jit(solution)/shard_map/ppermute | solution.py:29
  12.7 0.0 collective-permute-start.4
  12.7 0.0 collective-permute-done.5.refs_6_
  12.7 1.7 %collective-permute-start.2 = (bf16[8,2048]{1,0:T(8,128)(2,1)S(1)}, bf16[8,2048]{1,0:T(8,128)(2,1)S(1)}, u32[]{:S(2)}, u32[]{:S(2)}) collective-permute-start(bf16[8,2048]{1,0:T(8,128)(2,1)S(1)} %get-tuple-element.13), channel_id=1, source_target_pairs={{0,6},{2,4},{4,2},{6,0},{8,14},{10,12},{12,10},{14,8},{1,7},{3,5},... | collective-permute-start | bytes 98312 | tf_op jit(solution)/shard_map/ppermute | solution.py:29
  14.4 0.0 collective-permute-done.3.refs_4_
  14.4 0.4 %collective-permute-start = (bf16[8,2048]{1,0:T(8,128)(2,1)S(1)}, bf16[8,2048]{1,0:T(8,128)(2,1)S(1)}, u32[]{:S(2)}, u32[]{:S(2)}) collective-permute-start(bf16[8,2048]{1,0:T(8,128)(2,1)S(1)} %get-tuple-element.13), channel_id=1, source_target_pairs={{0,2},{2,0},{4,6},{6,4},{8,10},{10,8},{12,14},{14,12},{1,3},{3,1},... | collective-permute-start | bytes 98312 | tf_op jit(solution)/shard_map/ppermute | solution.py:29
  14.8 0.0 collective-permute-done.1.refs_2_
  14.8 0.6 %collective-permute-done.6.refs_7_ = bf16[8,2048]{1,0:T(8,128)(2,1)S(1)} collective-permute-done((bf16[8,2048]{1,0:T(8,128)(2,1)S(1)}, bf16[8,2048]{1,0:T(8,128)(2,1)S(1)}, u32[]{:S(2)}, u32[]{:S(2)}) %collective-permute-start.6) | collective-permute-done | bytes 32800 | tf_op jit(solution)/shard_map/ppermute | solution.py:29
  15.4 3.1 %collective-permute-done.4.refs_5_ = bf16[8,2048]{1,0:T(8,128)(2,1)S(1)} collective-permute-done((bf16[8,2048]{1,0:T(8,128)(2,1)S(1)}, bf16[8,2048]{1,0:T(8,128)(2,1)S(1)}, u32[]{:S(2)}, u32[]{:S(2)}) %collective-permute-start.4) | collective-permute-done | bytes 32800 | tf_op jit(solution)/shard_map/ppermute | solution.py:29
  18.5 0.0 collective-permute-done.2.refs_3_
  18.5 0.1 collective-permute-done.refs_1_
  18.7 1.1 %shard_map.83 = (f32[16,768]{1,0:T(8,128)S(1)}, bf16[16,768]{1,0:T(8,128)(2,1)S(1)}, bf16[16,768]{1,0:T(8,128)(2,1)S(1)}, bf16[16,768]{1,0:T(8,128)(2,1)S(1)}) custom-call(bf16[8,2048]{1,0:T(8,128)(2,1)S(1)} %get-tuple-element.12.refs_0_, bf16[8,2048]{1,0:T(8,128)(2,1)S(1)} %collective-permute-done.refs_1_, ...), custom_call_target="tpu_custom_call" | custom-call | flops 201326592 | bytes 3604480 | tf_op jit(solution)/shard_map/pallas_call | solution.py:231
  19.8 0.1 collective-permute-start.7
  19.8 0.5 %collective-permute-start.8 = (bf16[16,768]{1,0:T(8,128)(2,1)S(1)}, bf16[16,768]{1,0:T(8,128)(2,1)S(1)}, u32[]{:S(2)}, u32[]{:S(2)}) collective-permute-start(bf16[16,768]{1,0:T(8,128)(2,1)S(1)} %get-tuple-element.17), channel_id=1, source_target_pairs={{0,2},{1,3},{2,0},{3,1},{4,6},{5,7},{6,4},{7,5},{8,10},{9,11},{10,... | collective-permute-start | bytes 73736 | tf_op jit(solution)/shard_map/ppermute | solution.py:29
  20.3 1.4 %collective-permute-start.9 = (bf16[16,768]{1,0:T(8,128)(2,1)S(1)}, bf16[16,768]{1,0:T(8,128)(2,1)S(1)}, u32[]{:S(2)}, u32[]{:S(2)}) collective-permute-start(bf16[16,768]{1,0:T(8,128)(2,1)S(1)} %get-tuple-element.18), channel_id=1, source_target_pairs={{0,1},{1,0},{2,3},{3,2},{4,5},{5,4},{6,7},{7,6},{8,9},{9,8},{10,11... | collective-permute-start | bytes 73736 | tf_op jit(solution)/shard_map/ppermute | solution.py:29
  21.7 1.4 %collective-permute-done.7 = bf16[16,768]{1,0:T(8,128)(2,1)S(1)} collective-permute-done((bf16[16,768]{1,0:T(8,128)(2,1)S(1)}, bf16[16,768]{1,0:T(8,128)(2,1)S(1)}, u32[]{:S(2)}, u32[]{:S(2)}) %collective-permute-start.7) | collective-permute-done | bytes 24608 | tf_op jit(solution)/shard_map/ppermute | solution.py:29
  23.1 0.7 %collective-permute-done.8 = bf16[16,768]{1,0:T(8,128)(2,1)S(1)} collective-permute-done((bf16[16,768]{1,0:T(8,128)(2,1)S(1)}, bf16[16,768]{1,0:T(8,128)(2,1)S(1)}, u32[]{:S(2)}, u32[]{:S(2)}) %collective-permute-start.8) | collective-permute-done | bytes 24608 | tf_op jit(solution)/shard_map/ppermute | solution.py:29
  23.7 0.0 collective-permute-done.9
  23.7 0.0 copy-done
  23.7 0.0 copy-done.1
  23.7 0.7 %add_select_fusion = f32[16,768]{1,0:T(8,128)} fusion(bf16[16,768]{1,0:T(8,128)(2,1)S(1)} %collective-permute-done.9, bf16[16,768]{1,0:T(8,128)(2,1)S(1)} %collective-permute-done.8, f32[16,768]{1,0:T(8,128)S(1)} %get-tuple-element.15, bf16[16,768]{1,0:T(8,128)(2,1)S(1)} %collective-permute-done.7, s32[768]{0:T(1024)S(1)} %copy-done, s32[16]{0:T(128)S(1)} %copy-done.1), kind=kLoop, calls=%fused_computation | loop fusion | flops 98304 | bytes 175168 | tf_op jit(solution)/shard_map/jit(_where)/select_n | solution.py:255
Async XLA Ops:
  0.0 23.7 %copy-start = (s32[768]{0:T(1024)S(1)}, s32[768]{0:T(1024)}, u32[]{:S(2)}) copy-start(s32[768]{0:T(1024)} %param.12) | copy-start | bytes 9220
  0.0 23.7 %copy-start.1 = (s32[16]{0:T(128)S(1)}, s32[16]{0:T(128)}, u32[]{:S(2)}) copy-start(s32[16]{0:T(128)} %param.10) | copy-start | bytes 196
  2.3 10.4 %collective-permute-start.5 = (bf16[8,2048]{1,0:T(8,128)(2,1)S(1)}, bf16[8,2048]{1,0:T(8,128)(2,1)S(1)}, u32[]{:S(2)}, u32[]{:S(2)}) collective-permute-start(bf16[8,2048]{1,0:T(8,128)(2,1)S(1)} %get-tuple-element.12.refs_0_), channel_id=1, source_target_pairs={{0,12},{2,14},{4,8},{6,10},{8,4},{10,6},{12,0},{14,2},{1,13},{3,15... | collective-permute-start | bytes 98312 | tf_op jit(solution)/shard_map/ppermute | solution.py:29
  7.4 7.0 %collective-permute-start.3 = (bf16[8,2048]{1,0:T(8,128)(2,1)S(1)}, bf16[8,2048]{1,0:T(8,128)(2,1)S(1)}, u32[]{:S(2)}, u32[]{:S(2)}) collective-permute-start(bf16[8,2048]{1,0:T(8,128)(2,1)S(1)} %get-tuple-element.12.refs_0_), channel_id=1, source_target_pairs={{0,8},{2,10},{4,12},{6,14},{8,0},{10,2},{12,4},{14,6},{1,9},{3,11}... | collective-permute-start | bytes 98312 | tf_op jit(solution)/shard_map/ppermute | solution.py:29
  7.4 7.4 %collective-permute-start.1 = (bf16[8,2048]{1,0:T(8,128)(2,1)S(1)}, bf16[8,2048]{1,0:T(8,128)(2,1)S(1)}, u32[]{:S(2)}, u32[]{:S(2)}) collective-permute-start(bf16[8,2048]{1,0:T(8,128)(2,1)S(1)} %get-tuple-element.12.refs_0_), channel_id=1, source_target_pairs={{0,4},{2,6},{4,0},{6,2},{8,12},{10,14},{12,8},{14,10},{1,5},{3,7},... | collective-permute-start | bytes 98312 | tf_op jit(solution)/shard_map/ppermute | solution.py:29
  8.0 7.4 %collective-permute-start.6 = (bf16[8,2048]{1,0:T(8,128)(2,1)S(1)}, bf16[8,2048]{1,0:T(8,128)(2,1)S(1)}, u32[]{:S(2)}, u32[]{:S(2)}) collective-permute-start(bf16[8,2048]{1,0:T(8,128)(2,1)S(1)} %get-tuple-element.13), channel_id=1, source_target_pairs={{0,14},{2,12},{4,10},{6,8},{8,6},{10,4},{12,2},{14,0},{1,15},{3,13... | collective-permute-start | bytes 98312 | tf_op jit(solution)/shard_map/ppermute | solution.py:29
  12.7 5.8 %collective-permute-start.4 = (bf16[8,2048]{1,0:T(8,128)(2,1)S(1)}, bf16[8,2048]{1,0:T(8,128)(2,1)S(1)}, u32[]{:S(2)}, u32[]{:S(2)}) collective-permute-start(bf16[8,2048]{1,0:T(8,128)(2,1)S(1)} %get-tuple-element.13), channel_id=1, source_target_pairs={{0,10},{2,8},{4,14},{6,12},{8,2},{10,0},{12,6},{14,4},{1,11},{3,9}... | collective-permute-start | bytes 98312 | tf_op jit(solution)/shard_map/ppermute | solution.py:29
  12.7 5.8 %collective-permute-start.2 = (bf16[8,2048]{1,0:T(8,128)(2,1)S(1)}, bf16[8,2048]{1,0:T(8,128)(2,1)S(1)}, u32[]{:S(2)}, u32[]{:S(2)}) collective-permute-start(bf16[8,2048]{1,0:T(8,128)(2,1)S(1)} %get-tuple-element.13), channel_id=1, source_target_pairs={{0,6},{2,4},{4,2},{6,0},{8,14},{10,12},{12,10},{14,8},{1,7},{3,5},... | collective-permute-start | bytes 98312 | tf_op jit(solution)/shard_map/ppermute | solution.py:29
  14.4 4.3 %collective-permute-start = (bf16[8,2048]{1,0:T(8,128)(2,1)S(1)}, bf16[8,2048]{1,0:T(8,128)(2,1)S(1)}, u32[]{:S(2)}, u32[]{:S(2)}) collective-permute-start(bf16[8,2048]{1,0:T(8,128)(2,1)S(1)} %get-tuple-element.13), channel_id=1, source_target_pairs={{0,2},{2,0},{4,6},{6,4},{8,10},{10,8},{12,14},{14,12},{1,3},{3,1},... | collective-permute-start | bytes 98312 | tf_op jit(solution)/shard_map/ppermute | solution.py:29
  19.8 3.3 %collective-permute-start.7 = (bf16[16,768]{1,0:T(8,128)(2,1)S(1)}, bf16[16,768]{1,0:T(8,128)(2,1)S(1)}, u32[]{:S(2)}, u32[]{:S(2)}) collective-permute-start(bf16[16,768]{1,0:T(8,128)(2,1)S(1)} %get-tuple-element.16), channel_id=1, source_target_pairs={{0,3},{1,2},{2,1},{3,0},{4,7},{5,6},{6,5},{7,4},{8,11},{9,10},{10,... | collective-permute-start | bytes 73736 | tf_op jit(solution)/shard_map/ppermute | solution.py:29
  19.8 3.9 %collective-permute-start.8 = (bf16[16,768]{1,0:T(8,128)(2,1)S(1)}, bf16[16,768]{1,0:T(8,128)(2,1)S(1)}, u32[]{:S(2)}, u32[]{:S(2)}) collective-permute-start(bf16[16,768]{1,0:T(8,128)(2,1)S(1)} %get-tuple-element.17), channel_id=1, source_target_pairs={{0,2},{1,3},{2,0},{3,1},{4,6},{5,7},{6,4},{7,5},{8,10},{9,11},{10,... | collective-permute-start | bytes 73736 | tf_op jit(solution)/shard_map/ppermute | solution.py:29
  20.3 3.4 %collective-permute-start.9 = (bf16[16,768]{1,0:T(8,128)(2,1)S(1)}, bf16[16,768]{1,0:T(8,128)(2,1)S(1)}, u32[]{:S(2)}, u32[]{:S(2)}) collective-permute-start(bf16[16,768]{1,0:T(8,128)(2,1)S(1)} %get-tuple-element.18), channel_id=1, source_target_pairs={{0,1},{1,0},{2,3},{3,2},{4,5},{5,4},{6,7},{7,6},{8,9},{9,8},{10,11... | collective-permute-start | bytes 73736 | tf_op jit(solution)/shard_map/ppermute | solution.py:29
where the time goes:
time: 24.6 us; the launch traced here: 24.4 us
  starting transfers between devices  14.4 us (59%)
  waiting for transfers between devices  5.92 us (24%)
  Pallas kernels  3.34 us (14%)
  other arithmetic  0.69 us (3%)
    ppermute x10, starting transfers between devices, exchange(): return lax.ppermute(value, names, pairs)  14.4 us
    ppermute x10, waiting for transfers between devices, exchange(): return lax.ppermute(value, names, pairs)  5.92 us
    pallas_call x1, Pallas kernels, body(): pl.pallas_call(precondition_kernel, out_shape=[pltpu.VMEM((replay_total,...  2.26 us
    pallas_call x1, Pallas kernels, body(): pl.pallas_call(functools.partial(score_kernel, replay_count, module_count...  1.08 us
    select_n x1, other arithmetic, body(): return jnp.where(self_pairs, jnp.zeros((), jnp.float32), summed_scores)  0.69 us
  transfers between devices with their start and end apart: 10, of which 5 were waited for; matrix products, arithmetic and copies ran while one was open for 0% of the time, Pallas kernels for 0%

commit v1 on v0

--- a/solution.py
+++ b/solution.py
@@ -1,4 +1,5 @@
 import functools
+import itertools
 
 import jax
 import jax.numpy as jnp
@@ -13,19 +14,23 @@
 def partner(place, step, count):
     if count & (count - 1) == 0:
         return place ^ step
-    return lax.rem(place + step, count) if isinstance(place, jax.Array) else (place + step) % count
+    return (place + step) % count
 
 
 def origin(place, step, count):
-    return partner(place, step if count & (count - 1) == 0 else (count - step) % count, count)
+    if count & (count - 1) == 0:
+        return place ^ step
+    return (place + count - step) % count
 
 
 def exchange(value, names, counts, steps):
-    pairs = [
-        (a * counts[1] + b, partner(a, steps[0], counts[0]) * counts[1] + partner(b, steps[1], counts[1]))
-        for a in range(counts[0])
-        for b in range(counts[1])
-    ]
+    pairs = []
+    for place in itertools.product(*[range(count) for count in counts]):
+        source = target = 0
+        for spot, count, step in zip(place, counts, steps(place[-1])):
+            source = source * count + spot
+            target = target * count + partner(spot, step, count)
+        pairs.append((source, target))
     return lax.ppermute(value, names, pairs)
 
 
@@ -64,11 +69,12 @@
 
     examples, modules, tokens, width = factors.shape
     features = width // 2
-    share = rows[0].shape[1] // features
+    halves = rows[0].shape[0]
     pack = LANES // features
-    groups = share // pack
+    groups = features // pack
+    share = groups // halves
     module_place = lax.axis_index("module")
-    first_row = pl.multiple_of(lax.axis_index("half") * share, 8)
+    half_place = lax.axis_index("half")
     for copy_in in copies_in[:-1]:
         copy_in.wait()
 
@@ -80,8 +86,8 @@
         kept |= (example == e) & (column >= e * tokens) & (column < e * tokens + counts[e])
     lane = lax.broadcasted_iota(jnp.int32, (examples * tokens, LANES), 1)
 
-    for step in reversed(range(modules)):
-        module = slots[partner(module_place, step, modules)]
+    for turn, target in enumerate(rows):
+        module = slots[partner(module_place, turn * halves + half_place, modules)]
         tokens_in = factors[:, pl.ds(module, 1)].reshape(examples * tokens, width)
         twice = jnp.concatenate([tokens_in, tokens_in], axis=1)
 
@@ -91,8 +97,8 @@
         right = jnp.concatenate(split(right), axis=0)
         inner = jnp.dot(twice, right, preferred_element_type=jnp.float32)
 
-        left = output_inverse[module, pl.ds(first_row, share)]
-        left = jnp.concatenate([jnp.zeros((share, features), jnp.float32), left], axis=1)
+        left = output_inverse[module]
+        left = jnp.concatenate([jnp.zeros((features, features), jnp.float32), left], axis=1)
         left = jnp.concatenate(
             [
                 jnp.broadcast_to(left[pack * q + p : pack * q + p + 1], (examples, width))
@@ -121,15 +127,16 @@
                 total += jnp.dot(one, other, preferred_element_type=jnp.float32)
         total = total.astype(jnp.bfloat16)
         for q in range(groups):
-            rows[step][:, q * LANES : (q + 1) * LANES] = total[q * examples : (q + 1) * examples]
+            block = total[q * examples : (q + 1) * examples]
+            target[q // share, :, q % share * LANES : (q % share + 1) * LANES] = block
     copies_in[-1].wait()
 
 
-def score_kernel(replay_count, module_count, half_count, *refs):
-    block_count = replay_count * module_count
-    blocks, replay_rows = refs[:block_count], refs[block_count]
-    chunks, (joined, partials) = refs[block_count + 1 : -2], refs[-2:]
-    examples = blocks[0].shape[0]
+def score_kernel(sources, holders, *refs):
+    blocks, replay_rows = refs[: len(sources)], refs[len(sources)]
+    chunks, (joined, partials) = refs[len(sources) + 1 : -2], refs[-2:]
+    replay_count, module_count, half_count = holders
+    examples = blocks[0].shape[1]
     replay_place = lax.axis_index("replay")
     module_place = lax.axis_index("module")
     half_place = lax.axis_index("half")
@@ -138,13 +145,21 @@
     for group in range(joined.shape[0]):
         joined[group] = jnp.concatenate(
             [
-                block[...].astype(jnp.float32)
+                block[half_place].astype(jnp.float32)
                 for block in blocks[group * per_group : (group + 1) * per_group]
             ],
             axis=0,
         ).astype(jnp.bfloat16)
 
-    def one_group(group, carry):
+    def place_of(number):
+        replay_step, turn, half_step = sources[number]
+        handler = origin(half_place, half_step, half_count)
+        module_step = turn * half_count + handler
+        return origin(replay_place, replay_step, replay_count) * module_count + origin(
+            module_place, module_step, module_count
+        )
+
+    for group in range(joined.shape[0]):
         product = lax.dot_general(
             joined[group],
             replay_rows[...],
@@ -152,19 +167,11 @@
             preferred_element_type=jnp.float32,
         )
         for number in range(per_group):
-            step = group * per_group + number
-            source = origin(replay_place, step // module_count, replay_count) * module_count + origin(
-                module_place, step % module_count, module_count
-            )
-            partials[source] = product[number * examples : (number + 1) * examples]
-        return carry
-
-    if joined.shape[0] == 1:
-        one_group(0, 0)
-    else:
-        lax.fori_loop(0, joined.shape[0], one_group, 0)
-
-    share = block_count // (module_count * half_count)
+            partials[place_of(group * per_group + number)] = product[
+                number * examples : (number + 1) * examples
+            ]
+
+    share = len(sources) // (module_count * half_count)
     for step, chunk in enumerate(chunks):
         target = partner(module_place, step // half_count, module_count) * half_count + partner(
             half_place, step % half_count, half_count
@@ -189,6 +196,7 @@
     half_count = lax.axis_size("half")
     holders = module_count * half_count
     blocks = replay_count * module_count
+    turns = module_count // half_count
     vmem = pl.BlockSpec(memory_space=pltpu.VMEM)
     hbm = pl.BlockSpec(memory_space=pltpu.HBM)
 
@@ -203,9 +211,9 @@
     replay_rows, *outgoing = pl.pallas_call(
         precondition_kernel,
         out_shape=[pltpu.VMEM((replay_total, depth), jnp.bfloat16)]
-        + [pltpu.VMEM((examples, depth), jnp.bfloat16)] * module_count,
+        + [pltpu.VMEM((half_count, examples, depth), jnp.bfloat16)] * turns,
         in_specs=[hbm] * len(operands),
-        out_specs=[vmem] * (1 + module_count),
+        out_specs=[vmem] * (1 + turns),
         scratch_shapes=[
             pltpu.SMEM(new_counts.shape, jnp.int32),
             pltpu.SMEM(slot_module.shape, jnp.int32),
@@ -217,19 +225,25 @@
         compiler_params=pltpu.CompilerParams(vmem_limit_bytes=16 * 2**20),
     )(*[pltpu.with_memory_space_constraint(operand, pltpu.HBM) for operand in operands])
 
-    gathered = [None] * blocks
-    gathered[0] = outgoing[0]
-    for step in range(blocks - 1, 0, -1):
-        steps = step // module_count, step % module_count
-        gathered[step] = exchange(
-            outgoing[steps[1]], ("replay", "module"), (replay_count, module_count), steps
-        )
+    axes = ("replay", "module", "half")
+    counts = (replay_count, module_count, half_count)
+    gathered = {}
+    for replay_step in range(replay_count - 1, -1, -1):
+        for turn in range(turns):
+            gathered[replay_step, turn, 0] = exchange(
+                outgoing[turn], axes, counts, lambda half: (replay_step, turn * half_count + half, 0)
+            )
+    for replay_step, turn, _ in list(gathered):
+        for half_step in range(1, half_count):
+            gathered[replay_step, turn, half_step] = exchange(
+                gathered[replay_step, turn, 0], ("half",), (half_count,), lambda half: (half_step,)
+            )
 
     rows = blocks * examples
     group_rows = min(rows, 64)
     shape = (rows // holders, replay_total)
     chunks = pl.pallas_call(
-        functools.partial(score_kernel, replay_count, module_count, half_count),
+        functools.partial(score_kernel, tuple(gathered), counts),
         out_shape=[pltpu.VMEM(shape, jnp.float32)]
         + [pltpu.VMEM(shape, jnp.bfloat16)] * (holders - 1),
         in_specs=[vmem] * (blocks + 1),
@@ -244,12 +258,13 @@
             bytes_accessed=2 * (rows + replay_total) * depth + 4 * rows * replay_total,
             transcendentals=0,
         ),
-    )(*gathered, replay_rows)
+    )(*gathered.values(), replay_rows)
 
     summed_scores = chunks[0]
     for step in range(holders - 1, 0, -1):
-        steps = step // half_count, step % half_count
-        term = exchange(chunks[step], ("module", "half"), (module_count, half_count), steps)
+        term = exchange(
+            chunks[step], axes[1:], counts[1:], lambda half: (step // half_count, step % half_count)
+        )
         summed_scores = summed_scores + term.astype(jnp.float32)
     self_pairs = new_ids[:, None] == replay_ids[None, :]
     return jnp.where(self_pairs, jnp.zeros((), jnp.float32), summed_scores)

time: 24.6 us -> 24.2 us (0.984)
  waiting for transfers between devices: 5.92 us -> 3.89 us
  starting transfers between devices: 14.4 us -> 16.2 us
    ppermute x10 -> x11, waiting for transfers between devices: 5.92 us -> 3.89 us  [exchange(): return lax.ppermute(value, names, pairs)]
    ppermute x10 -> x11, starting transfers between devices: 14.4 us -> 16.2 us  [exchange(): return lax.ppermute(value, names, pairs)]
  transfers between devices with their start and end apart: 10 -> 11, of which waited for: 5 -> 5; matrix products, arithmetic and copies ran while one was open for 0% -> 0% of each run, Pallas kernels for 0% -> 0%
where the time goes in v1:
time: 24.2 us; the launch traced here: 24 us
  starting transfers between devices  16.2 us (67%)
  waiting for transfers between devices  3.89 us (16%)
  Pallas kernels  3.21 us (13%)
  other arithmetic  0.69 us (3%)
    ppermute x11, starting transfers between devices, exchange(): return lax.ppermute(value, names, pairs)  16.2 us
    ppermute x11, waiting for transfers between devices, exchange(): return lax.ppermute(value, names, pairs)  3.89 us
    pallas_call x1, Pallas kernels, body(): pl.pallas_call(precondition_kernel, out_shape=[pltpu.VMEM((replay_total,...  2.13 us
    pallas_call x1, Pallas kernels, body(): pl.pallas_call(functools.partial(score_kernel, tuple(gathered), counts),...  1.08 us
    select_n x1, other arithmetic, body(): return jnp.where(self_pairs, jnp.zeros((), jnp.float32), summed_scores)  0.69 us
  transfers between devices with their start and end apart: 11, of which 5 were waited for; matrix products, arithmetic and copies ran while one was open for 0% of the time, Pallas kernels for 0%

profile of v1, /device:TPU:0, one launch (start us, length us, event | category | flops | bytes accessed | tf_op | source)
XLA Modules:
  0.0 24.0 jit_solution(13569220495140734581)
XLA Ops:
  0.0 0.0 copy-start
  0.0 0.0 copy-start.1
  0.0 2.1 %shard_map.82 = (bf16[768,2048]{1,0:T(8,128)(2,1)S(1)}, bf16[2,8,2048]{2,1,0:T(8,128)(2,1)S(1)}) custom-call(s32[8]{0:T(128)} %counts_in.1, s32[2]{0:T(128)} %slots_in.1, bf16[8,2,64,128]{3,2,1,0:T(8,128)(2,1)} %factors_in.1, f32[2,64,64]{2,1,0:T(8,128)} %output_inverse_in.1, f32[2,64,64]{2,1,0:T(8,128)} %input_inverse_in.1, bf16[768,2048]{1,0:T(8,128)(2,1)} %bitcast.1), custom_call_target="tpu_custom_call" | custom-call | tf_op jit(solution)/shard_map/pallas_call | solution.py:211
  2.1 0.7 %collective-permute-start.3 = (bf16[2,8,2048]{2,1,0:T(8,128)(2,1)S(1)}, bf16[2,8,2048]{2,1,0:T(8,128)(2,1)S(1)}, u32[]{:S(2)}, u32[]{:S(2)}) collective-permute-start(bf16[2,8,2048]{2,1,0:T(8,128)(2,1)S(1)} %get-tuple-element.11), channel_id=1, source_target_pairs={{0,0},{1,3},{2,2},{3,1},{4,4},{5,7},{6,6},{7,5},{8,8},{9,11},{10,1... | collective-permute-start | bytes 196616 | tf_op jit(solution)/shard_map/ppermute | solution.py:34
  2.8 3.1 %collective-permute-start.2 = (bf16[2,8,2048]{2,1,0:T(8,128)(2,1)S(1)}, bf16[2,8,2048]{2,1,0:T(8,128)(2,1)S(1)}, u32[]{:S(2)}, u32[]{:S(2)}) collective-permute-start(bf16[2,8,2048]{2,1,0:T(8,128)(2,1)S(1)} %get-tuple-element.11), channel_id=1, source_target_pairs={{0,4},{1,7},{2,6},{3,5},{4,0},{5,3},{6,2},{7,1},{8,12},{9,15},{10,... | collective-permute-start | bytes 196616 | tf_op jit(solution)/shard_map/ppermute | solution.py:34
  5.9 2.6 %collective-permute-start.1 = (bf16[2,8,2048]{2,1,0:T(8,128)(2,1)S(1)}, bf16[2,8,2048]{2,1,0:T(8,128)(2,1)S(1)}, u32[]{:S(2)}, u32[]{:S(2)}) collective-permute-start(bf16[2,8,2048]{2,1,0:T(8,128)(2,1)S(1)} %get-tuple-element.11), channel_id=1, source_target_pairs={{0,8},{1,11},{2,10},{3,9},{4,12},{5,15},{6,14},{7,13},{8,0},{9,3},... | collective-permute-start | bytes 196616 | tf_op jit(solution)/shard_map/ppermute | solution.py:34
  8.5 0.0 collective-permute-start
  8.5 0.0 collective-permute-done.3.refs_3_
  8.5 2.6 %collective-permute-start.7 = (bf16[2,8,2048]{2,1,0:T(8,128)(2,1)S(1)}, bf16[2,8,2048]{2,1,0:T(8,128)(2,1)S(1)}, u32[]{:S(2)}, u32[]{:S(2)}) collective-permute-start(bf16[2,8,2048]{2,1,0:T(8,128)(2,1)S(1)} %collective-permute-done.3.refs_3_), channel_id=1, source_target_pairs={{0,1},{1,0},{2,3},{3,2},{4,5},{5,4},{6,7},{7,6},{8,9},{9,8},{10,11... | collective-permute-start | bytes 196616 | tf_op jit(solution)/shard_map/ppermute | solution.py:34
  11.1 0.0 collective-permute-done.2.refs_2_
  11.1 0.1 collective-permute-start.6
  11.2 0.6 %collective-permute-done.1.refs_1_ = bf16[2,8,2048]{2,1,0:T(8,128)(2,1)S(1)} collective-permute-done((bf16[2,8,2048]{2,1,0:T(8,128)(2,1)S(1)}, bf16[2,8,2048]{2,1,0:T(8,128)(2,1)S(1)}, u32[]{:S(2)}, u32[]{:S(2)}) %collective-permute-start.1) | collective-permute-done | bytes 65568 | tf_op jit(solution)/shard_map/ppermute | solution.py:34
  11.8 2.8 %collective-permute-start.5 = (bf16[2,8,2048]{2,1,0:T(8,128)(2,1)S(1)}, bf16[2,8,2048]{2,1,0:T(8,128)(2,1)S(1)}, u32[]{:S(2)}, u32[]{:S(2)}) collective-permute-start(bf16[2,8,2048]{2,1,0:T(8,128)(2,1)S(1)} %collective-permute-done.1.refs_1_), channel_id=1, source_target_pairs={{0,1},{1,0},{2,3},{3,2},{4,5},{5,4},{6,7},{7,6},{8,9},{9,8},{10,11... | collective-permute-start | bytes 196616 | tf_op jit(solution)/shard_map/ppermute | solution.py:34
  14.6 0.1 collective-permute-done.refs_0_
  14.7 2.3 %collective-permute-start.4 = (bf16[2,8,2048]{2,1,0:T(8,128)(2,1)S(1)}, bf16[2,8,2048]{2,1,0:T(8,128)(2,1)S(1)}, u32[]{:S(2)}, u32[]{:S(2)}) collective-permute-start(bf16[2,8,2048]{2,1,0:T(8,128)(2,1)S(1)} %collective-permute-done.refs_0_), channel_id=1, source_target_pairs={{0,1},{1,0},{2,3},{3,2},{4,5},{5,4},{6,7},{7,6},{8,9},{9,8},{10,11... | collective-permute-start | bytes 196616 | tf_op jit(solution)/shard_map/ppermute | solution.py:34
  16.9 0.0 collective-permute-done.7.refs_7_
  16.9 0.0 collective-permute-done.6.refs_6_
  16.9 0.0 collective-permute-done.5.refs_5_
  16.9 0.9 %collective-permute-done.4.refs_4_ = bf16[2,8,2048]{2,1,0:T(8,128)(2,1)S(1)} collective-permute-done((bf16[2,8,2048]{2,1,0:T(8,128)(2,1)S(1)}, bf16[2,8,2048]{2,1,0:T(8,128)(2,1)S(1)}, u32[]{:S(2)}, u32[]{:S(2)}) %collective-permute-start.4) | collective-permute-done | bytes 65568 | tf_op jit(solution)/shard_map/ppermute | solution.py:34
  17.8 1.1 %shard_map.83 = (f32[16,768]{1,0:T(8,128)S(1)}, bf16[16,768]{1,0:T(8,128)(2,1)S(1)}, bf16[16,768]{1,0:T(8,128)(2,1)S(1)}, bf16[16,768]{1,0:T(8,128)(2,1)S(1)}) custom-call(bf16[2,8,2048]{2,1,0:T(8,128)(2,1)S(1)} %collective-permute-done.refs_0_, bf16[2,8,2048]{2,1,0:T(8,128)(2,1)S(1)} %collective-permute-done.1.refs_1_, ...), custom_call_target="tpu_custom_call" | custom-call | flops 201326592 | bytes 3604480 | tf_op jit(solution)/shard_map/pallas_call | solution.py:245
  18.9 0.6 %collective-permute-start.8 = (bf16[16,768]{1,0:T(8,128)(2,1)S(1)}, bf16[16,768]{1,0:T(8,128)(2,1)S(1)}, u32[]{:S(2)}, u32[]{:S(2)}) collective-permute-start(bf16[16,768]{1,0:T(8,128)(2,1)S(1)} %get-tuple-element.14), channel_id=1, source_target_pairs={{0,3},{1,2},{2,1},{3,0},{4,7},{5,6},{6,5},{7,4},{8,11},{9,10},{10,... | collective-permute-start | bytes 73736 | tf_op jit(solution)/shard_map/ppermute | solution.py:34
  19.5 1.5 %collective-permute-start.9 = (bf16[16,768]{1,0:T(8,128)(2,1)S(1)}, bf16[16,768]{1,0:T(8,128)(2,1)S(1)}, u32[]{:S(2)}, u32[]{:S(2)}) collective-permute-start(bf16[16,768]{1,0:T(8,128)(2,1)S(1)} %get-tuple-element.15), channel_id=1, source_target_pairs={{0,2},{1,3},{2,0},{3,1},{4,6},{5,7},{6,4},{7,5},{8,10},{9,11},{10,... | collective-permute-start | bytes 73736 | tf_op jit(solution)/shard_map/ppermute | solution.py:34
  21.0 0.0 collective-permute-start.10
  21.0 1.3 %collective-permute-done.8 = bf16[16,768]{1,0:T(8,128)(2,1)S(1)} collective-permute-done((bf16[16,768]{1,0:T(8,128)(2,1)S(1)}, bf16[16,768]{1,0:T(8,128)(2,1)S(1)}, u32[]{:S(2)}, u32[]{:S(2)}) %collective-permute-start.8) | collective-permute-done | bytes 24608 | tf_op jit(solution)/shard_map/ppermute | solution.py:34
  22.3 1.0 %collective-permute-done.9 = bf16[16,768]{1,0:T(8,128)(2,1)S(1)} collective-permute-done((bf16[16,768]{1,0:T(8,128)(2,1)S(1)}, bf16[16,768]{1,0:T(8,128)(2,1)S(1)}, u32[]{:S(2)}, u32[]{:S(2)}) %collective-permute-start.9) | collective-permute-done | bytes 24608 | tf_op jit(solution)/shard_map/ppermute | solution.py:34
  23.3 0.0 collective-permute-done.10
  23.3 0.0 copy-done
  23.3 0.0 copy-done.1
  23.3 0.7 %add_select_fusion = f32[16,768]{1,0:T(8,128)} fusion(bf16[16,768]{1,0:T(8,128)(2,1)S(1)} %collective-permute-done.10, bf16[16,768]{1,0:T(8,128)(2,1)S(1)} %collective-permute-done.9, f32[16,768]{1,0:T(8,128)S(1)} %get-tuple-element.13, bf16[16,768]{1,0:T(8,128)(2,1)S(1)} %collective-permute-done.8, s32[768]{0:T(1024)S(1)} %copy-done, s32[16]{0:T(128)S(1)} %copy-done.1), kind=kLoop, calls=%fused_computation | loop fusion | flops 98304 | bytes 175168 | tf_op jit(solution)/shard_map/jit(_where)/select_n | solution.py:270
Async XLA Ops:
  0.0 23.3 %copy-start = (s32[768]{0:T(1024)S(1)}, s32[768]{0:T(1024)}, u32[]{:S(2)}) copy-start(s32[768]{0:T(1024)} %param.12) | copy-start | bytes 9220
  0.0 23.3 %copy-start.1 = (s32[16]{0:T(128)S(1)}, s32[16]{0:T(128)}, u32[]{:S(2)}) copy-start(s32[16]{0:T(128)} %param.10) | copy-start | bytes 196
  2.1 6.4 %collective-permute-start.3 = (bf16[2,8,2048]{2,1,0:T(8,128)(2,1)S(1)}, bf16[2,8,2048]{2,1,0:T(8,128)(2,1)S(1)}, u32[]{:S(2)}, u32[]{:S(2)}) collective-permute-start(bf16[2,8,2048]{2,1,0:T(8,128)(2,1)S(1)} %get-tuple-element.11), channel_id=1, source_target_pairs={{0,0},{1,3},{2,2},{3,1},{4,4},{5,7},{6,6},{7,5},{8,8},{9,11},{10,1... | collective-permute-start | bytes 196616 | tf_op jit(solution)/shard_map/ppermute | solution.py:34
  2.8 8.3 %collective-permute-start.2 = (bf16[2,8,2048]{2,1,0:T(8,128)(2,1)S(1)}, bf16[2,8,2048]{2,1,0:T(8,128)(2,1)S(1)}, u32[]{:S(2)}, u32[]{:S(2)}) collective-permute-start(bf16[2,8,2048]{2,1,0:T(8,128)(2,1)S(1)} %get-tuple-element.11), channel_id=1, source_target_pairs={{0,4},{1,7},{2,6},{3,5},{4,0},{5,3},{6,2},{7,1},{8,12},{9,15},{10,... | collective-permute-start | bytes 196616 | tf_op jit(solution)/shard_map/ppermute | solution.py:34
  5.9 5.9 %collective-permute-start.1 = (bf16[2,8,2048]{2,1,0:T(8,128)(2,1)S(1)}, bf16[2,8,2048]{2,1,0:T(8,128)(2,1)S(1)}, u32[]{:S(2)}, u32[]{:S(2)}) collective-permute-start(bf16[2,8,2048]{2,1,0:T(8,128)(2,1)S(1)} %get-tuple-element.11), channel_id=1, source_target_pairs={{0,8},{1,11},{2,10},{3,9},{4,12},{5,15},{6,14},{7,13},{8,0},{9,3},... | collective-permute-start | bytes 196616 | tf_op jit(solution)/shard_map/ppermute | solution.py:34
  8.5 6.2 %collective-permute-start = (bf16[2,8,2048]{2,1,0:T(8,128)(2,1)S(1)}, bf16[2,8,2048]{2,1,0:T(8,128)(2,1)S(1)}, u32[]{:S(2)}, u32[]{:S(2)}) collective-permute-start(bf16[2,8,2048]{2,1,0:T(8,128)(2,1)S(1)} %get-tuple-element.11), channel_id=1, source_target_pairs={{0,12},{1,15},{2,14},{3,13},{4,8},{5,11},{6,10},{7,9},{8,4},{9,7},... | collective-permute-start | bytes 196616 | tf_op jit(solution)/shard_map/ppermute | solution.py:34
  8.5 8.4 %collective-permute-start.7 = (bf16[2,8,2048]{2,1,0:T(8,128)(2,1)S(1)}, bf16[2,8,2048]{2,1,0:T(8,128)(2,1)S(1)}, u32[]{:S(2)}, u32[]{:S(2)}) collective-permute-start(bf16[2,8,2048]{2,1,0:T(8,128)(2,1)S(1)} %collective-permute-done.3.refs_3_), channel_id=1, source_target_pairs={{0,1},{1,0},{2,3},{3,2},{4,5},{5,4},{6,7},{7,6},{8,9},{9,8},{10,11... | collective-permute-start | bytes 196616 | tf_op jit(solution)/shard_map/ppermute | solution.py:34
  11.1 5.8 %collective-permute-start.6 = (bf16[2,8,2048]{2,1,0:T(8,128)(2,1)S(1)}, bf16[2,8,2048]{2,1,0:T(8,128)(2,1)S(1)}, u32[]{:S(2)}, u32[]{:S(2)}) collective-permute-start(bf16[2,8,2048]{2,1,0:T(8,128)(2,1)S(1)} %collective-permute-done.2.refs_2_), channel_id=1, source_target_pairs={{0,1},{1,0},{2,3},{3,2},{4,5},{5,4},{6,7},{7,6},{8,9},{9,8},{10,11... | collective-permute-start | bytes 196616 | tf_op jit(solution)/shard_map/ppermute | solution.py:34
  11.8 5.2 %collective-permute-start.5 = (bf16[2,8,2048]{2,1,0:T(8,128)(2,1)S(1)}, bf16[2,8,2048]{2,1,0:T(8,128)(2,1)S(1)}, u32[]{:S(2)}, u32[]{:S(2)}) collective-permute-start(bf16[2,8,2048]{2,1,0:T(8,128)(2,1)S(1)} %collective-permute-done.1.refs_1_), channel_id=1, source_target_pairs={{0,1},{1,0},{2,3},{3,2},{4,5},{5,4},{6,7},{7,6},{8,9},{9,8},{10,11... | collective-permute-start | bytes 196616 | tf_op jit(solution)/shard_map/ppermute | solution.py:34
  14.7 3.2 %collective-permute-start.4 = (bf16[2,8,2048]{2,1,0:T(8,128)(2,1)S(1)}, bf16[2,8,2048]{2,1,0:T(8,128)(2,1)S(1)}, u32[]{:S(2)}, u32[]{:S(2)}) collective-permute-start(bf16[2,8,2048]{2,1,0:T(8,128)(2,1)S(1)} %collective-permute-done.refs_0_), channel_id=1, source_target_pairs={{0,1},{1,0},{2,3},{3,2},{4,5},{5,4},{6,7},{7,6},{8,9},{9,8},{10,11... | collective-permute-start | bytes 196616 | tf_op jit(solution)/shard_map/ppermute | solution.py:34
  18.9 3.3 %collective-permute-start.8 = (bf16[16,768]{1,0:T(8,128)(2,1)S(1)}, bf16[16,768]{1,0:T(8,128)(2,1)S(1)}, u32[]{:S(2)}, u32[]{:S(2)}) collective-permute-start(bf16[16,768]{1,0:T(8,128)(2,1)S(1)} %get-tuple-element.14), channel_id=1, source_target_pairs={{0,3},{1,2},{2,1},{3,0},{4,7},{5,6},{6,5},{7,4},{8,11},{9,10},{10,... | collective-permute-start | bytes 73736 | tf_op jit(solution)/shard_map/ppermute | solution.py:34
  19.5 3.8 %collective-permute-start.9 = (bf16[16,768]{1,0:T(8,128)(2,1)S(1)}, bf16[16,768]{1,0:T(8,128)(2,1)S(1)}, u32[]{:S(2)}, u32[]{:S(2)}) collective-permute-start(bf16[16,768]{1,0:T(8,128)(2,1)S(1)} %get-tuple-element.15), channel_id=1, source_target_pairs={{0,2},{1,3},{2,0},{3,1},{4,6},{5,7},{6,4},{7,5},{8,10},{9,11},{10,... | collective-permute-start | bytes 73736 | tf_op jit(solution)/shard_map/ppermute | solution.py:34
  21.0 2.3 %collective-permute-start.10 = (bf16[16,768]{1,0:T(8,128)(2,1)S(1)}, bf16[16,768]{1,0:T(8,128)(2,1)S(1)}, u32[]{:S(2)}, u32[]{:S(2)}) collective-permute-start(bf16[16,768]{1,0:T(8,128)(2,1)S(1)} %get-tuple-element.16), channel_id=1, source_target_pairs={{0,1},{1,0},{2,3},{3,2},{4,5},{5,4},{6,7},{7,6},{8,9},{9,8},{10,11... | collective-permute-start | bytes 73736 | tf_op jit(solution)/shard_map/ppermute | solution.py:34

commit v2 on v1

--- a/solution.py
+++ b/solution.py
@@ -228,7 +228,7 @@
     axes = ("replay", "module", "half")
     counts = (replay_count, module_count, half_count)
     gathered = {}
-    for replay_step in range(replay_count - 1, -1, -1):
+    for replay_step in range(replay_count):
         for turn in range(turns):
             gathered[replay_step, turn, 0] = exchange(
                 outgoing[turn], axes, counts, lambda half: (replay_step, turn * half_count + half, 0)

time: 24.2 us -> 22 us (0.909)
  starting transfers between devices: 16.2 us -> 9.89 us
  waiting for transfers between devices: 3.89 us -> 7.97 us
    ppermute x11, starting transfers between devices: 16.2 us -> 9.89 us  [exchange(): return lax.ppermute(value, names, pairs)]
    ppermute x11, waiting for transfers between devices: 3.89 us -> 7.97 us  [exchange(): return lax.ppermute(value, names, pairs)]
  transfers between devices with their start and end apart: 11 -> 11, of which waited for: 5 -> 7; matrix products, arithmetic and copies ran while one was open for 0% -> 0% of each run, Pallas kernels for 0% -> 0%
where the time goes in v2:
time: 22 us; the launch traced here: 21.8 us
  starting transfers between devices  9.89 us (45%)
  waiting for transfers between devices  7.97 us (36%)
  Pallas kernels  3.21 us (15%)
  other arithmetic  0.69 us (3%)
    ppermute x11, starting transfers between devices, exchange(): return lax.ppermute(value, names, pairs)  9.89 us
    ppermute x11, waiting for transfers between devices, exchange(): return lax.ppermute(value, names, pairs)  7.97 us
    pallas_call x1, Pallas kernels, body(): pl.pallas_call(precondition_kernel, out_shape=[pltpu.VMEM((replay_total,...  2.13 us
    pallas_call x1, Pallas kernels, body(): pl.pallas_call(functools.partial(score_kernel, tuple(gathered), counts),...  1.09 us
    select_n x1, other arithmetic, body(): return jnp.where(self_pairs, jnp.zeros((), jnp.float32), summed_scores)  0.69 us
  transfers between devices with their start and end apart: 11, of which 7 were waited for; matrix products, arithmetic and copies ran while one was open for 0% of the time, Pallas kernels for 0%

profile of v2, /device:TPU:0, one launch (start us, length us, event | category | flops | bytes accessed | tf_op | source)
XLA Modules:
  0.0 21.8 jit_solution(16607179060981754597)
XLA Ops:
  0.0 0.0 copy-start
  0.0 0.0 copy-start.1
  0.0 2.1 %shard_map.82 = (bf16[768,2048]{1,0:T(8,128)(2,1)S(1)}, bf16[2,8,2048]{2,1,0:T(8,128)(2,1)S(1)}) custom-call(s32[8]{0:T(128)} %counts_in.1, s32[2]{0:T(128)} %slots_in.1, bf16[8,2,64,128]{3,2,1,0:T(8,128)(2,1)} %factors_in.1, f32[2,64,64]{2,1,0:T(8,128)} %output_inverse_in.1, f32[2,64,64]{2,1,0:T(8,128)} %input_inverse_in.1, bf16[768,2048]{1,0:T(8,128)(2,1)} %bitcast.1), custom_call_target="tpu_custom_call" | custom-call | tf_op jit(solution)/shard_map/pallas_call | solution.py:211
  2.1 5.1 %collective-permute-start.3 = (bf16[2,8,2048]{2,1,0:T(8,128)(2,1)S(1)}, bf16[2,8,2048]{2,1,0:T(8,128)(2,1)S(1)}, u32[]{:S(2)}, u32[]{:S(2)}) collective-permute-start(bf16[2,8,2048]{2,1,0:T(8,128)(2,1)S(1)} %get-tuple-element.11), channel_id=1, source_target_pairs={{0,12},{1,15},{2,14},{3,13},{4,8},{5,11},{6,10},{7,9},{8,4},{9,7},... | collective-permute-start | bytes 196616 | tf_op jit(solution)/shard_map/ppermute | solution.py:34
  7.3 0.0 collective-permute-start.2
  7.3 0.6 %collective-permute-start.1 = (bf16[2,8,2048]{2,1,0:T(8,128)(2,1)S(1)}, bf16[2,8,2048]{2,1,0:T(8,128)(2,1)S(1)}, u32[]{:S(2)}, u32[]{:S(2)}) collective-permute-start(bf16[2,8,2048]{2,1,0:T(8,128)(2,1)S(1)} %get-tuple-element.11), channel_id=1, source_target_pairs={{0,4},{1,7},{2,6},{3,5},{4,0},{5,3},{6,2},{7,1},{8,12},{9,15},{10,... | collective-permute-start | bytes 196616 | tf_op jit(solution)/shard_map/ppermute | solution.py:34
  7.9 0.7 %collective-permute-start = (bf16[2,8,2048]{2,1,0:T(8,128)(2,1)S(1)}, bf16[2,8,2048]{2,1,0:T(8,128)(2,1)S(1)}, u32[]{:S(2)}, u32[]{:S(2)}) collective-permute-start(bf16[2,8,2048]{2,1,0:T(8,128)(2,1)S(1)} %get-tuple-element.11), channel_id=1, source_target_pairs={{0,0},{1,3},{2,2},{3,1},{4,4},{5,7},{6,6},{7,5},{8,8},{9,11},{10,1... | collective-permute-start | bytes 196616 | tf_op jit(solution)/shard_map/ppermute | solution.py:34
  8.6 1.7 %collective-permute-done.3.refs_3_ = bf16[2,8,2048]{2,1,0:T(8,128)(2,1)S(1)} collective-permute-done((bf16[2,8,2048]{2,1,0:T(8,128)(2,1)S(1)}, bf16[2,8,2048]{2,1,0:T(8,128)(2,1)S(1)}, u32[]{:S(2)}, u32[]{:S(2)}) %collective-permute-start.3) | collective-permute-done | bytes 65568 | tf_op jit(solution)/shard_map/ppermute | solution.py:34
  10.3 1.0 %collective-permute-start.7 = (bf16[2,8,2048]{2,1,0:T(8,128)(2,1)S(1)}, bf16[2,8,2048]{2,1,0:T(8,128)(2,1)S(1)}, u32[]{:S(2)}, u32[]{:S(2)}) collective-permute-start(bf16[2,8,2048]{2,1,0:T(8,128)(2,1)S(1)} %collective-permute-done.3.refs_3_), channel_id=1, source_target_pairs={{0,1},{1,0},{2,3},{3,2},{4,5},{5,4},{6,7},{7,6},{8,9},{9,8},{10,11... | collective-permute-start | bytes 196616 | tf_op jit(solution)/shard_map/ppermute | solution.py:34
  11.3 2.4 %collective-permute-done.2.refs_2_ = bf16[2,8,2048]{2,1,0:T(8,128)(2,1)S(1)} collective-permute-done((bf16[2,8,2048]{2,1,0:T(8,128)(2,1)S(1)}, bf16[2,8,2048]{2,1,0:T(8,128)(2,1)S(1)}, u32[]{:S(2)}, u32[]{:S(2)}) %collective-permute-start.2) | collective-permute-done | bytes 65568 | tf_op jit(solution)/shard_map/ppermute | solution.py:34
  13.6 0.1 collective-permute-start.6
  13.7 0.0 collective-permute-done.1.refs_1_
  13.7 0.4 %collective-permute-start.5 = (bf16[2,8,2048]{2,1,0:T(8,128)(2,1)S(1)}, bf16[2,8,2048]{2,1,0:T(8,128)(2,1)S(1)}, u32[]{:S(2)}, u32[]{:S(2)}) collective-permute-start(bf16[2,8,2048]{2,1,0:T(8,128)(2,1)S(1)} %collective-permute-done.1.refs_1_), channel_id=1, source_target_pairs={{0,1},{1,0},{2,3},{3,2},{4,5},{5,4},{6,7},{7,6},{8,9},{9,8},{10,11... | collective-permute-start | bytes 196616 | tf_op jit(solution)/shard_map/ppermute | solution.py:34
  14.2 0.0 collective-permute-done.refs_0_
  14.2 0.1 collective-permute-start.4
  14.2 0.0 collective-permute-done.7.refs_7_
  14.2 0.7 %collective-permute-done.6.refs_6_ = bf16[2,8,2048]{2,1,0:T(8,128)(2,1)S(1)} collective-permute-done((bf16[2,8,2048]{2,1,0:T(8,128)(2,1)S(1)}, bf16[2,8,2048]{2,1,0:T(8,128)(2,1)S(1)}, u32[]{:S(2)}, u32[]{:S(2)}) %collective-permute-start.6) | collective-permute-done | bytes 65568 | tf_op jit(solution)/shard_map/ppermute | solution.py:34
  14.9 0.2 collective-permute-done.5.refs_5_
  15.1 0.4 %collective-permute-done.4.refs_4_ = bf16[2,8,2048]{2,1,0:T(8,128)(2,1)S(1)} collective-permute-done((bf16[2,8,2048]{2,1,0:T(8,128)(2,1)S(1)}, bf16[2,8,2048]{2,1,0:T(8,128)(2,1)S(1)}, u32[]{:S(2)}, u32[]{:S(2)}) %collective-permute-start.4) | collective-permute-done | bytes 65568 | tf_op jit(solution)/shard_map/ppermute | solution.py:34
  15.4 1.1 %shard_map.83 = (f32[16,768]{1,0:T(8,128)S(1)}, bf16[16,768]{1,0:T(8,128)(2,1)S(1)}, bf16[16,768]{1,0:T(8,128)(2,1)S(1)}, bf16[16,768]{1,0:T(8,128)(2,1)S(1)}) custom-call(bf16[2,8,2048]{2,1,0:T(8,128)(2,1)S(1)} %collective-permute-done.refs_0_, bf16[2,8,2048]{2,1,0:T(8,128)(2,1)S(1)} %collective-permute-done.1.refs_1_, ...), custom_call_target="tpu_custom_call" | custom-call | flops 201326592 | bytes 3604480 | tf_op jit(solution)/shard_map/pallas_call | solution.py:245
  16.5 0.8 %collective-permute-start.8 = (bf16[16,768]{1,0:T(8,128)(2,1)S(1)}, bf16[16,768]{1,0:T(8,128)(2,1)S(1)}, u32[]{:S(2)}, u32[]{:S(2)}) collective-permute-start(bf16[16,768]{1,0:T(8,128)(2,1)S(1)} %get-tuple-element.14), channel_id=1, source_target_pairs={{0,3},{1,2},{2,1},{3,0},{4,7},{5,6},{6,5},{7,4},{8,11},{9,10},{10,... | collective-permute-start | bytes 73736 | tf_op jit(solution)/shard_map/ppermute | solution.py:34
  17.3 1.1 %collective-permute-start.9 = (bf16[16,768]{1,0:T(8,128)(2,1)S(1)}, bf16[16,768]{1,0:T(8,128)(2,1)S(1)}, u32[]{:S(2)}, u32[]{:S(2)}) collective-permute-start(bf16[16,768]{1,0:T(8,128)(2,1)S(1)} %get-tuple-element.15), channel_id=1, source_target_pairs={{0,2},{1,3},{2,0},{3,1},{4,6},{5,7},{6,4},{7,5},{8,10},{9,11},{10,... | collective-permute-start | bytes 73736 | tf_op jit(solution)/shard_map/ppermute | solution.py:34
  18.4 0.1 collective-permute-start.10
  18.4 1.4 %collective-permute-done.8 = bf16[16,768]{1,0:T(8,128)(2,1)S(1)} collective-permute-done((bf16[16,768]{1,0:T(8,128)(2,1)S(1)}, bf16[16,768]{1,0:T(8,128)(2,1)S(1)}, u32[]{:S(2)}, u32[]{:S(2)}) %collective-permute-start.8) | collective-permute-done | bytes 24608 | tf_op jit(solution)/shard_map/ppermute | solution.py:34
  19.8 1.3 %collective-permute-done.9 = bf16[16,768]{1,0:T(8,128)(2,1)S(1)} collective-permute-done((bf16[16,768]{1,0:T(8,128)(2,1)S(1)}, bf16[16,768]{1,0:T(8,128)(2,1)S(1)}, u32[]{:S(2)}, u32[]{:S(2)}) %collective-permute-start.9) | collective-permute-done | bytes 24608 | tf_op jit(solution)/shard_map/ppermute | solution.py:34
  21.1 0.0 collective-permute-done.10
  21.1 0.0 copy-done
  21.1 0.0 copy-done.1
  21.1 0.7 %add_select_fusion = f32[16,768]{1,0:T(8,128)} fusion(bf16[16,768]{1,0:T(8,128)(2,1)S(1)} %collective-permute-done.10, bf16[16,768]{1,0:T(8,128)(2,1)S(1)} %collective-permute-done.9, f32[16,768]{1,0:T(8,128)S(1)} %get-tuple-element.13, bf16[16,768]{1,0:T(8,128)(2,1)S(1)} %collective-permute-done.8, s32[768]{0:T(1024)S(1)} %copy-done, s32[16]{0:T(128)S(1)} %copy-done.1), kind=kLoop, calls=%fused_computation | loop fusion | flops 98304 | bytes 175168 | tf_op jit(solution)/shard_map/jit(_where)/select_n | solution.py:270
Async XLA Ops:
  0.0 21.1 %copy-start = (s32[768]{0:T(1024)S(1)}, s32[768]{0:T(1024)}, u32[]{:S(2)}) copy-start(s32[768]{0:T(1024)} %param.12) | copy-start | bytes 9220
  0.0 21.1 %copy-start.1 = (s32[16]{0:T(128)S(1)}, s32[16]{0:T(128)}, u32[]{:S(2)}) copy-start(s32[16]{0:T(128)} %param.10) | copy-start | bytes 196
  2.1 8.2 %collective-permute-start.3 = (bf16[2,8,2048]{2,1,0:T(8,128)(2,1)S(1)}, bf16[2,8,2048]{2,1,0:T(8,128)(2,1)S(1)}, u32[]{:S(2)}, u32[]{:S(2)}) collective-permute-start(bf16[2,8,2048]{2,1,0:T(8,128)(2,1)S(1)} %get-tuple-element.11), channel_id=1, source_target_pairs={{0,12},{1,15},{2,14},{3,13},{4,8},{5,11},{6,10},{7,9},{8,4},{9,7},... | collective-permute-start | bytes 196616 | tf_op jit(solution)/shard_map/ppermute | solution.py:34
  7.3 6.4 %collective-permute-start.2 = (bf16[2,8,2048]{2,1,0:T(8,128)(2,1)S(1)}, bf16[2,8,2048]{2,1,0:T(8,128)(2,1)S(1)}, u32[]{:S(2)}, u32[]{:S(2)}) collective-permute-start(bf16[2,8,2048]{2,1,0:T(8,128)(2,1)S(1)} %get-tuple-element.11), channel_id=1, source_target_pairs={{0,8},{1,11},{2,10},{3,9},{4,12},{5,15},{6,14},{7,13},{8,0},{9,3},... | collective-permute-start | bytes 196616 | tf_op jit(solution)/shard_map/ppermute | solution.py:34
  7.3 6.5 %collective-permute-start.1 = (bf16[2,8,2048]{2,1,0:T(8,128)(2,1)S(1)}, bf16[2,8,2048]{2,1,0:T(8,128)(2,1)S(1)}, u32[]{:S(2)}, u32[]{:S(2)}) collective-permute-start(bf16[2,8,2048]{2,1,0:T(8,128)(2,1)S(1)} %get-tuple-element.11), channel_id=1, source_target_pairs={{0,4},{1,7},{2,6},{3,5},{4,0},{5,3},{6,2},{7,1},{8,12},{9,15},{10,... | collective-permute-start | bytes 196616 | tf_op jit(solution)/shard_map/ppermute | solution.py:34
  7.9 6.3 %collective-permute-start = (bf16[2,8,2048]{2,1,0:T(8,128)(2,1)S(1)}, bf16[2,8,2048]{2,1,0:T(8,128)(2,1)S(1)}, u32[]{:S(2)}, u32[]{:S(2)}) collective-permute-start(bf16[2,8,2048]{2,1,0:T(8,128)(2,1)S(1)} %get-tuple-element.11), channel_id=1, source_target_pairs={{0,0},{1,3},{2,2},{3,1},{4,4},{5,7},{6,6},{7,5},{8,8},{9,11},{10,1... | collective-permute-start | bytes 196616 | tf_op jit(solution)/shard_map/ppermute | solution.py:34
  10.3 3.9 %collective-permute-start.7 = (bf16[2,8,2048]{2,1,0:T(8,128)(2,1)S(1)}, bf16[2,8,2048]{2,1,0:T(8,128)(2,1)S(1)}, u32[]{:S(2)}, u32[]{:S(2)}) collective-permute-start(bf16[2,8,2048]{2,1,0:T(8,128)(2,1)S(1)} %collective-permute-done.3.refs_3_), channel_id=1, source_target_pairs={{0,1},{1,0},{2,3},{3,2},{4,5},{5,4},{6,7},{7,6},{8,9},{9,8},{10,11... | collective-permute-start | bytes 196616 | tf_op jit(solution)/shard_map/ppermute | solution.py:34
  13.6 1.3 %collective-permute-start.6 = (bf16[2,8,2048]{2,1,0:T(8,128)(2,1)S(1)}, bf16[2,8,2048]{2,1,0:T(8,128)(2,1)S(1)}, u32[]{:S(2)}, u32[]{:S(2)}) collective-permute-start(bf16[2,8,2048]{2,1,0:T(8,128)(2,1)S(1)} %collective-permute-done.2.refs_2_), channel_id=1, source_target_pairs={{0,1},{1,0},{2,3},{3,2},{4,5},{5,4},{6,7},{7,6},{8,9},{9,8},{10,11... | collective-permute-start | bytes 196616 | tf_op jit(solution)/shard_map/ppermute | solution.py:34
  13.7 1.3 %collective-permute-start.5 = (bf16[2,8,2048]{2,1,0:T(8,128)(2,1)S(1)}, bf16[2,8,2048]{2,1,0:T(8,128)(2,1)S(1)}, u32[]{:S(2)}, u32[]{:S(2)}) collective-permute-start(bf16[2,8,2048]{2,1,0:T(8,128)(2,1)S(1)} %collective-permute-done.1.refs_1_), channel_id=1, source_target_pairs={{0,1},{1,0},{2,3},{3,2},{4,5},{5,4},{6,7},{7,6},{8,9},{9,8},{10,11... | collective-permute-start | bytes 196616 | tf_op jit(solution)/shard_map/ppermute | solution.py:34
  14.2 1.3 %collective-permute-start.4 = (bf16[2,8,2048]{2,1,0:T(8,128)(2,1)S(1)}, bf16[2,8,2048]{2,1,0:T(8,128)(2,1)S(1)}, u32[]{:S(2)}, u32[]{:S(2)}) collective-permute-start(bf16[2,8,2048]{2,1,0:T(8,128)(2,1)S(1)} %collective-permute-done.refs_0_), channel_id=1, source_target_pairs={{0,1},{1,0},{2,3},{3,2},{4,5},{5,4},{6,7},{7,6},{8,9},{9,8},{10,11... | collective-permute-start | bytes 196616 | tf_op jit(solution)/shard_map/ppermute | solution.py:34
  16.5 3.3 %collective-permute-start.8 = (bf16[16,768]{1,0:T(8,128)(2,1)S(1)}, bf16[16,768]{1,0:T(8,128)(2,1)S(1)}, u32[]{:S(2)}, u32[]{:S(2)}) collective-permute-start(bf16[16,768]{1,0:T(8,128)(2,1)S(1)} %get-tuple-element.14), channel_id=1, source_target_pairs={{0,3},{1,2},{2,1},{3,0},{4,7},{5,6},{6,5},{7,4},{8,11},{9,10},{10,... | collective-permute-start | bytes 73736 | tf_op jit(solution)/shard_map/ppermute | solution.py:34
  17.3 3.8 %collective-permute-start.9 = (bf16[16,768]{1,0:T(8,128)(2,1)S(1)}, bf16[16,768]{1,0:T(8,128)(2,1)S(1)}, u32[]{:S(2)}, u32[]{:S(2)}) collective-permute-start(bf16[16,768]{1,0:T(8,128)(2,1)S(1)} %get-tuple-element.15), channel_id=1, source_target_pairs={{0,2},{1,3},{2,0},{3,1},{4,6},{5,7},{6,4},{7,5},{8,10},{9,11},{10,... | collective-permute-start | bytes 73736 | tf_op jit(solution)/shard_map/ppermute | solution.py:34
  18.4 2.8 %collective-permute-start.10 = (bf16[16,768]{1,0:T(8,128)(2,1)S(1)}, bf16[16,768]{1,0:T(8,128)(2,1)S(1)}, u32[]{:S(2)}, u32[]{:S(2)}) collective-permute-start(bf16[16,768]{1,0:T(8,128)(2,1)S(1)} %get-tuple-element.16), channel_id=1, source_target_pairs={{0,1},{1,0},{2,3},{3,2},{4,5},{5,4},{6,7},{7,6},{8,9},{9,8},{10,11... | collective-permute-start | bytes 73736 | tf_op jit(solution)/shard_map/ppermute | solution.py:34

commit v3 on v2

--- a/solution.py
+++ b/solution.py
@@ -172,12 +172,13 @@
             ]
 
     share = len(sources) // (module_count * half_count)
-    for step, chunk in enumerate(chunks):
-        target = partner(module_place, step // half_count, module_count) * half_count + partner(
-            half_place, step % half_count, half_count
-        )
-        value = partials[pl.ds(target * share, share)]
-        chunk[...] = value.reshape(chunk.shape).astype(chunk.dtype)
+    for half_step, chunk in enumerate(chunks):
+        for module_step in range(module_count):
+            target = partner(module_place, module_step, module_count) * half_count + partner(
+                half_place, half_step, half_count
+            )
+            value = partials[pl.ds(target * share, share)]
+            chunk[module_step] = value.reshape(chunk.shape[1:])
 
 
 def body(
@@ -241,13 +242,12 @@
 
     rows = blocks * examples
     group_rows = min(rows, 64)
-    shape = (rows // holders, replay_total)
+    shape = (module_count, rows // holders, replay_total)
     chunks = pl.pallas_call(
         functools.partial(score_kernel, tuple(gathered), counts),
-        out_shape=[pltpu.VMEM(shape, jnp.float32)]
-        + [pltpu.VMEM(shape, jnp.bfloat16)] * (holders - 1),
+        out_shape=[pltpu.VMEM(shape, jnp.float32)] * half_count,
         in_specs=[vmem] * (blocks + 1),
-        out_specs=[vmem] * holders,
+        out_specs=[vmem] * half_count,
         scratch_shapes=[
             pltpu.VMEM((rows // group_rows, group_rows, depth), jnp.bfloat16),
             pltpu.VMEM((blocks, examples, replay_total), jnp.float32),
@@ -260,10 +260,13 @@
         ),
     )(*gathered.values(), replay_rows)
 
-    summed_scores = chunks[0]
-    for step in range(holders - 1, 0, -1):
+    chip_sum = chunks[0]
+    for step in range(1, half_count):
+        chip_sum = chip_sum + exchange(chunks[step], ("half",), (half_count,), lambda half: (step,))
+    summed_scores = chip_sum[0]
+    for step in range(1, module_count):
         term = exchange(
-            chunks[step], axes[1:], counts[1:], lambda half: (step // half_count, step % half_count)
+            chip_sum[step].astype(jnp.bfloat16), ("module",), (module_count,), lambda module: (step,)
         )
         summed_scores = summed_scores + term.astype(jnp.float32)
     self_pairs = new_ids[:, None] == replay_ids[None, :]

time: 22 us -> 22.6 us (1.027)
  waiting for transfers between devices: 7.97 us -> 9.31 us
  starting transfers between devices: 9.89 us -> 9.21 us
    ppermute x11 -> x10, waiting for transfers between devices: 7.97 us -> 9.31 us  [exchange(): return lax.ppermute(value, names, pairs)]
    ppermute x11 -> x10, starting transfers between devices: 9.89 us -> 9.21 us  [exchange(): return lax.ppermute(value, names, pairs)]
  transfers between devices with their start and end apart: 11 -> 10, of which waited for: 7 -> 7; matrix products, arithmetic and copies ran while one was open for 0% -> 0% of each run, Pallas kernels for 0% -> 0%
where the time goes in v3:
time: 22.6 us; the launch traced here: 22.5 us
  waiting for transfers between devices  9.31 us (41%)
  starting transfers between devices  9.21 us (41%)
  Pallas kernels  3.21 us (14%)
  other arithmetic  0.71 us (3%)
    ppermute x10, waiting for transfers between devices, exchange(): return lax.ppermute(value, names, pairs)  9.31 us
    ppermute x10, starting transfers between devices, exchange(): return lax.ppermute(value, names, pairs)  9.21 us
    pallas_call x1, Pallas kernels, body(): pl.pallas_call(precondition_kernel, out_shape=[pltpu.VMEM((replay_total,...  2.13 us
    pallas_call x1, Pallas kernels, body(): pl.pallas_call(functools.partial(score_kernel, tuple(gathered), counts),...  1.09 us
    select_n x1, other arithmetic, body(): return jnp.where(self_pairs, jnp.zeros((), jnp.float32), summed_scores)  0.69 us
  transfers between devices with their start and end apart: 10, of which 7 were waited for; matrix products, arithmetic and copies ran while one was open for 0% of the time, Pallas kernels for 0%

profile of v3, /device:TPU:0, one launch (start us, length us, event | category | flops | bytes accessed | tf_op | source)
XLA Modules:
  0.0 22.5 jit_solution(3471272177357456210)
XLA Ops:
  0.0 0.0 copy-start
  0.0 0.0 copy-start.1
  0.0 2.1 %shard_map.82 = (bf16[768,2048]{1,0:T(8,128)(2,1)S(1)}, bf16[2,8,2048]{2,1,0:T(8,128)(2,1)S(1)}) custom-call(s32[8]{0:T(128)} %counts_in.1, s32[2]{0:T(128)} %slots_in.1, bf16[8,2,64,128]{3,2,1,0:T(8,128)(2,1)} %factors_in.1, f32[2,64,64]{2,1,0:T(8,128)} %output_inverse_in.1, f32[2,64,64]{2,1,0:T(8,128)} %input_inverse_in.1, bf16[768,2048]{1,0:T(8,128)(2,1)} %bitcast.9), custom_call_target="tpu_custom_call" | custom-call | tf_op jit(solution)/shard_map/pallas_call | solution.py:212
  2.1 5.1 %collective-permute-start.3 = (bf16[2,8,2048]{2,1,0:T(8,128)(2,1)S(1)}, bf16[2,8,2048]{2,1,0:T(8,128)(2,1)S(1)}, u32[]{:S(2)}, u32[]{:S(2)}) collective-permute-start(bf16[2,8,2048]{2,1,0:T(8,128)(2,1)S(1)} %get-tuple-element.9), channel_id=1, source_target_pairs={{0,12},{1,15},{2,14},{3,13},{4,8},{5,11},{6,10},{7,9},{8,4},{9,7},... | collective-permute-start | bytes 196616 | tf_op jit(solution)/shard_map/ppermute | solution.py:34
  7.3 0.0 collective-permute-start.2
  7.3 0.6 %collective-permute-start.1 = (bf16[2,8,2048]{2,1,0:T(8,128)(2,1)S(1)}, bf16[2,8,2048]{2,1,0:T(8,128)(2,1)S(1)}, u32[]{:S(2)}, u32[]{:S(2)}) collective-permute-start(bf16[2,8,2048]{2,1,0:T(8,128)(2,1)S(1)} %get-tuple-element.9), channel_id=1, source_target_pairs={{0,4},{1,7},{2,6},{3,5},{4,0},{5,3},{6,2},{7,1},{8,12},{9,15},{10,... | collective-permute-start | bytes 196616 | tf_op jit(solution)/shard_map/ppermute | solution.py:34
  7.9 0.7 %collective-permute-start = (bf16[2,8,2048]{2,1,0:T(8,128)(2,1)S(1)}, bf16[2,8,2048]{2,1,0:T(8,128)(2,1)S(1)}, u32[]{:S(2)}, u32[]{:S(2)}) collective-permute-start(bf16[2,8,2048]{2,1,0:T(8,128)(2,1)S(1)} %get-tuple-element.9), channel_id=1, source_target_pairs={{0,0},{1,3},{2,2},{3,1},{4,4},{5,7},{6,6},{7,5},{8,8},{9,11},{10,1... | collective-permute-start | bytes 196616 | tf_op jit(solution)/shard_map/ppermute | solution.py:34
  8.6 1.7 %collective-permute-done.3.refs_3_ = bf16[2,8,2048]{2,1,0:T(8,128)(2,1)S(1)} collective-permute-done((bf16[2,8,2048]{2,1,0:T(8,128)(2,1)S(1)}, bf16[2,8,2048]{2,1,0:T(8,128)(2,1)S(1)}, u32[]{:S(2)}, u32[]{:S(2)}) %collective-permute-start.3) | collective-permute-done | bytes 65568 | tf_op jit(solution)/shard_map/ppermute | solution.py:34
  10.3 1.0 %collective-permute-start.7 = (bf16[2,8,2048]{2,1,0:T(8,128)(2,1)S(1)}, bf16[2,8,2048]{2,1,0:T(8,128)(2,1)S(1)}, u32[]{:S(2)}, u32[]{:S(2)}) collective-permute-start(bf16[2,8,2048]{2,1,0:T(8,128)(2,1)S(1)} %collective-permute-done.3.refs_3_), channel_id=1, source_target_pairs={{0,1},{1,0},{2,3},{3,2},{4,5},{5,4},{6,7},{7,6},{8,9},{9,8},{10,11... | collective-permute-start | bytes 196616 | tf_op jit(solution)/shard_map/ppermute | solution.py:34
  11.3 2.4 %collective-permute-done.2.refs_2_ = bf16[2,8,2048]{2,1,0:T(8,128)(2,1)S(1)} collective-permute-done((bf16[2,8,2048]{2,1,0:T(8,128)(2,1)S(1)}, bf16[2,8,2048]{2,1,0:T(8,128)(2,1)S(1)}, u32[]{:S(2)}, u32[]{:S(2)}) %collective-permute-start.2) | collective-permute-done | bytes 65568 | tf_op jit(solution)/shard_map/ppermute | solution.py:34
  13.6 0.1 collective-permute-start.6
  13.7 0.0 collective-permute-done.1.refs_1_
  13.7 0.4 %collective-permute-start.5 = (bf16[2,8,2048]{2,1,0:T(8,128)(2,1)S(1)}, bf16[2,8,2048]{2,1,0:T(8,128)(2,1)S(1)}, u32[]{:S(2)}, u32[]{:S(2)}) collective-permute-start(bf16[2,8,2048]{2,1,0:T(8,128)(2,1)S(1)} %collective-permute-done.1.refs_1_), channel_id=1, source_target_pairs={{0,1},{1,0},{2,3},{3,2},{4,5},{5,4},{6,7},{7,6},{8,9},{9,8},{10,11... | collective-permute-start | bytes 196616 | tf_op jit(solution)/shard_map/ppermute | solution.py:34
  14.2 0.0 collective-permute-done.refs_0_
  14.2 0.1 collective-permute-start.4
  14.2 0.0 collective-permute-done.7.refs_7_
  14.2 0.7 %collective-permute-done.6.refs_6_ = bf16[2,8,2048]{2,1,0:T(8,128)(2,1)S(1)} collective-permute-done((bf16[2,8,2048]{2,1,0:T(8,128)(2,1)S(1)}, bf16[2,8,2048]{2,1,0:T(8,128)(2,1)S(1)}, u32[]{:S(2)}, u32[]{:S(2)}) %collective-permute-start.6) | collective-permute-done | bytes 65568 | tf_op jit(solution)/shard_map/ppermute | solution.py:34
  14.9 0.2 collective-permute-done.5.refs_5_
  15.1 0.4 %collective-permute-done.4.refs_4_ = bf16[2,8,2048]{2,1,0:T(8,128)(2,1)S(1)} collective-permute-done((bf16[2,8,2048]{2,1,0:T(8,128)(2,1)S(1)}, bf16[2,8,2048]{2,1,0:T(8,128)(2,1)S(1)}, u32[]{:S(2)}, u32[]{:S(2)}) %collective-permute-start.4) | collective-permute-done | bytes 65568 | tf_op jit(solution)/shard_map/ppermute | solution.py:34
  15.4 1.1 %shard_map.83 = (f32[2,16,768]{2,1,0:T(8,128)S(1)}, f32[2,16,768]{2,1,0:T(8,128)S(1)}) custom-call(bf16[2,8,2048]{2,1,0:T(8,128)(2,1)S(1)} %collective-permute-done.refs_0_, bf16[2,8,2048]{2,1,0:T(8,128)(2,1)S(1)} %collective-permute-done.1.refs_1_, bf16[2,8,2048]{2,1,0:T(8,128)(2,1)S(1)} %collective-permute-done.2.refs_2_, ...), custom_call_target="tpu_custom_call" | custom-call | flops 201326592 | bytes 3604480 | tf_op jit(solution)/shard_map/pallas_call | solution.py:246
  16.5 0.2 collective-permute-start.8
  16.7 1.1 %collective-permute-done.8 = f32[2,16,768]{2,1,0:T(8,128)S(1)} collective-permute-done((f32[2,16,768]{2,1,0:T(8,128)S(1)}, f32[2,16,768]{2,1,0:T(8,128)S(1)}, u32[]{:S(2)}, u32[]{:S(2)}) %collective-permute-start.8) | collective-permute-done | bytes 98336 | tf_op jit(solution)/shard_map/ppermute | solution.py:34
  17.9 1.0 %collective-permute-start.9 = (bf16[16,768]{1,0:T(8,128)(2,1)S(1)}, bf16[16,768]{1,0:T(8,128)(2,1)S(1)}, u32[]{:S(2)}, u32[]{:S(2)}) collective-permute-start(bf16[16,768]{1,0:T(8,128)(2,1)S(1)} %fusion.2), channel_id=1, source_target_pairs={{0,2},{2,0},{1,3},{3,1},{4,6},{6,4},{5,7},{7,5},{8,10},{10,8},{9,1... | collective-permute-start | bytes 73736 | tf_op jit(solution)/shard_map/ppermute | solution.py:34
  18.9 2.9 %collective-permute-done.9 = bf16[16,768]{1,0:T(8,128)(2,1)S(1)} collective-permute-done((bf16[16,768]{1,0:T(8,128)(2,1)S(1)}, bf16[16,768]{1,0:T(8,128)(2,1)S(1)}, u32[]{:S(2)}, u32[]{:S(2)}) %collective-permute-start.9) | collective-permute-done | bytes 24608 | tf_op jit(solution)/shard_map/ppermute | solution.py:34
  21.8 0.0 copy-done
  21.8 0.0 copy-done.1
  21.8 0.7 %fusion.1 = f32[16,768]{1,0:T(8,128)} fusion(f32[2,16,768]{2,1,0:T(8,128)S(1)} %add.6, bf16[16,768]{1,0:T(8,128)(2,1)S(1)} %collective-permute-done.9, s32[768]{0:T(1024)S(1)} %copy-done, s32[16]{0:T(128)S(1)} %copy-done.1), kind=kLoop, calls=%fused_computation.3 | loop fusion | flops 49152 | bytes 126016 | tf_op jit(solution)/shard_map/jit(_where)/select_n | solution.py:273
  (2 shorter events, 0.0 us)
Async XLA Ops:
  0.0 21.8 %copy-start = (s32[768]{0:T(1024)S(1)}, s32[768]{0:T(1024)}, u32[]{:S(2)}) copy-start(s32[768]{0:T(1024)} %param.12) | copy-start | bytes 9220
  0.0 21.8 %copy-start.1 = (s32[16]{0:T(128)S(1)}, s32[16]{0:T(128)}, u32[]{:S(2)}) copy-start(s32[16]{0:T(128)} %param.10) | copy-start | bytes 196
  2.1 8.2 %collective-permute-start.3 = (bf16[2,8,2048]{2,1,0:T(8,128)(2,1)S(1)}, bf16[2,8,2048]{2,1,0:T(8,128)(2,1)S(1)}, u32[]{:S(2)}, u32[]{:S(2)}) collective-permute-start(bf16[2,8,2048]{2,1,0:T(8,128)(2,1)S(1)} %get-tuple-element.9), channel_id=1, source_target_pairs={{0,12},{1,15},{2,14},{3,13},{4,8},{5,11},{6,10},{7,9},{8,4},{9,7},... | collective-permute-start | bytes 196616 | tf_op jit(solution)/shard_map/ppermute | solution.py:34
  7.3 6.4 %collective-permute-start.2 = (bf16[2,8,2048]{2,1,0:T(8,128)(2,1)S(1)}, bf16[2,8,2048]{2,1,0:T(8,128)(2,1)S(1)}, u32[]{:S(2)}, u32[]{:S(2)}) collective-permute-start(bf16[2,8,2048]{2,1,0:T(8,128)(2,1)S(1)} %get-tuple-element.9), channel_id=1, source_target_pairs={{0,8},{1,11},{2,10},{3,9},{4,12},{5,15},{6,14},{7,13},{8,0},{9,3},... | collective-permute-start | bytes 196616 | tf_op jit(solution)/shard_map/ppermute | solution.py:34
  7.3 6.5 %collective-permute-start.1 = (bf16[2,8,2048]{2,1,0:T(8,128)(2,1)S(1)}, bf16[2,8,2048]{2,1,0:T(8,128)(2,1)S(1)}, u32[]{:S(2)}, u32[]{:S(2)}) collective-permute-start(bf16[2,8,2048]{2,1,0:T(8,128)(2,1)S(1)} %get-tuple-element.9), channel_id=1, source_target_pairs={{0,4},{1,7},{2,6},{3,5},{4,0},{5,3},{6,2},{7,1},{8,12},{9,15},{10,... | collective-permute-start | bytes 196616 | tf_op jit(solution)/shard_map/ppermute | solution.py:34
  7.9 6.3 %collective-permute-start = (bf16[2,8,2048]{2,1,0:T(8,128)(2,1)S(1)}, bf16[2,8,2048]{2,1,0:T(8,128)(2,1)S(1)}, u32[]{:S(2)}, u32[]{:S(2)}) collective-permute-start(bf16[2,8,2048]{2,1,0:T(8,128)(2,1)S(1)} %get-tuple-element.9), channel_id=1, source_target_pairs={{0,0},{1,3},{2,2},{3,1},{4,4},{5,7},{6,6},{7,5},{8,8},{9,11},{10,1... | collective-permute-start | bytes 196616 | tf_op jit(solution)/shard_map/ppermute | solution.py:34
  10.3 3.9 %collective-permute-start.7 = (bf16[2,8,2048]{2,1,0:T(8,128)(2,1)S(1)}, bf16[2,8,2048]{2,1,0:T(8,128)(2,1)S(1)}, u32[]{:S(2)}, u32[]{:S(2)}) collective-permute-start(bf16[2,8,2048]{2,1,0:T(8,128)(2,1)S(1)} %collective-permute-done.3.refs_3_), channel_id=1, source_target_pairs={{0,1},{1,0},{2,3},{3,2},{4,5},{5,4},{6,7},{7,6},{8,9},{9,8},{10,11... | collective-permute-start | bytes 196616 | tf_op jit(solution)/shard_map/ppermute | solution.py:34
  13.6 1.3 %collective-permute-start.6 = (bf16[2,8,2048]{2,1,0:T(8,128)(2,1)S(1)}, bf16[2,8,2048]{2,1,0:T(8,128)(2,1)S(1)}, u32[]{:S(2)}, u32[]{:S(2)}) collective-permute-start(bf16[2,8,2048]{2,1,0:T(8,128)(2,1)S(1)} %collective-permute-done.2.refs_2_), channel_id=1, source_target_pairs={{0,1},{1,0},{2,3},{3,2},{4,5},{5,4},{6,7},{7,6},{8,9},{9,8},{10,11... | collective-permute-start | bytes 196616 | tf_op jit(solution)/shard_map/ppermute | solution.py:34
  13.7 1.3 %collective-permute-start.5 = (bf16[2,8,2048]{2,1,0:T(8,128)(2,1)S(1)}, bf16[2,8,2048]{2,1,0:T(8,128)(2,1)S(1)}, u32[]{:S(2)}, u32[]{:S(2)}) collective-permute-start(bf16[2,8,2048]{2,1,0:T(8,128)(2,1)S(1)} %collective-permute-done.1.refs_1_), channel_id=1, source_target_pairs={{0,1},{1,0},{2,3},{3,2},{4,5},{5,4},{6,7},{7,6},{8,9},{9,8},{10,11... | collective-permute-start | bytes 196616 | tf_op jit(solution)/shard_map/ppermute | solution.py:34
  14.2 1.3 %collective-permute-start.4 = (bf16[2,8,2048]{2,1,0:T(8,128)(2,1)S(1)}, bf16[2,8,2048]{2,1,0:T(8,128)(2,1)S(1)}, u32[]{:S(2)}, u32[]{:S(2)}) collective-permute-start(bf16[2,8,2048]{2,1,0:T(8,128)(2,1)S(1)} %collective-permute-done.refs_0_), channel_id=1, source_target_pairs={{0,1},{1,0},{2,3},{3,2},{4,5},{5,4},{6,7},{7,6},{8,9},{9,8},{10,11... | collective-permute-start | bytes 196616 | tf_op jit(solution)/shard_map/ppermute | solution.py:34
  16.5 1.4 %collective-permute-start.8 = (f32[2,16,768]{2,1,0:T(8,128)S(1)}, f32[2,16,768]{2,1,0:T(8,128)S(1)}, u32[]{:S(2)}, u32[]{:S(2)}) collective-permute-start(f32[2,16,768]{2,1,0:T(8,128)S(1)} %get-tuple-element.12), channel_id=1, source_target_pairs={{0,1},{1,0},{2,3},{3,2},{4,5},{5,4},{6,7},{7,6},{8,9},{9,8},{10,11... | collective-permute-start | bytes 294920 | tf_op jit(solution)/shard_map/ppermute | solution.py:34
  17.9 3.9 %collective-permute-start.9 = (bf16[16,768]{1,0:T(8,128)(2,1)S(1)}, bf16[16,768]{1,0:T(8,128)(2,1)S(1)}, u32[]{:S(2)}, u32[]{:S(2)}) collective-permute-start(bf16[16,768]{1,0:T(8,128)(2,1)S(1)} %fusion.2), channel_id=1, source_target_pairs={{0,2},{2,0},{1,3},{3,1},{4,6},{6,4},{5,7},{7,5},{8,10},{10,8},{9,1... | collective-permute-start | bytes 73736 | tf_op jit(solution)/shard_map/ppermute | solution.py:34

commit v4 on v2

--- a/solution.py
+++ b/solution.py
@@ -64,7 +64,7 @@
             )
         )
     ]
-    for copy_in in copies_in:
+    for copy_in in copies_in[:-1]:
         copy_in.start()
 
     examples, modules, tokens, width = factors.shape
@@ -77,6 +77,7 @@
     half_place = lax.axis_index("half")
     for copy_in in copies_in[:-1]:
         copy_in.wait()
+    copies_in[-1].start()
 
     place = (examples, examples * tokens)
     example = lax.broadcasted_iota(jnp.int32, place, 0)
@@ -136,7 +137,7 @@
     blocks, replay_rows = refs[: len(sources)], refs[len(sources)]
     chunks, (joined, partials) = refs[len(sources) + 1 : -2], refs[-2:]
     replay_count, module_count, half_count = holders
-    examples = blocks[0].shape[1]
+    examples = blocks[0].shape[-2]
     replay_place = lax.axis_index("replay")
     module_place = lax.axis_index("module")
     half_place = lax.axis_index("half")
@@ -145,7 +146,7 @@
     for group in range(joined.shape[0]):
         joined[group] = jnp.concatenate(
             [
-                block[half_place].astype(jnp.float32)
+                (block[half_place] if len(block.shape) == 3 else block[...]).astype(jnp.float32)
                 for block in blocks[group * per_group : (group + 1) * per_group]
             ],
             axis=0,
@@ -235,8 +236,12 @@
             )
     for replay_step, turn, _ in list(gathered):
         for half_step in range(1, half_count):
+            needed = partner(lax.axis_index("half"), half_step, half_count)
             gathered[replay_step, turn, half_step] = exchange(
-                gathered[replay_step, turn, 0], ("half",), (half_count,), lambda half: (half_step,)
+                lax.dynamic_index_in_dim(gathered[replay_step, turn, 0], needed, 0, keepdims=False),
+                ("half",),
+                (half_count,),
+                lambda half: (half_step,),
             )
 
     rows = blocks * examples
@@ -261,7 +266,7 @@
     )(*gathered.values(), replay_rows)
 
     summed_scores = chunks[0]
-    for step in range(holders - 1, 0, -1):
+    for step in sorted(range(1, holders), key=lambda step: (step < half_count, step)):
         term = exchange(
             chunks[step], axes[1:], counts[1:], lambda half: (step // half_count, step % half_count)
         )

time: 22 us -> 22.7 us (1.032)
  Pallas kernels: 3.21 us -> 4.07 us
  waiting for transfers between devices: 7.97 us -> 7.42 us
  starting transfers between devices: 9.89 us -> 10.2 us
    pallas_call x1, Pallas kernels: 2.13 us -> 2.99 us  [body(): pl.pallas_call(precondition_kernel, out_shape=[pltpu.VMEM((replay_total,...]
    ppermute x11, waiting for transfers between devices: 7.97 us -> 7.42 us  [exchange(): return lax.ppermute(value, names, pairs)]
    ppermute x11, starting transfers between devices: 9.89 us -> 10.2 us  [exchange(): return lax.ppermute(value, names, pairs)]
where the time goes in v4:
time: 22.7 us; the launch traced here: 22.5 us
  starting transfers between devices  10.2 us (45%)
  waiting for transfers between devices  7.42 us (33%)
  Pallas kernels  4.07 us (18%)
  other arithmetic  0.69 us (3%)
    ppermute x11, starting transfers between devices, exchange(): return lax.ppermute(value, names, pairs)  10.2 us
    ppermute x11, waiting for transfers between devices, exchange(): return lax.ppermute(value, names, pairs)  7.42 us
    pallas_call x1, Pallas kernels, body(): pl.pallas_call(precondition_kernel, out_shape=[pltpu.VMEM((replay_total,...  2.99 us
    pallas_call x1, Pallas kernels, body(): pl.pallas_call(functools.partial(score_kernel, tuple(gathered), counts),...  1.08 us
    select_n x1, other arithmetic, body(): return jnp.where(self_pairs, jnp.zeros((), jnp.float32), summed_scores)  0.69 us
  transfers between devices with their start and end apart: 11, of which 7 were waited for; matrix products, arithmetic and copies ran while one was open for 0% of the time, Pallas kernels for 0%

profile of v4, /device:TPU:0, one launch (start us, length us, event | category | flops | bytes accessed | tf_op | source)
XLA Modules:
  0.0 22.5 jit_solution(1983569064035806411)
XLA Ops:
  0.0 0.0 copy-start
  0.0 0.0 copy-start.1
  0.0 3.0 %shard_map.82 = (bf16[768,2048]{1,0:T(8,128)(2,1)S(1)}, bf16[2,8,2048]{2,1,0:T(8,128)(2,1)S(1)}) custom-call(s32[8]{0:T(128)} %counts_in.1, s32[2]{0:T(128)} %slots_in.1, bf16[8,2,64,128]{3,2,1,0:T(8,128)(2,1)} %factors_in.1, f32[2,64,64]{2,1,0:T(8,128)} %output_inverse_in.1, f32[2,64,64]{2,1,0:T(8,128)} %input_inverse_in.1, bf16[768,2048]{1,0:T(8,128)(2,1)} %bitcast.9), custom_call_target="tpu_custom_call" | custom-call | tf_op jit(solution)/shard_map/pallas_call | solution.py:212
  3.0 5.1 %collective-permute-start.3 = (bf16[2,8,2048]{2,1,0:T(8,128)(2,1)S(1)}, bf16[2,8,2048]{2,1,0:T(8,128)(2,1)S(1)}, u32[]{:S(2)}, u32[]{:S(2)}) collective-permute-start(bf16[2,8,2048]{2,1,0:T(8,128)(2,1)S(1)} %get-tuple-element.11), channel_id=1, source_target_pairs={{0,12},{1,15},{2,14},{3,13},{4,8},{5,11},{6,10},{7,9},{8,4},{9,7},... | collective-permute-start | bytes 196616 | tf_op jit(solution)/shard_map/ppermute | solution.py:34
  8.1 0.0 collective-permute-start.2
  8.1 0.6 %collective-permute-start.1 = (bf16[2,8,2048]{2,1,0:T(8,128)(2,1)S(1)}, bf16[2,8,2048]{2,1,0:T(8,128)(2,1)S(1)}, u32[]{:S(2)}, u32[]{:S(2)}) collective-permute-start(bf16[2,8,2048]{2,1,0:T(8,128)(2,1)S(1)} %get-tuple-element.11), channel_id=1, source_target_pairs={{0,4},{1,7},{2,6},{3,5},{4,0},{5,3},{6,2},{7,1},{8,12},{9,15},{10,... | collective-permute-start | bytes 196616 | tf_op jit(solution)/shard_map/ppermute | solution.py:34
  8.8 0.7 %collective-permute-start = (bf16[2,8,2048]{2,1,0:T(8,128)(2,1)S(1)}, bf16[2,8,2048]{2,1,0:T(8,128)(2,1)S(1)}, u32[]{:S(2)}, u32[]{:S(2)}) collective-permute-start(bf16[2,8,2048]{2,1,0:T(8,128)(2,1)S(1)} %get-tuple-element.11), channel_id=1, source_target_pairs={{0,0},{1,3},{2,2},{3,1},{4,4},{5,7},{6,6},{7,5},{8,8},{9,11},{10,1... | collective-permute-start | bytes 196616 | tf_op jit(solution)/shard_map/ppermute | solution.py:34
  9.4 1.7 %collective-permute-done.3.refs_3_ = bf16[2,8,2048]{2,1,0:T(8,128)(2,1)S(1)} collective-permute-done((bf16[2,8,2048]{2,1,0:T(8,128)(2,1)S(1)}, bf16[2,8,2048]{2,1,0:T(8,128)(2,1)S(1)}, u32[]{:S(2)}, u32[]{:S(2)}) %collective-permute-start.3) | collective-permute-done | bytes 65568 | tf_op jit(solution)/shard_map/ppermute | solution.py:34
  11.2 1.0 %collective-permute-start.7 = (bf16[8,2048]{1,0:T(8,128)(2,1)S(1)}, bf16[8,2048]{1,0:T(8,128)(2,1)S(1)}, u32[]{:S(2)}, u32[]{:S(2)}) collective-permute-start(bf16[8,2048]{1,0:T(8,128)(2,1)S(1)} %dynamic-slice_bitcast_fusion), channel_id=1, source_target_pairs={{0,1},{1,0},{2,3},{3,2},{4,5},{5,4},{6,7},{7,6},{8,9},{9,8},{10,11... | collective-permute-start | bytes 98312 | tf_op jit(solution)/shard_map/ppermute | solution.py:34
  12.2 2.4 %collective-permute-done.2.refs_2_ = bf16[2,8,2048]{2,1,0:T(8,128)(2,1)S(1)} collective-permute-done((bf16[2,8,2048]{2,1,0:T(8,128)(2,1)S(1)}, bf16[2,8,2048]{2,1,0:T(8,128)(2,1)S(1)}, u32[]{:S(2)}, u32[]{:S(2)}) %collective-permute-start.2) | collective-permute-done | bytes 65568 | tf_op jit(solution)/shard_map/ppermute | solution.py:34
  14.5 0.1 collective-permute-start.6
  14.6 0.0 collective-permute-done.1.refs_1_
  14.6 0.4 %collective-permute-start.5 = (bf16[8,2048]{1,0:T(8,128)(2,1)S(1)}, bf16[8,2048]{1,0:T(8,128)(2,1)S(1)}, u32[]{:S(2)}, u32[]{:S(2)}) collective-permute-start(bf16[8,2048]{1,0:T(8,128)(2,1)S(1)} %dynamic-slice_bitcast_fusion.2), channel_id=1, source_target_pairs={{0,1},{1,0},{2,3},{3,2},{4,5},{5,4},{6,7},{7,6},{8,9},{9,8},{10,11... | collective-permute-start | bytes 98312 | tf_op jit(solution)/shard_map/ppermute | solution.py:34
  15.0 0.0 collective-permute-done.refs_0_
  15.0 0.1 collective-permute-start.4
  15.2 0.0 collective-permute-done.7.refs_7_
  15.2 0.5 %collective-permute-done.6.refs_6_ = bf16[8,2048]{1,0:T(8,128)(2,1)S(1)} collective-permute-done((bf16[8,2048]{1,0:T(8,128)(2,1)S(1)}, bf16[8,2048]{1,0:T(8,128)(2,1)S(1)}, u32[]{:S(2)}, u32[]{:S(2)}) %collective-permute-start.6) | collective-permute-done | bytes 32800 | tf_op jit(solution)/shard_map/ppermute | solution.py:34
  15.7 0.2 collective-permute-done.5.refs_5_
  15.9 0.4 %collective-permute-done.4.refs_4_ = bf16[8,2048]{1,0:T(8,128)(2,1)S(1)} collective-permute-done((bf16[8,2048]{1,0:T(8,128)(2,1)S(1)}, bf16[8,2048]{1,0:T(8,128)(2,1)S(1)}, u32[]{:S(2)}, u32[]{:S(2)}) %collective-permute-start.4) | collective-permute-done | bytes 32800 | tf_op jit(solution)/shard_map/ppermute | solution.py:34
  16.2 1.1 %shard_map.83 = (f32[16,768]{1,0:T(8,128)S(1)}, bf16[16,768]{1,0:T(8,128)(2,1)S(1)}, bf16[16,768]{1,0:T(8,128)(2,1)S(1)}, bf16[16,768]{1,0:T(8,128)(2,1)S(1)}) custom-call(bf16[2,8,2048]{2,1,0:T(8,128)(2,1)S(1)} %collective-permute-done.refs_0_, bf16[2,8,2048]{2,1,0:T(8,128)(2,1)S(1)} %collective-permute-done.1.refs_1_, ...), custom_call_target="tpu_custom_call" | custom-call | flops 201326592 | bytes 3604480 | tf_op jit(solution)/shard_map/pallas_call | solution.py:250
  17.3 1.0 %collective-permute-start.8 = (bf16[16,768]{1,0:T(8,128)(2,1)S(1)}, bf16[16,768]{1,0:T(8,128)(2,1)S(1)}, u32[]{:S(2)}, u32[]{:S(2)}) collective-permute-start(bf16[16,768]{1,0:T(8,128)(2,1)S(1)} %get-tuple-element.14), channel_id=1, source_target_pairs={{0,2},{1,3},{2,0},{3,1},{4,6},{5,7},{6,4},{7,5},{8,10},{9,11},{10,... | collective-permute-start | bytes 73736 | tf_op jit(solution)/shard_map/ppermute | solution.py:34
  18.4 0.6 %collective-permute-start.9 = (bf16[16,768]{1,0:T(8,128)(2,1)S(1)}, bf16[16,768]{1,0:T(8,128)(2,1)S(1)}, u32[]{:S(2)}, u32[]{:S(2)}) collective-permute-start(bf16[16,768]{1,0:T(8,128)(2,1)S(1)} %get-tuple-element.15), channel_id=1, source_target_pairs={{0,3},{1,2},{2,1},{3,0},{4,7},{5,6},{6,5},{7,4},{8,11},{9,10},{10,... | collective-permute-start | bytes 73736 | tf_op jit(solution)/shard_map/ppermute | solution.py:34
  18.9 0.6 %collective-permute-start.10 = (bf16[16,768]{1,0:T(8,128)(2,1)S(1)}, bf16[16,768]{1,0:T(8,128)(2,1)S(1)}, u32[]{:S(2)}, u32[]{:S(2)}) collective-permute-start(bf16[16,768]{1,0:T(8,128)(2,1)S(1)} %get-tuple-element.16), channel_id=1, source_target_pairs={{0,1},{1,0},{2,3},{3,2},{4,5},{5,4},{6,7},{7,6},{8,9},{9,8},{10,11... | collective-permute-start | bytes 73736 | tf_op jit(solution)/shard_map/ppermute | solution.py:34
  19.5 1.7 %collective-permute-done.8 = bf16[16,768]{1,0:T(8,128)(2,1)S(1)} collective-permute-done((bf16[16,768]{1,0:T(8,128)(2,1)S(1)}, bf16[16,768]{1,0:T(8,128)(2,1)S(1)}, u32[]{:S(2)}, u32[]{:S(2)}) %collective-permute-start.8) | collective-permute-done | bytes 24608 | tf_op jit(solution)/shard_map/ppermute | solution.py:34
  21.2 0.6 %collective-permute-done.9 = bf16[16,768]{1,0:T(8,128)(2,1)S(1)} collective-permute-done((bf16[16,768]{1,0:T(8,128)(2,1)S(1)}, bf16[16,768]{1,0:T(8,128)(2,1)S(1)}, u32[]{:S(2)}, u32[]{:S(2)}) %collective-permute-start.9) | collective-permute-done | bytes 24608 | tf_op jit(solution)/shard_map/ppermute | solution.py:34
  21.8 0.0 collective-permute-done.10
  21.8 0.0 copy-done
  21.8 0.0 copy-done.1
  21.8 0.7 %add_select_fusion = f32[16,768]{1,0:T(8,128)} fusion(bf16[16,768]{1,0:T(8,128)(2,1)S(1)} %collective-permute-done.10, bf16[16,768]{1,0:T(8,128)(2,1)S(1)} %collective-permute-done.9, f32[16,768]{1,0:T(8,128)S(1)} %get-tuple-element.13, bf16[16,768]{1,0:T(8,128)(2,1)S(1)} %collective-permute-done.8, s32[768]{0:T(1024)S(1)} %copy-done, s32[16]{0:T(128)S(1)} %copy-done.1), kind=kLoop, calls=%fused_computation | loop fusion | flops 98304 | bytes 175168 | tf_op jit(solution)/shard_map/jit(_where)/select_n | solution.py:275
  (4 shorter events, 0.0 us)
Async XLA Ops:
  0.0 21.8 %copy-start = (s32[768]{0:T(1024)S(1)}, s32[768]{0:T(1024)}, u32[]{:S(2)}) copy-start(s32[768]{0:T(1024)} %param.12) | copy-start | bytes 9220
  0.0 21.8 %copy-start.1 = (s32[16]{0:T(128)S(1)}, s32[16]{0:T(128)}, u32[]{:S(2)}) copy-start(s32[16]{0:T(128)} %param.10) | copy-start | bytes 196
  3.0 8.2 %collective-permute-start.3 = (bf16[2,8,2048]{2,1,0:T(8,128)(2,1)S(1)}, bf16[2,8,2048]{2,1,0:T(8,128)(2,1)S(1)}, u32[]{:S(2)}, u32[]{:S(2)}) collective-permute-start(bf16[2,8,2048]{2,1,0:T(8,128)(2,1)S(1)} %get-tuple-element.11), channel_id=1, source_target_pairs={{0,12},{1,15},{2,14},{3,13},{4,8},{5,11},{6,10},{7,9},{8,4},{9,7},... | collective-permute-start | bytes 196616 | tf_op jit(solution)/shard_map/ppermute | solution.py:34
  8.1 6.4 %collective-permute-start.2 = (bf16[2,8,2048]{2,1,0:T(8,128)(2,1)S(1)}, bf16[2,8,2048]{2,1,0:T(8,128)(2,1)S(1)}, u32[]{:S(2)}, u32[]{:S(2)}) collective-permute-start(bf16[2,8,2048]{2,1,0:T(8,128)(2,1)S(1)} %get-tuple-element.11), channel_id=1, source_target_pairs={{0,8},{1,11},{2,10},{3,9},{4,12},{5,15},{6,14},{7,13},{8,0},{9,3},... | collective-permute-start | bytes 196616 | tf_op jit(solution)/shard_map/ppermute | solution.py:34
  8.1 6.5 %collective-permute-start.1 = (bf16[2,8,2048]{2,1,0:T(8,128)(2,1)S(1)}, bf16[2,8,2048]{2,1,0:T(8,128)(2,1)S(1)}, u32[]{:S(2)}, u32[]{:S(2)}) collective-permute-start(bf16[2,8,2048]{2,1,0:T(8,128)(2,1)S(1)} %get-tuple-element.11), channel_id=1, source_target_pairs={{0,4},{1,7},{2,6},{3,5},{4,0},{5,3},{6,2},{7,1},{8,12},{9,15},{10,... | collective-permute-start | bytes 196616 | tf_op jit(solution)/shard_map/ppermute | solution.py:34
  8.8 6.3 %collective-permute-start = (bf16[2,8,2048]{2,1,0:T(8,128)(2,1)S(1)}, bf16[2,8,2048]{2,1,0:T(8,128)(2,1)S(1)}, u32[]{:S(2)}, u32[]{:S(2)}) collective-permute-start(bf16[2,8,2048]{2,1,0:T(8,128)(2,1)S(1)} %get-tuple-element.11), channel_id=1, source_target_pairs={{0,0},{1,3},{2,2},{3,1},{4,4},{5,7},{6,6},{7,5},{8,8},{9,11},{10,1... | collective-permute-start | bytes 196616 | tf_op jit(solution)/shard_map/ppermute | solution.py:34
  11.2 4.0 %collective-permute-start.7 = (bf16[8,2048]{1,0:T(8,128)(2,1)S(1)}, bf16[8,2048]{1,0:T(8,128)(2,1)S(1)}, u32[]{:S(2)}, u32[]{:S(2)}) collective-permute-start(bf16[8,2048]{1,0:T(8,128)(2,1)S(1)} %dynamic-slice_bitcast_fusion), channel_id=1, source_target_pairs={{0,1},{1,0},{2,3},{3,2},{4,5},{5,4},{6,7},{7,6},{8,9},{9,8},{10,11... | collective-permute-start | bytes 98312 | tf_op jit(solution)/shard_map/ppermute | solution.py:34
  14.5 1.2 %collective-permute-start.6 = (bf16[8,2048]{1,0:T(8,128)(2,1)S(1)}, bf16[8,2048]{1,0:T(8,128)(2,1)S(1)}, u32[]{:S(2)}, u32[]{:S(2)}) collective-permute-start(bf16[8,2048]{1,0:T(8,128)(2,1)S(1)} %dynamic-slice_bitcast_fusion.1), channel_id=1, source_target_pairs={{0,1},{1,0},{2,3},{3,2},{4,5},{5,4},{6,7},{7,6},{8,9},{9,8},{10,11... | collective-permute-start | bytes 98312 | tf_op jit(solution)/shard_map/ppermute | solution.py:34
  14.6 1.3 %collective-permute-start.5 = (bf16[8,2048]{1,0:T(8,128)(2,1)S(1)}, bf16[8,2048]{1,0:T(8,128)(2,1)S(1)}, u32[]{:S(2)}, u32[]{:S(2)}) collective-permute-start(bf16[8,2048]{1,0:T(8,128)(2,1)S(1)} %dynamic-slice_bitcast_fusion.2), channel_id=1, source_target_pairs={{0,1},{1,0},{2,3},{3,2},{4,5},{5,4},{6,7},{7,6},{8,9},{9,8},{10,11... | collective-permute-start | bytes 98312 | tf_op jit(solution)/shard_map/ppermute | solution.py:34
  15.0 1.2 %collective-permute-start.4 = (bf16[8,2048]{1,0:T(8,128)(2,1)S(1)}, bf16[8,2048]{1,0:T(8,128)(2,1)S(1)}, u32[]{:S(2)}, u32[]{:S(2)}) collective-permute-start(bf16[8,2048]{1,0:T(8,128)(2,1)S(1)} %dynamic-slice_bitcast_fusion.3), channel_id=1, source_target_pairs={{0,1},{1,0},{2,3},{3,2},{4,5},{5,4},{6,7},{7,6},{8,9},{9,8},{10,11... | collective-permute-start | bytes 98312 | tf_op jit(solution)/shard_map/ppermute | solution.py:34
  17.3 3.9 %collective-permute-start.8 = (bf16[16,768]{1,0:T(8,128)(2,1)S(1)}, bf16[16,768]{1,0:T(8,128)(2,1)S(1)}, u32[]{:S(2)}, u32[]{:S(2)}) collective-permute-start(bf16[16,768]{1,0:T(8,128)(2,1)S(1)} %get-tuple-element.14), channel_id=1, source_target_pairs={{0,2},{1,3},{2,0},{3,1},{4,6},{5,7},{6,4},{7,5},{8,10},{9,11},{10,... | collective-permute-start | bytes 73736 | tf_op jit(solution)/shard_map/ppermute | solution.py:34
  18.4 3.4 %collective-permute-start.9 = (bf16[16,768]{1,0:T(8,128)(2,1)S(1)}, bf16[16,768]{1,0:T(8,128)(2,1)S(1)}, u32[]{:S(2)}, u32[]{:S(2)}) collective-permute-start(bf16[16,768]{1,0:T(8,128)(2,1)S(1)} %get-tuple-element.15), channel_id=1, source_target_pairs={{0,3},{1,2},{2,1},{3,0},{4,7},{5,6},{6,5},{7,4},{8,11},{9,10},{10,... | collective-permute-start | bytes 73736 | tf_op jit(solution)/shard_map/ppermute | solution.py:34
  18.9 2.9 %collective-permute-start.10 = (bf16[16,768]{1,0:T(8,128)(2,1)S(1)}, bf16[16,768]{1,0:T(8,128)(2,1)S(1)}, u32[]{:S(2)}, u32[]{:S(2)}) collective-permute-start(bf16[16,768]{1,0:T(8,128)(2,1)S(1)} %get-tuple-element.16), channel_id=1, source_target_pairs={{0,1},{1,0},{2,3},{3,2},{4,5},{5,4},{6,7},{7,6},{8,9},{9,8},{10,11... | collective-permute-start | bytes 73736 | tf_op jit(solution)/shard_map/ppermute | solution.py:34

commit v5 on v2

--- a/solution.py
+++ b/solution.py
@@ -45,8 +45,6 @@
     factors_in,
     output_inverse_in,
     input_inverse_in,
-    replay_in,
-    replay_rows,
     *rest,
 ):
     counts, slots, factors, output_inverse, input_inverse, arrived = rest[-6:]
@@ -60,7 +58,6 @@
                 (input_inverse_in, input_inverse),
                 (output_inverse_in, output_inverse),
                 (factors_in, factors),
-                (replay_in, replay_rows),
             )
         )
     ]
@@ -75,7 +72,7 @@
     share = groups // halves
     module_place = lax.axis_index("module")
     half_place = lax.axis_index("half")
-    for copy_in in copies_in[:-1]:
+    for copy_in in copies_in:
         copy_in.wait()
 
     place = (examples, examples * tokens)
@@ -129,23 +126,40 @@
         for q in range(groups):
             block = total[q * examples : (q + 1) * examples]
             target[q // share, :, q % share * LANES : (q % share + 1) * LANES] = block
-    copies_in[-1].wait()
+
+
+def copy_kernel(source, after, target, arrived):
+    copy_in = pltpu.make_async_copy(source, target, arrived)
+    copy_in.start()
+    copy_in.wait()
+
+
+def pack_kernel(half_count, *refs):
+    half_place = lax.axis_index("half")
+    blocks, packs = refs[:-half_count], refs[1 - half_count :]
+    for half_step, pack in enumerate(packs, 1):
+        needed = partner(half_place, half_step, half_count)
+        for number, block in enumerate(blocks):
+            pack[number] = block[needed]
 
 
 def score_kernel(sources, holders, *refs):
-    blocks, replay_rows = refs[: len(sources)], refs[len(sources)]
-    chunks, (joined, partials) = refs[len(sources) + 1 : -2], refs[-2:]
     replay_count, module_count, half_count = holders
-    examples = blocks[0].shape[1]
+    own_count = len(sources) // half_count
+    own, passed = refs[:own_count], refs[own_count : own_count + half_count - 1]
+    replay_rows, *chunks, joined, partials = refs[own_count + half_count - 1 :]
+    examples = own[0].shape[-2]
     replay_place = lax.axis_index("replay")
     module_place = lax.axis_index("module")
     half_place = lax.axis_index("half")
 
     per_group = joined.shape[1] // examples
+    blocks = [block.at[half_place] for block in own]
+    blocks += [pack.at[number] for pack in passed for number in range(own_count)]
     for group in range(joined.shape[0]):
         joined[group] = jnp.concatenate(
             [
-                block[half_place].astype(jnp.float32)
+                block[...].astype(jnp.float32)
                 for block in blocks[group * per_group : (group + 1) * per_group]
             ],
             axis=0,
@@ -206,14 +220,12 @@
         new_factors,
         output_inverse,
         input_inverse,
-        replay_grads.reshape(replay_total, depth),
     )
-    replay_rows, *outgoing = pl.pallas_call(
+    outgoing = pl.pallas_call(
         precondition_kernel,
-        out_shape=[pltpu.VMEM((replay_total, depth), jnp.bfloat16)]
-        + [pltpu.VMEM((half_count, examples, depth), jnp.bfloat16)] * turns,
+        out_shape=[pltpu.VMEM((half_count, examples, depth), jnp.bfloat16)] * turns,
         in_specs=[hbm] * len(operands),
-        out_specs=[vmem] * (1 + turns),
+        out_specs=[vmem] * turns,
         scratch_shapes=[
             pltpu.SMEM(new_counts.shape, jnp.int32),
             pltpu.SMEM(slot_module.shape, jnp.int32),
@@ -233,20 +245,47 @@
             gathered[replay_step, turn, 0] = exchange(
                 outgoing[turn], axes, counts, lambda half: (replay_step, turn * half_count + half, 0)
             )
-    for replay_step, turn, _ in list(gathered):
-        for half_step in range(1, half_count):
-            gathered[replay_step, turn, half_step] = exchange(
-                gathered[replay_step, turn, 0], ("half",), (half_count,), lambda half: (half_step,)
-            )
+    replay_rows = pl.pallas_call(
+        copy_kernel,
+        out_shape=pltpu.VMEM((replay_total, depth), jnp.bfloat16),
+        in_specs=[hbm, vmem],
+        out_specs=vmem,
+        scratch_shapes=[pltpu.SemaphoreType.DMA],
+        compiler_params=pltpu.CompilerParams(vmem_limit_bytes=2**20),
+        cost_estimate=pl.CostEstimate(
+            flops=0, bytes_accessed=4 * replay_total * depth, transcendentals=0
+        ),
+    )(
+        pltpu.with_memory_space_constraint(replay_grads.reshape(replay_total, depth), pltpu.HBM),
+        outgoing[0],
+    )
+
+    own = list(gathered.values())
+    packs = pl.pallas_call(
+        functools.partial(pack_kernel, half_count),
+        out_shape=[pltpu.VMEM((len(own), examples, depth), jnp.bfloat16)] * (half_count - 1),
+        in_specs=[vmem] * len(own) + [pl.BlockSpec(memory_space=pl.ANY)],
+        out_specs=[vmem] * (half_count - 1),
+        compiler_params=pltpu.CompilerParams(vmem_limit_bytes=24 * 2**20),
+    )(*own, replay_rows)
+    passed = [
+        exchange(pack, ("half",), (half_count,), lambda half: (half_step,))
+        for half_step, pack in enumerate(packs, 1)
+    ]
+    sources = [
+        (replay_step, turn, half_step)
+        for half_step in range(half_count)
+        for replay_step, turn, _ in gathered
+    ]
 
     rows = blocks * examples
     group_rows = min(rows, 64)
     shape = (rows // holders, replay_total)
     chunks = pl.pallas_call(
-        functools.partial(score_kernel, tuple(gathered), counts),
+        functools.partial(score_kernel, sources, counts),
         out_shape=[pltpu.VMEM(shape, jnp.float32)]
         + [pltpu.VMEM(shape, jnp.bfloat16)] * (holders - 1),
-        in_specs=[vmem] * (blocks + 1),
+        in_specs=[vmem] * (len(own) + half_count),
         out_specs=[vmem] * holders,
         scratch_shapes=[
             pltpu.VMEM((rows // group_rows, group_rows, depth), jnp.bfloat16),
@@ -258,10 +297,10 @@
             bytes_accessed=2 * (rows + replay_total) * depth + 4 * rows * replay_total,
             transcendentals=0,
         ),
-    )(*gathered.values(), replay_rows)
+    )(*own, *passed, replay_rows)
 
     summed_scores = chunks[0]
-    for step in range(holders - 1, 0, -1):
+    for step in sorted(range(1, holders), key=lambda step: (step < half_count, step)):
         term = exchange(
             chunks[step], axes[1:], counts[1:], lambda half: (step // half_count, step % half_count)
         )

time: 22 us -> 21.2 us (0.964)
  waiting for transfers between devices: 7.97 us -> 6.11 us
  Pallas kernels: 3.21 us -> 4.98 us
  starting transfers between devices: 9.89 us -> 9.18 us
    ppermute x11 -> x8, waiting for transfers between devices: 7.97 us -> 6.11 us  [exchange(): return lax.ppermute(value, names, pairs)]
    pallas_call x2 -> x4, Pallas kernels: 3.21 us -> 4.98 us  [the longest x1 1.98 us: body(): pl.pallas_call(precondition_kernel, out_shape=[pltpu.VMEM((half_count, ex...]
    ppermute x11 -> x8, starting transfers between devices: 9.89 us -> 9.18 us  [exchange(): return lax.ppermute(value, names, pairs)]
  transfers between devices with their start and end apart: 11 -> 8, of which waited for: 7 -> 4; matrix products, arithmetic and copies ran while one was open for 0% -> 0% of each run, Pallas kernels for 0% -> 9%
where the time goes in v5:
time: 21.2 us; the launch traced here: 21.1 us
  starting transfers between devices  9.18 us (43%)
  waiting for transfers between devices  6.11 us (29%)
  Pallas kernels  4.98 us (23%)
  other arithmetic  0.69 us (3%)
    ppermute x8, starting transfers between devices, exchange(): return lax.ppermute(value, names, pairs)  9.18 us
    ppermute x8, waiting for transfers between devices, exchange(): return lax.ppermute(value, names, pairs)  6.11 us
    pallas_call x1, Pallas kernels, body(): pl.pallas_call(precondition_kernel, out_shape=[pltpu.VMEM((half_count, ex...  1.98 us
    pallas_call x1, Pallas kernels, body(): pl.pallas_call(copy_kernel, out_shape=pltpu.VMEM((replay_total, depth), j...  1.9 us
    pallas_call x1, Pallas kernels, body(): pl.pallas_call(functools.partial(score_kernel, sources, counts), out_shap...  1.09 us
    select_n x1, other arithmetic, body(): return jnp.where(self_pairs, jnp.zeros((), jnp.float32), summed_scores)  0.69 us
  transfers between devices with their start and end apart: 8, of which 4 were waited for; matrix products, arithmetic and copies ran while one was open for 0% of the time, Pallas kernels for 9%

profile of v5, /device:TPU:0, one launch (start us, length us, event | category | flops | bytes accessed | tf_op | source)
XLA Modules:
  0.0 21.1 jit_solution(7113555992454577532)
XLA Ops:
  0.0 2.0 %shard_map.82.after = bf16[2,8,2048]{2,1,0:T(8,128)(2,1)S(1)} custom-call(s32[8]{0:T(128)} %counts_in.1, s32[2]{0:T(128)} %slots_in.1, bf16[8,2,64,128]{3,2,1,0:T(8,128)(2,1)} %factors_in.1, f32[2,64,64]{2,1,0:T(8,128)} %output_inverse_in.1, f32[2,64,64]{2,1,0:T(8,128)} %input_inverse_in.1), custom_call_target="tpu_custom_call" | custom-call | tf_op jit(solution)/shard_map/pallas_call | solution.py:224
  2.0 5.1 %collective-permute-start.3 = (bf16[2,8,2048]{2,1,0:T(8,128)(2,1)S(1)}, bf16[2,8,2048]{2,1,0:T(8,128)(2,1)S(1)}, u32[]{:S(2)}, u32[]{:S(2)}) collective-permute-start(bf16[2,8,2048]{2,1,0:T(8,128)(2,1)S(1)} %shard_map.82.after), channel_id=1, source_target_pairs={{0,12},{1,15},{2,14},{3,13},{4,8},{5,11},{6,10},{7,9},{8,4},{9,7},... | collective-permute-start | bytes 196616 | tf_op jit(solution)/shard_map/ppermute | solution.py:34
  7.1 0.0 collective-permute-start.2
  7.1 0.6 %collective-permute-start.1 = (bf16[2,8,2048]{2,1,0:T(8,128)(2,1)S(1)}, bf16[2,8,2048]{2,1,0:T(8,128)(2,1)S(1)}, u32[]{:S(2)}, u32[]{:S(2)}) collective-permute-start(bf16[2,8,2048]{2,1,0:T(8,128)(2,1)S(1)} %shard_map.82.after), channel_id=1, source_target_pairs={{0,4},{1,7},{2,6},{3,5},{4,0},{5,3},{6,2},{7,1},{8,12},{9,15},{10,... | collective-permute-start | bytes 196616 | tf_op jit(solution)/shard_map/ppermute | solution.py:34
  7.7 0.7 %collective-permute-start = (bf16[2,8,2048]{2,1,0:T(8,128)(2,1)S(1)}, bf16[2,8,2048]{2,1,0:T(8,128)(2,1)S(1)}, u32[]{:S(2)}, u32[]{:S(2)}) collective-permute-start(bf16[2,8,2048]{2,1,0:T(8,128)(2,1)S(1)} %shard_map.82.after), channel_id=1, source_target_pairs={{0,0},{1,3},{2,2},{3,1},{4,4},{5,7},{6,6},{7,5},{8,8},{9,11},{10,1... | collective-permute-start | bytes 196616 | tf_op jit(solution)/shard_map/ppermute | solution.py:34
  8.4 1.9 %shard_map.83.refs_4_.refs_5_ = bf16[768,2048]{1,0:T(8,128)(2,1)S(1)} custom-call(bf16[768,2048]{1,0:T(8,128)(2,1)} %bitcast.1, bf16[2,8,2048]{2,1,0:T(8,128)(2,1)S(1)} %shard_map.82.after), custom_call_target="tpu_custom_call" | custom-call | bytes 6291456 | tf_op jit(solution)/shard_map/pallas_call | solution.py:248
  10.3 0.0 copy-start
  10.3 0.0 copy-start.1
  10.3 0.0 collective-permute-done.3.refs_3_
  10.3 3.1 %collective-permute-done.2.refs_2_ = bf16[2,8,2048]{2,1,0:T(8,128)(2,1)S(1)} collective-permute-done((bf16[2,8,2048]{2,1,0:T(8,128)(2,1)S(1)}, bf16[2,8,2048]{2,1,0:T(8,128)(2,1)S(1)}, u32[]{:S(2)}, u32[]{:S(2)}) %collective-permute-start.2) | collective-permute-done | bytes 65568 | tf_op jit(solution)/shard_map/ppermute | solution.py:34
  13.5 0.0 collective-permute-done.1.refs_1_
  13.5 0.0 collective-permute-done.refs_0_
  13.5 0.6 %collective-permute-start.4 = (bf16[4,8,2048]{2,1,0:T(8,128)(2,1)S(1)}, bf16[4,8,2048]{2,1,0:T(8,128)(2,1)S(1)}, u32[]{:S(2)}, u32[]{:S(2)}) collective-permute-start(bf16[4,8,2048]{2,1,0:T(8,128)(2,1)S(1)} %shard_map.84), channel_id=1, source_target_pairs={{0,1},{1,0},{2,3},{3,2},{4,5},{5,4},{6,7},{7,6},{8,9},{9,8},{10,11... | collective-permute-start | bytes 393224 | tf_op jit(solution)/shard_map/ppermute | solution.py:34
  14.1 1.0 %collective-permute-done.4.refs_4_ = bf16[4,8,2048]{2,1,0:T(8,128)(2,1)S(1)} collective-permute-done((bf16[4,8,2048]{2,1,0:T(8,128)(2,1)S(1)}, bf16[4,8,2048]{2,1,0:T(8,128)(2,1)S(1)}, u32[]{:S(2)}, u32[]{:S(2)}) %collective-permute-start.4) | collective-permute-done | bytes 131104 | tf_op jit(solution)/shard_map/ppermute | solution.py:34
  15.1 1.1 %shard_map.85 = (f32[16,768]{1,0:T(8,128)S(1)}, bf16[16,768]{1,0:T(8,128)(2,1)S(1)}, bf16[16,768]{1,0:T(8,128)(2,1)S(1)}, bf16[16,768]{1,0:T(8,128)(2,1)S(1)}) custom-call(bf16[2,8,2048]{2,1,0:T(8,128)(2,1)S(1)} %collective-permute-done.refs_0_, bf16[2,8,2048]{2,1,0:T(8,128)(2,1)S(1)} %collective-permute-done.1.refs_1_, ...), custom_call_target="tpu_custom_call" | custom-call | flops 201326592 | bytes 3604480 | tf_op jit(solution)/shard_map/pallas_call | solution.py:284
  16.2 0.9 %collective-permute-start.5 = (bf16[16,768]{1,0:T(8,128)(2,1)S(1)}, bf16[16,768]{1,0:T(8,128)(2,1)S(1)}, u32[]{:S(2)}, u32[]{:S(2)}) collective-permute-start(bf16[16,768]{1,0:T(8,128)(2,1)S(1)} %get-tuple-element.10), channel_id=1, source_target_pairs={{0,2},{1,3},{2,0},{3,1},{4,6},{5,7},{6,4},{7,5},{8,10},{9,11},{10,... | collective-permute-start | bytes 73736 | tf_op jit(solution)/shard_map/ppermute | solution.py:34
  17.1 0.9 %collective-permute-start.6 = (bf16[16,768]{1,0:T(8,128)(2,1)S(1)}, bf16[16,768]{1,0:T(8,128)(2,1)S(1)}, u32[]{:S(2)}, u32[]{:S(2)}) collective-permute-start(bf16[16,768]{1,0:T(8,128)(2,1)S(1)} %get-tuple-element.11), channel_id=1, source_target_pairs={{0,3},{1,2},{2,1},{3,0},{4,7},{5,6},{6,5},{7,4},{8,11},{9,10},{10,... | collective-permute-start | bytes 73736 | tf_op jit(solution)/shard_map/ppermute | solution.py:34
  17.9 0.4 %collective-permute-start.7 = (bf16[16,768]{1,0:T(8,128)(2,1)S(1)}, bf16[16,768]{1,0:T(8,128)(2,1)S(1)}, u32[]{:S(2)}, u32[]{:S(2)}) collective-permute-start(bf16[16,768]{1,0:T(8,128)(2,1)S(1)} %get-tuple-element.12), channel_id=1, source_target_pairs={{0,1},{1,0},{2,3},{3,2},{4,5},{5,4},{6,7},{7,6},{8,9},{9,8},{10,11... | collective-permute-start | bytes 73736 | tf_op jit(solution)/shard_map/ppermute | solution.py:34
  18.4 1.7 %collective-permute-done.5 = bf16[16,768]{1,0:T(8,128)(2,1)S(1)} collective-permute-done((bf16[16,768]{1,0:T(8,128)(2,1)S(1)}, bf16[16,768]{1,0:T(8,128)(2,1)S(1)}, u32[]{:S(2)}, u32[]{:S(2)}) %collective-permute-start.5) | collective-permute-done | bytes 24608 | tf_op jit(solution)/shard_map/ppermute | solution.py:34
  20.1 0.3 %collective-permute-done.6 = bf16[16,768]{1,0:T(8,128)(2,1)S(1)} collective-permute-done((bf16[16,768]{1,0:T(8,128)(2,1)S(1)}, bf16[16,768]{1,0:T(8,128)(2,1)S(1)}, u32[]{:S(2)}, u32[]{:S(2)}) %collective-permute-start.6) | collective-permute-done | bytes 24608 | tf_op jit(solution)/shard_map/ppermute | solution.py:34
  20.3 0.0 collective-permute-done.7
  20.3 0.0 copy-done
  20.4 0.0 copy-done.1
  20.4 0.7 %add_select_fusion = f32[16,768]{1,0:T(8,128)} fusion(bf16[16,768]{1,0:T(8,128)(2,1)S(1)} %collective-permute-done.7, bf16[16,768]{1,0:T(8,128)(2,1)S(1)} %collective-permute-done.6, f32[16,768]{1,0:T(8,128)S(1)} %get-tuple-element.9, bf16[16,768]{1,0:T(8,128)(2,1)S(1)} %collective-permute-done.5, s32[768]{0:T(1024)S(1)} %copy-done, s32[16]{0:T(128)S(1)} %copy-done.1), kind=kLoop, calls=%fused_computation | loop fusion | flops 98304 | bytes 175168 | tf_op jit(solution)/shard_map/jit(_where)/select_n | solution.py:309
  (1 shorter events, 0.0 us)
Async XLA Ops:
  2.0 8.3 %collective-permute-start.3 = (bf16[2,8,2048]{2,1,0:T(8,128)(2,1)S(1)}, bf16[2,8,2048]{2,1,0:T(8,128)(2,1)S(1)}, u32[]{:S(2)}, u32[]{:S(2)}) collective-permute-start(bf16[2,8,2048]{2,1,0:T(8,128)(2,1)S(1)} %shard_map.82.after), channel_id=1, source_target_pairs={{0,12},{1,15},{2,14},{3,13},{4,8},{5,11},{6,10},{7,9},{8,4},{9,7},... | collective-permute-start | bytes 196616 | tf_op jit(solution)/shard_map/ppermute | solution.py:34
  7.1 6.4 %collective-permute-start.2 = (bf16[2,8,2048]{2,1,0:T(8,128)(2,1)S(1)}, bf16[2,8,2048]{2,1,0:T(8,128)(2,1)S(1)}, u32[]{:S(2)}, u32[]{:S(2)}) collective-permute-start(bf16[2,8,2048]{2,1,0:T(8,128)(2,1)S(1)} %shard_map.82.after), channel_id=1, source_target_pairs={{0,8},{1,11},{2,10},{3,9},{4,12},{5,15},{6,14},{7,13},{8,0},{9,3},... | collective-permute-start | bytes 196616 | tf_op jit(solution)/shard_map/ppermute | solution.py:34
  7.1 6.4 %collective-permute-start.1 = (bf16[2,8,2048]{2,1,0:T(8,128)(2,1)S(1)}, bf16[2,8,2048]{2,1,0:T(8,128)(2,1)S(1)}, u32[]{:S(2)}, u32[]{:S(2)}) collective-permute-start(bf16[2,8,2048]{2,1,0:T(8,128)(2,1)S(1)} %shard_map.82.after), channel_id=1, source_target_pairs={{0,4},{1,7},{2,6},{3,5},{4,0},{5,3},{6,2},{7,1},{8,12},{9,15},{10,... | collective-permute-start | bytes 196616 | tf_op jit(solution)/shard_map/ppermute | solution.py:34
  7.7 5.8 %collective-permute-start = (bf16[2,8,2048]{2,1,0:T(8,128)(2,1)S(1)}, bf16[2,8,2048]{2,1,0:T(8,128)(2,1)S(1)}, u32[]{:S(2)}, u32[]{:S(2)}) collective-permute-start(bf16[2,8,2048]{2,1,0:T(8,128)(2,1)S(1)} %shard_map.82.after), channel_id=1, source_target_pairs={{0,0},{1,3},{2,2},{3,1},{4,4},{5,7},{6,6},{7,5},{8,8},{9,11},{10,1... | collective-permute-start | bytes 196616 | tf_op jit(solution)/shard_map/ppermute | solution.py:34
  10.3 10.0 %copy-start = (s32[768]{0:T(1024)S(1)}, s32[768]{0:T(1024)}, u32[]{:S(2)}) copy-start(s32[768]{0:T(1024)} %param.12) | copy-start | bytes 9220
  10.3 10.0 %copy-start.1 = (s32[16]{0:T(128)S(1)}, s32[16]{0:T(128)}, u32[]{:S(2)}) copy-start(s32[16]{0:T(128)} %param.10) | copy-start | bytes 196
  13.5 1.5 %collective-permute-start.4 = (bf16[4,8,2048]{2,1,0:T(8,128)(2,1)S(1)}, bf16[4,8,2048]{2,1,0:T(8,128)(2,1)S(1)}, u32[]{:S(2)}, u32[]{:S(2)}) collective-permute-start(bf16[4,8,2048]{2,1,0:T(8,128)(2,1)S(1)} %shard_map.84), channel_id=1, source_target_pairs={{0,1},{1,0},{2,3},{3,2},{4,5},{5,4},{6,7},{7,6},{8,9},{9,8},{10,11... | collective-permute-start | bytes 393224 | tf_op jit(solution)/shard_map/ppermute | solution.py:34
  16.2 3.9 %collective-permute-start.5 = (bf16[16,768]{1,0:T(8,128)(2,1)S(1)}, bf16[16,768]{1,0:T(8,128)(2,1)S(1)}, u32[]{:S(2)}, u32[]{:S(2)}) collective-permute-start(bf16[16,768]{1,0:T(8,128)(2,1)S(1)} %get-tuple-element.10), channel_id=1, source_target_pairs={{0,2},{1,3},{2,0},{3,1},{4,6},{5,7},{6,4},{7,5},{8,10},{9,11},{10,... | collective-permute-start | bytes 73736 | tf_op jit(solution)/shard_map/ppermute | solution.py:34
  17.1 3.3 %collective-permute-start.6 = (bf16[16,768]{1,0:T(8,128)(2,1)S(1)}, bf16[16,768]{1,0:T(8,128)(2,1)S(1)}, u32[]{:S(2)}, u32[]{:S(2)}) collective-permute-start(bf16[16,768]{1,0:T(8,128)(2,1)S(1)} %get-tuple-element.11), channel_id=1, source_target_pairs={{0,3},{1,2},{2,1},{3,0},{4,7},{5,6},{6,5},{7,4},{8,11},{9,10},{10,... | collective-permute-start | bytes 73736 | tf_op jit(solution)/shard_map/ppermute | solution.py:34
  17.9 2.4 %collective-permute-start.7 = (bf16[16,768]{1,0:T(8,128)(2,1)S(1)}, bf16[16,768]{1,0:T(8,128)(2,1)S(1)}, u32[]{:S(2)}, u32[]{:S(2)}) collective-permute-start(bf16[16,768]{1,0:T(8,128)(2,1)S(1)} %get-tuple-element.12), channel_id=1, source_target_pairs={{0,1},{1,0},{2,3},{3,2},{4,5},{5,4},{6,7},{7,6},{8,9},{9,8},{10,11... | collective-permute-start | bytes 73736 | tf_op jit(solution)/shard_map/ppermute | solution.py:34

commit v6 on v5

--- a/solution.py
+++ b/solution.py
@@ -30,7 +30,8 @@
         for spot, count, step in zip(place, counts, steps(place[-1])):
             source = source * count + spot
             target = target * count + partner(spot, step, count)
-        pairs.append((source, target))
+        if target != source:
+            pairs.append((source, target))
     return lax.ppermute(value, names, pairs)
 
 
@@ -72,7 +73,7 @@
     share = groups // halves
     module_place = lax.axis_index("module")
     half_place = lax.axis_index("half")
-    for copy_in in copies_in:
+    for copy_in in copies_in[:-1]:
         copy_in.wait()
 
     place = (examples, examples * tokens)
@@ -83,28 +84,31 @@
         kept |= (example == e) & (column >= e * tokens) & (column < e * tokens + counts[e])
     lane = lax.broadcasted_iota(jnp.int32, (examples * tokens, LANES), 1)
 
-    for turn, target in enumerate(rows):
+    weights = []
+    for turn in range(len(rows)):
         module = slots[partner(module_place, turn * halves + half_place, modules)]
-        tokens_in = factors[:, pl.ds(module, 1)].reshape(examples * tokens, width)
-        twice = jnp.concatenate([tokens_in, tokens_in], axis=1)
-
         right = input_inverse[module]
         right = jnp.concatenate([right] * pack, axis=1)
         right = jnp.concatenate([right, jnp.zeros((features, LANES), jnp.float32)], axis=0)
         right = jnp.concatenate(split(right), axis=0)
-        inner = jnp.dot(twice, right, preferred_element_type=jnp.float32)
-
         left = output_inverse[module]
         left = jnp.concatenate([jnp.zeros((features, features), jnp.float32), left], axis=1)
+        left = jnp.concatenate(split(left), axis=1).astype(jnp.float32)
         left = jnp.concatenate(
             [
-                jnp.broadcast_to(left[pack * q + p : pack * q + p + 1], (examples, width))
+                jnp.broadcast_to(left[pack * q + p : pack * q + p + 1], (examples, 2 * width))
                 for p in range(pack)
                 for q in range(groups)
             ],
             axis=0,
-        )
-        left = jnp.concatenate(split(left), axis=1)
+        ).astype(jnp.bfloat16)
+        weights.append((module, left, right))
+
+    copies_in[-1].wait()
+    for target, (module, left, right) in zip(rows, weights):
+        tokens_in = factors[:, pl.ds(module, 1)].reshape(examples * tokens, width)
+        twice = jnp.concatenate([tokens_in, tokens_in], axis=1)
+        inner = jnp.dot(twice, right, preferred_element_type=jnp.float32)
         outer = lax.dot_general(
             left, twice, (((1,), (1,)), ((), ())), preferred_element_type=jnp.float32
         )
@@ -116,12 +120,13 @@
             outer_high, outer_low = split(outer[p * groups * examples : (p + 1) * groups * examples])
             mine = (lane >= p * features) & (lane < (p + 1) * features)
             inner_high, inner_low = split(jnp.where(mine, inner, 0.0))
-            for one, other in (
-                (outer_high, inner_high),
-                (outer_high, inner_low),
-                (outer_low, inner_high),
-            ):
-                total += jnp.dot(one, other, preferred_element_type=jnp.float32)
+            both = jnp.dot(
+                outer_high,
+                jnp.concatenate([inner_high, inner_low], axis=1),
+                preferred_element_type=jnp.float32,
+            )
+            total += both[:, :LANES] + both[:, LANES:]
+            total += jnp.dot(outer_low, inner_high, preferred_element_type=jnp.float32)
         total = total.astype(jnp.bfloat16)
         for q in range(groups):
             block = total[q * examples : (q + 1) * examples]
@@ -136,30 +141,32 @@
 
 def pack_kernel(half_count, *refs):
     half_place = lax.axis_index("half")
-    blocks, packs = refs[:-half_count], refs[1 - half_count :]
+    kept, blocks, packs = refs[0], refs[1:-half_count], refs[1 - half_count :]
     for half_step, pack in enumerate(packs, 1):
         needed = partner(half_place, half_step, half_count)
-        for number, block in enumerate(blocks):
+        pack[0] = jnp.where(half_place == 0, kept[needed], blocks[0][needed])
+        for number, block in enumerate(blocks[1:], 1):
             pack[number] = block[needed]
 
 
 def score_kernel(sources, holders, *refs):
     replay_count, module_count, half_count = holders
     own_count = len(sources) // half_count
-    own, passed = refs[:own_count], refs[own_count : own_count + half_count - 1]
-    replay_rows, *chunks, joined, partials = refs[own_count + half_count - 1 :]
+    kept, own, passed = refs[0], refs[1 : 1 + own_count], refs[1 + own_count : own_count + half_count]
+    replay_rows, *chunks, joined, partials = refs[own_count + half_count :]
     examples = own[0].shape[-2]
     replay_place = lax.axis_index("replay")
     module_place = lax.axis_index("module")
     half_place = lax.axis_index("half")
 
     per_group = joined.shape[1] // examples
-    blocks = [block.at[half_place] for block in own]
-    blocks += [pack.at[number] for pack in passed for number in range(own_count)]
+    blocks = [block[half_place] for block in own]
+    blocks[0] = jnp.where(half_place == 0, kept[half_place], blocks[0])
+    blocks += [pack[number] for pack in passed for number in range(own_count)]
     for group in range(joined.shape[0]):
         joined[group] = jnp.concatenate(
             [
-                block[...].astype(jnp.float32)
+                block.astype(jnp.float32)
                 for block in blocks[group * per_group : (group + 1) * per_group]
             ],
             axis=0,
@@ -264,10 +271,10 @@
     packs = pl.pallas_call(
         functools.partial(pack_kernel, half_count),
         out_shape=[pltpu.VMEM((len(own), examples, depth), jnp.bfloat16)] * (half_count - 1),
-        in_specs=[vmem] * len(own) + [pl.BlockSpec(memory_space=pl.ANY)],
+        in_specs=[vmem] * (1 + len(own)) + [pl.BlockSpec(memory_space=pl.ANY)],
         out_specs=[vmem] * (half_count - 1),
         compiler_params=pltpu.CompilerParams(vmem_limit_bytes=24 * 2**20),
-    )(*own, replay_rows)
+    )(outgoing[0], *own, replay_rows)
     passed = [
         exchange(pack, ("half",), (half_count,), lambda half: (half_step,))
         for half_step, pack in enumerate(packs, 1)
@@ -285,7 +292,7 @@
         functools.partial(score_kernel, sources, counts),
         out_shape=[pltpu.VMEM(shape, jnp.float32)]
         + [pltpu.VMEM(shape, jnp.bfloat16)] * (holders - 1),
-        in_specs=[vmem] * (len(own) + half_count),
+        in_specs=[vmem] * (1 + len(own) + half_count),
         out_specs=[vmem] * holders,
         scratch_shapes=[
             pltpu.VMEM((rows // group_rows, group_rows, depth), jnp.bfloat16),
@@ -297,7 +304,7 @@
             bytes_accessed=2 * (rows + replay_total) * depth + 4 * rows * replay_total,
             transcendentals=0,
         ),
-    )(*own, *passed, replay_rows)
+    )(outgoing[0], *own, *passed, replay_rows)
 
     summed_scores = chunks[0]
     for step in sorted(range(1, holders), key=lambda step: (step < half_count, step)):

time: 21.2 us -> 21 us (level)
    pallas_call x1, Pallas kernels: 1.98 us -> 1.77 us  [body(): pl.pallas_call(precondition_kernel, out_shape=[pltpu.VMEM((half_count, ex...]
where the time goes in v6:
time: 21 us; the launch traced here: 20.8 us
  starting transfers between devices  9.19 us (44%)
  waiting for transfers between devices  6.1 us (29%)
  Pallas kernels  4.77 us (23%)
  other arithmetic  0.69 us (3%)
    ppermute x8, starting transfers between devices, exchange(): return lax.ppermute(value, names, pairs)  9.19 us
    ppermute x8, waiting for transfers between devices, exchange(): return lax.ppermute(value, names, pairs)  6.1 us
    pallas_call x1, Pallas kernels, body(): pl.pallas_call(copy_kernel, out_shape=pltpu.VMEM((replay_total, depth), j...  1.9 us
    pallas_call x1, Pallas kernels, body(): pl.pallas_call(precondition_kernel, out_shape=[pltpu.VMEM((half_count, ex...  1.77 us
    pallas_call x1, Pallas kernels, body(): pl.pallas_call(functools.partial(score_kernel, sources, counts), out_shap...  1.09 us
    select_n x1, other arithmetic, body(): return jnp.where(self_pairs, jnp.zeros((), jnp.float32), summed_scores)  0.69 us
  transfers between devices with their start and end apart: 8, of which 4 were waited for; matrix products, arithmetic and copies ran while one was open for 0% of the time, Pallas kernels for 9%

profile of v6, /device:TPU:0, one launch (start us, length us, event | category | flops | bytes accessed | tf_op | source)
XLA Modules:
  0.0 20.8 jit_solution(9404132698035598631)
XLA Ops:
  0.0 1.8 %shard_map.82.after.refs_0_ = bf16[2,8,2048]{2,1,0:T(8,128)(2,1)S(1)} custom-call(s32[8]{0:T(128)} %counts_in.1, s32[2]{0:T(128)} %slots_in.1, bf16[8,2,64,128]{3,2,1,0:T(8,128)(2,1)} %factors_in.1, f32[2,64,64]{2,1,0:T(8,128)} %output_inverse_in.1, f32[2,64,64]{2,1,0:T(8,128)} %input_inverse_in.1), custom_call_target="tpu_custom_call" | custom-call | tf_op jit(solution)/shard_map/pallas_call | solution.py:231
  1.8 5.1 %collective-permute-start.3 = (bf16[2,8,2048]{2,1,0:T(8,128)(2,1)S(1)}, bf16[2,8,2048]{2,1,0:T(8,128)(2,1)S(1)}, u32[]{:S(2)}, u32[]{:S(2)}) collective-permute-start(bf16[2,8,2048]{2,1,0:T(8,128)(2,1)S(1)} %shard_map.82.after.refs_0_), channel_id=1, source_target_pairs={{0,12},{1,15},{2,14},{3,13},{4,8},{5,11},{6,10},{7,9},{8,4},{9,7},... | collective-permute-start | bytes 196616 | tf_op jit(solution)/shard_map/ppermute | solution.py:35
  6.9 0.0 collective-permute-start.2
  6.9 0.6 %collective-permute-start.1 = (bf16[2,8,2048]{2,1,0:T(8,128)(2,1)S(1)}, bf16[2,8,2048]{2,1,0:T(8,128)(2,1)S(1)}, u32[]{:S(2)}, u32[]{:S(2)}) collective-permute-start(bf16[2,8,2048]{2,1,0:T(8,128)(2,1)S(1)} %shard_map.82.after.refs_0_), channel_id=1, source_target_pairs={{0,4},{1,7},{2,6},{3,5},{4,0},{5,3},{6,2},{7,1},{8,12},{9,15},{10,... | collective-permute-start | bytes 196616 | tf_op jit(solution)/shard_map/ppermute | solution.py:35
  7.5 0.7 %collective-permute-start = (bf16[2,8,2048]{2,1,0:T(8,128)(2,1)S(1)}, bf16[2,8,2048]{2,1,0:T(8,128)(2,1)S(1)}, u32[]{:S(2)}, u32[]{:S(2)}) collective-permute-start(bf16[2,8,2048]{2,1,0:T(8,128)(2,1)S(1)} %shard_map.82.after.refs_0_), channel_id=1, source_target_pairs={{1,3},{3,1},{5,7},{7,5},{9,11},{11,9},{13,15},{15,13},{17,19},{19,... | collective-permute-start | bytes 196616 | tf_op jit(solution)/shard_map/ppermute | solution.py:35
  8.2 1.9 %shard_map.83.refs_5_.refs_6_ = bf16[768,2048]{1,0:T(8,128)(2,1)S(1)} custom-call(bf16[768,2048]{1,0:T(8,128)(2,1)} %bitcast.1, bf16[2,8,2048]{2,1,0:T(8,128)(2,1)S(1)} %shard_map.82.after.refs_0_), custom_call_target="tpu_custom_call" | custom-call | bytes 6291456 | tf_op jit(solution)/shard_map/pallas_call | solution.py:255
  10.1 0.0 copy-start
  10.1 0.0 copy-start.1
  10.1 0.0 collective-permute-done.3.refs_4_
  10.1 3.1 %collective-permute-done.2.refs_3_ = bf16[2,8,2048]{2,1,0:T(8,128)(2,1)S(1)} collective-permute-done((bf16[2,8,2048]{2,1,0:T(8,128)(2,1)S(1)}, bf16[2,8,2048]{2,1,0:T(8,128)(2,1)S(1)}, u32[]{:S(2)}, u32[]{:S(2)}) %collective-permute-start.2) | collective-permute-done | bytes 65568 | tf_op jit(solution)/shard_map/ppermute | solution.py:35
  13.3 0.0 collective-permute-done.1.refs_2_
  13.3 0.0 collective-permute-done.refs_1_
  13.3 0.6 %collective-permute-start.4 = (bf16[4,8,2048]{2,1,0:T(8,128)(2,1)S(1)}, bf16[4,8,2048]{2,1,0:T(8,128)(2,1)S(1)}, u32[]{:S(2)}, u32[]{:S(2)}) collective-permute-start(bf16[4,8,2048]{2,1,0:T(8,128)(2,1)S(1)} %shard_map.84), channel_id=1, source_target_pairs={{0,1},{1,0},{2,3},{3,2},{4,5},{5,4},{6,7},{7,6},{8,9},{9,8},{10,11... | collective-permute-start | bytes 393224 | tf_op jit(solution)/shard_map/ppermute | solution.py:35
  13.9 1.0 %collective-permute-done.4.refs_5_ = bf16[4,8,2048]{2,1,0:T(8,128)(2,1)S(1)} collective-permute-done((bf16[4,8,2048]{2,1,0:T(8,128)(2,1)S(1)}, bf16[4,8,2048]{2,1,0:T(8,128)(2,1)S(1)}, u32[]{:S(2)}, u32[]{:S(2)}) %collective-permute-start.4) | collective-permute-done | bytes 131104 | tf_op jit(solution)/shard_map/ppermute | solution.py:35
  14.8 1.1 %shard_map.85 = (f32[16,768]{1,0:T(8,128)S(1)}, bf16[16,768]{1,0:T(8,128)(2,1)S(1)}, bf16[16,768]{1,0:T(8,128)(2,1)S(1)}, bf16[16,768]{1,0:T(8,128)(2,1)S(1)}) custom-call(bf16[2,8,2048]{2,1,0:T(8,128)(2,1)S(1)} %shard_map.82.after.refs_0_, bf16[2,8,2048]{2,1,0:T(8,128)(2,1)S(1)} %collective-permute-done.refs_1_, ...), custom_call_target="tpu_custom_call" | custom-call | flops 201326592 | bytes 3604480 | tf_op jit(solution)/shard_map/pallas_call | solution.py:291
  15.9 0.9 %collective-permute-start.5 = (bf16[16,768]{1,0:T(8,128)(2,1)S(1)}, bf16[16,768]{1,0:T(8,128)(2,1)S(1)}, u32[]{:S(2)}, u32[]{:S(2)}) collective-permute-start(bf16[16,768]{1,0:T(8,128)(2,1)S(1)} %get-tuple-element.10), channel_id=1, source_target_pairs={{0,2},{1,3},{2,0},{3,1},{4,6},{5,7},{6,4},{7,5},{8,10},{9,11},{10,... | collective-permute-start | bytes 73736 | tf_op jit(solution)/shard_map/ppermute | solution.py:35
  16.9 0.9 %collective-permute-start.6 = (bf16[16,768]{1,0:T(8,128)(2,1)S(1)}, bf16[16,768]{1,0:T(8,128)(2,1)S(1)}, u32[]{:S(2)}, u32[]{:S(2)}) collective-permute-start(bf16[16,768]{1,0:T(8,128)(2,1)S(1)} %get-tuple-element.11), channel_id=1, source_target_pairs={{0,3},{1,2},{2,1},{3,0},{4,7},{5,6},{6,5},{7,4},{8,11},{9,10},{10,... | collective-permute-start | bytes 73736 | tf_op jit(solution)/shard_map/ppermute | solution.py:35
  17.7 0.4 %collective-permute-start.7 = (bf16[16,768]{1,0:T(8,128)(2,1)S(1)}, bf16[16,768]{1,0:T(8,128)(2,1)S(1)}, u32[]{:S(2)}, u32[]{:S(2)}) collective-permute-start(bf16[16,768]{1,0:T(8,128)(2,1)S(1)} %get-tuple-element.12), channel_id=1, source_target_pairs={{0,1},{1,0},{2,3},{3,2},{4,5},{5,4},{6,7},{7,6},{8,9},{9,8},{10,11... | collective-permute-start | bytes 73736 | tf_op jit(solution)/shard_map/ppermute | solution.py:35
  18.2 1.7 %collective-permute-done.5 = bf16[16,768]{1,0:T(8,128)(2,1)S(1)} collective-permute-done((bf16[16,768]{1,0:T(8,128)(2,1)S(1)}, bf16[16,768]{1,0:T(8,128)(2,1)S(1)}, u32[]{:S(2)}, u32[]{:S(2)}) %collective-permute-start.5) | collective-permute-done | bytes 24608 | tf_op jit(solution)/shard_map/ppermute | solution.py:35
  19.8 0.3 %collective-permute-done.6 = bf16[16,768]{1,0:T(8,128)(2,1)S(1)} collective-permute-done((bf16[16,768]{1,0:T(8,128)(2,1)S(1)}, bf16[16,768]{1,0:T(8,128)(2,1)S(1)}, u32[]{:S(2)}, u32[]{:S(2)}) %collective-permute-start.6) | collective-permute-done | bytes 24608 | tf_op jit(solution)/shard_map/ppermute | solution.py:35
  20.1 0.0 collective-permute-done.7
  20.1 0.0 copy-done
  20.1 0.0 copy-done.1
  20.1 0.7 %add_select_fusion = f32[16,768]{1,0:T(8,128)} fusion(bf16[16,768]{1,0:T(8,128)(2,1)S(1)} %collective-permute-done.7, bf16[16,768]{1,0:T(8,128)(2,1)S(1)} %collective-permute-done.6, f32[16,768]{1,0:T(8,128)S(1)} %get-tuple-element.9, bf16[16,768]{1,0:T(8,128)(2,1)S(1)} %collective-permute-done.5, s32[768]{0:T(1024)S(1)} %copy-done, s32[16]{0:T(128)S(1)} %copy-done.1), kind=kLoop, calls=%fused_computation | loop fusion | flops 98304 | bytes 175168 | tf_op jit(solution)/shard_map/jit(_where)/select_n | solution.py:316
  (1 shorter events, 0.0 us)
Async XLA Ops:
  1.8 8.3 %collective-permute-start.3 = (bf16[2,8,2048]{2,1,0:T(8,128)(2,1)S(1)}, bf16[2,8,2048]{2,1,0:T(8,128)(2,1)S(1)}, u32[]{:S(2)}, u32[]{:S(2)}) collective-permute-start(bf16[2,8,2048]{2,1,0:T(8,128)(2,1)S(1)} %shard_map.82.after.refs_0_), channel_id=1, source_target_pairs={{0,12},{1,15},{2,14},{3,13},{4,8},{5,11},{6,10},{7,9},{8,4},{9,7},... | collective-permute-start | bytes 196616 | tf_op jit(solution)/shard_map/ppermute | solution.py:35
  6.9 6.4 %collective-permute-start.2 = (bf16[2,8,2048]{2,1,0:T(8,128)(2,1)S(1)}, bf16[2,8,2048]{2,1,0:T(8,128)(2,1)S(1)}, u32[]{:S(2)}, u32[]{:S(2)}) collective-permute-start(bf16[2,8,2048]{2,1,0:T(8,128)(2,1)S(1)} %shard_map.82.after.refs_0_), channel_id=1, source_target_pairs={{0,8},{1,11},{2,10},{3,9},{4,12},{5,15},{6,14},{7,13},{8,0},{9,3},... | collective-permute-start | bytes 196616 | tf_op jit(solution)/shard_map/ppermute | solution.py:35
  6.9 6.4 %collective-permute-start.1 = (bf16[2,8,2048]{2,1,0:T(8,128)(2,1)S(1)}, bf16[2,8,2048]{2,1,0:T(8,128)(2,1)S(1)}, u32[]{:S(2)}, u32[]{:S(2)}) collective-permute-start(bf16[2,8,2048]{2,1,0:T(8,128)(2,1)S(1)} %shard_map.82.after.refs_0_), channel_id=1, source_target_pairs={{0,4},{1,7},{2,6},{3,5},{4,0},{5,3},{6,2},{7,1},{8,12},{9,15},{10,... | collective-permute-start | bytes 196616 | tf_op jit(solution)/shard_map/ppermute | solution.py:35
  7.5 5.7 %collective-permute-start = (bf16[2,8,2048]{2,1,0:T(8,128)(2,1)S(1)}, bf16[2,8,2048]{2,1,0:T(8,128)(2,1)S(1)}, u32[]{:S(2)}, u32[]{:S(2)}) collective-permute-start(bf16[2,8,2048]{2,1,0:T(8,128)(2,1)S(1)} %shard_map.82.after.refs_0_), channel_id=1, source_target_pairs={{1,3},{3,1},{5,7},{7,5},{9,11},{11,9},{13,15},{15,13},{17,19},{19,... | collective-permute-start | bytes 196616 | tf_op jit(solution)/shard_map/ppermute | solution.py:35
  10.1 10.0 %copy-start = (s32[768]{0:T(1024)S(1)}, s32[768]{0:T(1024)}, u32[]{:S(2)}) copy-start(s32[768]{0:T(1024)} %param.12) | copy-start | bytes 9220
  10.1 10.0 %copy-start.1 = (s32[16]{0:T(128)S(1)}, s32[16]{0:T(128)}, u32[]{:S(2)}) copy-start(s32[16]{0:T(128)} %param.10) | copy-start | bytes 196
  13.3 1.5 %collective-permute-start.4 = (bf16[4,8,2048]{2,1,0:T(8,128)(2,1)S(1)}, bf16[4,8,2048]{2,1,0:T(8,128)(2,1)S(1)}, u32[]{:S(2)}, u32[]{:S(2)}) collective-permute-start(bf16[4,8,2048]{2,1,0:T(8,128)(2,1)S(1)} %shard_map.84), channel_id=1, source_target_pairs={{0,1},{1,0},{2,3},{3,2},{4,5},{5,4},{6,7},{7,6},{8,9},{9,8},{10,11... | collective-permute-start | bytes 393224 | tf_op jit(solution)/shard_map/ppermute | solution.py:35
  15.9 3.9 %collective-permute-start.5 = (bf16[16,768]{1,0:T(8,128)(2,1)S(1)}, bf16[16,768]{1,0:T(8,128)(2,1)S(1)}, u32[]{:S(2)}, u32[]{:S(2)}) collective-permute-start(bf16[16,768]{1,0:T(8,128)(2,1)S(1)} %get-tuple-element.10), channel_id=1, source_target_pairs={{0,2},{1,3},{2,0},{3,1},{4,6},{5,7},{6,4},{7,5},{8,10},{9,11},{10,... | collective-permute-start | bytes 73736 | tf_op jit(solution)/shard_map/ppermute | solution.py:35
  16.9 3.3 %collective-permute-start.6 = (bf16[16,768]{1,0:T(8,128)(2,1)S(1)}, bf16[16,768]{1,0:T(8,128)(2,1)S(1)}, u32[]{:S(2)}, u32[]{:S(2)}) collective-permute-start(bf16[16,768]{1,0:T(8,128)(2,1)S(1)} %get-tuple-element.11), channel_id=1, source_target_pairs={{0,3},{1,2},{2,1},{3,0},{4,7},{5,6},{6,5},{7,4},{8,11},{9,10},{10,... | collective-permute-start | bytes 73736 | tf_op jit(solution)/shard_map/ppermute | solution.py:35
  17.7 2.4 %collective-permute-start.7 = (bf16[16,768]{1,0:T(8,128)(2,1)S(1)}, bf16[16,768]{1,0:T(8,128)(2,1)S(1)}, u32[]{:S(2)}, u32[]{:S(2)}) collective-permute-start(bf16[16,768]{1,0:T(8,128)(2,1)S(1)} %get-tuple-element.12), channel_id=1, source_target_pairs={{0,1},{1,0},{2,3},{3,2},{4,5},{5,4},{6,7},{7,6},{8,9},{9,8},{10,11... | collective-permute-start | bytes 73736 | tf_op jit(solution)/shard_map/ppermute | solution.py:35

commit v7 on v6

--- a/solution.py
+++ b/solution.py
@@ -1,5 +1,6 @@
 import functools
 import itertools
+import math
 
 import jax
 import jax.numpy as jnp
@@ -40,6 +41,22 @@
     return high, (value - high.astype(jnp.float32)).astype(jnp.bfloat16)
 
 
+def cut(source, target, pieces):
+    size = source.shape[0] // pieces
+    places = [pl.ds(piece * size, size) for piece in range(pieces)]
+    return tuple((source.at[place], target.at[place]) for place in places)
+
+
+def start_copies(pairs, arrived, first):
+    copies = [
+        pltpu.make_async_copy(source, target, arrived.at[first + number])
+        for number, (source, target) in enumerate(pairs)
+    ]
+    for copy in copies:
+        copy.start()
+    return copies
+
+
 def precondition_kernel(
     counts_in,
     slots_in,
@@ -50,20 +67,11 @@
 ):
     counts, slots, factors, output_inverse, input_inverse, arrived = rest[-6:]
     rows = rest[:-6]
-    copies_in = [
-        pltpu.make_async_copy(source, target, arrived.at[number])
-        for number, (source, target) in enumerate(
-            (
-                (slots_in, slots),
-                (counts_in, counts),
-                (input_inverse_in, input_inverse),
-                (output_inverse_in, output_inverse),
-                (factors_in, factors),
-            )
-        )
-    ]
-    for copy_in in copies_in:
-        copy_in.start()
+    small = ((slots_in, slots), (counts_in, counts))
+    small += cut(input_inverse_in, input_inverse, input_inverse.shape[0])
+    small += cut(output_inverse_in, output_inverse, output_inverse.shape[0])
+    early = start_copies(small, arrived, 0)
+    late = start_copies(cut(factors_in, factors, factors.shape[0]), arrived, len(small))
 
     examples, modules, tokens, width = factors.shape
     features = width // 2
@@ -73,7 +81,7 @@
     share = groups // halves
     module_place = lax.axis_index("module")
     half_place = lax.axis_index("half")
-    for copy_in in copies_in[:-1]:
+    for copy_in in early:
         copy_in.wait()
 
     place = (examples, examples * tokens)
@@ -104,7 +112,8 @@
         ).astype(jnp.bfloat16)
         weights.append((module, left, right))
 
-    copies_in[-1].wait()
+    for copy_in in late:
+        copy_in.wait()
     for target, (module, left, right) in zip(rows, weights):
         tokens_in = factors[:, pl.ds(module, 1)].reshape(examples * tokens, width)
         twice = jnp.concatenate([tokens_in, tokens_in], axis=1)
@@ -134,9 +143,8 @@
 
 
 def copy_kernel(source, after, target, arrived):
-    copy_in = pltpu.make_async_copy(source, target, arrived)
-    copy_in.start()
-    copy_in.wait()
+    for copy in start_copies(cut(source, target, arrived.shape[0]), arrived, 0):
+        copy.wait()
 
 
 def pack_kernel(half_count, *refs):
@@ -239,7 +247,7 @@
             pltpu.VMEM(new_factors.shape, jnp.bfloat16),
             pltpu.VMEM(output_inverse.shape, jnp.float32),
             pltpu.VMEM(input_inverse.shape, jnp.float32),
-            pltpu.SemaphoreType.DMA((len(operands),)),
+            pltpu.SemaphoreType.DMA((2 + 2 * module_count + examples,)),
         ],
         compiler_params=pltpu.CompilerParams(vmem_limit_bytes=16 * 2**20),
     )(*[pltpu.with_memory_space_constraint(operand, pltpu.HBM) for operand in operands])
@@ -257,7 +265,7 @@
         out_shape=pltpu.VMEM((replay_total, depth), jnp.bfloat16),
         in_specs=[hbm, vmem],
         out_specs=vmem,
-        scratch_shapes=[pltpu.SemaphoreType.DMA],
+        scratch_shapes=[pltpu.SemaphoreType.DMA((math.gcd(replay_total // 16, 8),))],
         compiler_params=pltpu.CompilerParams(vmem_limit_bytes=2**20),
         cost_estimate=pl.CostEstimate(
             flops=0, bytes_accessed=4 * replay_total * depth, transcendentals=0

time: 21 us -> 21 us (level)
  no operation moved by 1% of the time
where the time goes in v7:
time: 21 us; the launch traced here: 20.8 us
  starting transfers between devices  9.19 us (44%)
  waiting for transfers between devices  6.1 us (29%)
  Pallas kernels  4.74 us (23%)
  other arithmetic  0.69 us (3%)
    ppermute x8, starting transfers between devices, exchange(): return lax.ppermute(value, names, pairs)  9.19 us
    ppermute x8, waiting for transfers between devices, exchange(): return lax.ppermute(value, names, pairs)  6.1 us
    pallas_call x1, Pallas kernels, body(): pl.pallas_call(copy_kernel, out_shape=pltpu.VMEM((replay_total, depth), j...  1.9 us
    pallas_call x1, Pallas kernels, body(): pl.pallas_call(precondition_kernel, out_shape=[pltpu.VMEM((half_count, ex...  1.75 us
    pallas_call x1, Pallas kernels, body(): pl.pallas_call(functools.partial(score_kernel, sources, counts), out_shap...  1.09 us
    select_n x1, other arithmetic, body(): return jnp.where(self_pairs, jnp.zeros((), jnp.float32), summed_scores)  0.69 us
  transfers between devices with their start and end apart: 8, of which 4 were waited for; matrix products, arithmetic and copies ran while one was open for 0% of the time, Pallas kernels for 9%

profile of v7, /device:TPU:0, one launch (start us, length us, event | category | flops | bytes accessed | tf_op | source)
XLA Modules:
  0.0 20.8 jit_solution(14599658154759729892)
XLA Ops:
  0.0 1.7 %shard_map.82.after.refs_0_ = bf16[2,8,2048]{2,1,0:T(8,128)(2,1)S(1)} custom-call(s32[8]{0:T(128)} %counts_in.1, s32[2]{0:T(128)} %slots_in.1, bf16[8,2,64,128]{3,2,1,0:T(8,128)(2,1)} %factors_in.1, f32[2,64,64]{2,1,0:T(8,128)} %output_inverse_in.1, f32[2,64,64]{2,1,0:T(8,128)} %input_inverse_in.1), custom_call_target="tpu_custom_call" | custom-call | tf_op jit(solution)/shard_map/pallas_call | solution.py:239
  1.8 5.1 %collective-permute-start.3 = (bf16[2,8,2048]{2,1,0:T(8,128)(2,1)S(1)}, bf16[2,8,2048]{2,1,0:T(8,128)(2,1)S(1)}, u32[]{:S(2)}, u32[]{:S(2)}) collective-permute-start(bf16[2,8,2048]{2,1,0:T(8,128)(2,1)S(1)} %shard_map.82.after.refs_0_), channel_id=1, source_target_pairs={{0,12},{1,15},{2,14},{3,13},{4,8},{5,11},{6,10},{7,9},{8,4},{9,7},... | collective-permute-start | bytes 196616 | tf_op jit(solution)/shard_map/ppermute | solution.py:36
  6.9 0.0 collective-permute-start.2
  6.9 0.6 %collective-permute-start.1 = (bf16[2,8,2048]{2,1,0:T(8,128)(2,1)S(1)}, bf16[2,8,2048]{2,1,0:T(8,128)(2,1)S(1)}, u32[]{:S(2)}, u32[]{:S(2)}) collective-permute-start(bf16[2,8,2048]{2,1,0:T(8,128)(2,1)S(1)} %shard_map.82.after.refs_0_), channel_id=1, source_target_pairs={{0,4},{1,7},{2,6},{3,5},{4,0},{5,3},{6,2},{7,1},{8,12},{9,15},{10,... | collective-permute-start | bytes 196616 | tf_op jit(solution)/shard_map/ppermute | solution.py:36
  7.5 0.7 %collective-permute-start = (bf16[2,8,2048]{2,1,0:T(8,128)(2,1)S(1)}, bf16[2,8,2048]{2,1,0:T(8,128)(2,1)S(1)}, u32[]{:S(2)}, u32[]{:S(2)}) collective-permute-start(bf16[2,8,2048]{2,1,0:T(8,128)(2,1)S(1)} %shard_map.82.after.refs_0_), channel_id=1, source_target_pairs={{1,3},{3,1},{5,7},{7,5},{9,11},{11,9},{13,15},{15,13},{17,19},{19,... | collective-permute-start | bytes 196616 | tf_op jit(solution)/shard_map/ppermute | solution.py:36
  8.2 1.9 %shard_map.83.refs_5_.refs_6_ = bf16[768,2048]{1,0:T(8,128)(2,1)S(1)} custom-call(bf16[768,2048]{1,0:T(8,128)(2,1)} %bitcast.1, bf16[2,8,2048]{2,1,0:T(8,128)(2,1)S(1)} %shard_map.82.after.refs_0_), custom_call_target="tpu_custom_call" | custom-call | bytes 6291456 | tf_op jit(solution)/shard_map/pallas_call | solution.py:263
  10.1 0.0 copy-start
  10.1 0.0 copy-start.1
  10.1 0.0 collective-permute-done.3.refs_4_
  10.1 3.1 %collective-permute-done.2.refs_3_ = bf16[2,8,2048]{2,1,0:T(8,128)(2,1)S(1)} collective-permute-done((bf16[2,8,2048]{2,1,0:T(8,128)(2,1)S(1)}, bf16[2,8,2048]{2,1,0:T(8,128)(2,1)S(1)}, u32[]{:S(2)}, u32[]{:S(2)}) %collective-permute-start.2) | collective-permute-done | bytes 65568 | tf_op jit(solution)/shard_map/ppermute | solution.py:36
  13.3 0.0 collective-permute-done.1.refs_2_
  13.3 0.0 collective-permute-done.refs_1_
  13.3 0.6 %collective-permute-start.4 = (bf16[4,8,2048]{2,1,0:T(8,128)(2,1)S(1)}, bf16[4,8,2048]{2,1,0:T(8,128)(2,1)S(1)}, u32[]{:S(2)}, u32[]{:S(2)}) collective-permute-start(bf16[4,8,2048]{2,1,0:T(8,128)(2,1)S(1)} %shard_map.84), channel_id=1, source_target_pairs={{0,1},{1,0},{2,3},{3,2},{4,5},{5,4},{6,7},{7,6},{8,9},{9,8},{10,11... | collective-permute-start | bytes 393224 | tf_op jit(solution)/shard_map/ppermute | solution.py:36
  13.8 1.0 %collective-permute-done.4.refs_5_ = bf16[4,8,2048]{2,1,0:T(8,128)(2,1)S(1)} collective-permute-done((bf16[4,8,2048]{2,1,0:T(8,128)(2,1)S(1)}, bf16[4,8,2048]{2,1,0:T(8,128)(2,1)S(1)}, u32[]{:S(2)}, u32[]{:S(2)}) %collective-permute-start.4) | collective-permute-done | bytes 131104 | tf_op jit(solution)/shard_map/ppermute | solution.py:36
  14.8 1.1 %shard_map.85 = (f32[16,768]{1,0:T(8,128)S(1)}, bf16[16,768]{1,0:T(8,128)(2,1)S(1)}, bf16[16,768]{1,0:T(8,128)(2,1)S(1)}, bf16[16,768]{1,0:T(8,128)(2,1)S(1)}) custom-call(bf16[2,8,2048]{2,1,0:T(8,128)(2,1)S(1)} %shard_map.82.after.refs_0_, bf16[2,8,2048]{2,1,0:T(8,128)(2,1)S(1)} %collective-permute-done.refs_1_, ...), custom_call_target="tpu_custom_call" | custom-call | flops 201326592 | bytes 3604480 | tf_op jit(solution)/shard_map/pallas_call | solution.py:299
  15.9 0.9 %collective-permute-start.5 = (bf16[16,768]{1,0:T(8,128)(2,1)S(1)}, bf16[16,768]{1,0:T(8,128)(2,1)S(1)}, u32[]{:S(2)}, u32[]{:S(2)}) collective-permute-start(bf16[16,768]{1,0:T(8,128)(2,1)S(1)} %get-tuple-element.10), channel_id=1, source_target_pairs={{0,2},{1,3},{2,0},{3,1},{4,6},{5,7},{6,4},{7,5},{8,10},{9,11},{10,... | collective-permute-start | bytes 73736 | tf_op jit(solution)/shard_map/ppermute | solution.py:36
  16.9 0.9 %collective-permute-start.6 = (bf16[16,768]{1,0:T(8,128)(2,1)S(1)}, bf16[16,768]{1,0:T(8,128)(2,1)S(1)}, u32[]{:S(2)}, u32[]{:S(2)}) collective-permute-start(bf16[16,768]{1,0:T(8,128)(2,1)S(1)} %get-tuple-element.11), channel_id=1, source_target_pairs={{0,3},{1,2},{2,1},{3,0},{4,7},{5,6},{6,5},{7,4},{8,11},{9,10},{10,... | collective-permute-start | bytes 73736 | tf_op jit(solution)/shard_map/ppermute | solution.py:36
  17.7 0.4 %collective-permute-start.7 = (bf16[16,768]{1,0:T(8,128)(2,1)S(1)}, bf16[16,768]{1,0:T(8,128)(2,1)S(1)}, u32[]{:S(2)}, u32[]{:S(2)}) collective-permute-start(bf16[16,768]{1,0:T(8,128)(2,1)S(1)} %get-tuple-element.12), channel_id=1, source_target_pairs={{0,1},{1,0},{2,3},{3,2},{4,5},{5,4},{6,7},{7,6},{8,9},{9,8},{10,11... | collective-permute-start | bytes 73736 | tf_op jit(solution)/shard_map/ppermute | solution.py:36
  18.1 1.7 %collective-permute-done.5 = bf16[16,768]{1,0:T(8,128)(2,1)S(1)} collective-permute-done((bf16[16,768]{1,0:T(8,128)(2,1)S(1)}, bf16[16,768]{1,0:T(8,128)(2,1)S(1)}, u32[]{:S(2)}, u32[]{:S(2)}) %collective-permute-start.5) | collective-permute-done | bytes 24608 | tf_op jit(solution)/shard_map/ppermute | solution.py:36
  19.8 0.3 %collective-permute-done.6 = bf16[16,768]{1,0:T(8,128)(2,1)S(1)} collective-permute-done((bf16[16,768]{1,0:T(8,128)(2,1)S(1)}, bf16[16,768]{1,0:T(8,128)(2,1)S(1)}, u32[]{:S(2)}, u32[]{:S(2)}) %collective-permute-start.6) | collective-permute-done | bytes 24608 | tf_op jit(solution)/shard_map/ppermute | solution.py:36
  20.1 0.0 collective-permute-done.7
  20.1 0.0 copy-done
  20.1 0.0 copy-done.1
  20.1 0.7 %add_select_fusion = f32[16,768]{1,0:T(8,128)} fusion(bf16[16,768]{1,0:T(8,128)(2,1)S(1)} %collective-permute-done.7, bf16[16,768]{1,0:T(8,128)(2,1)S(1)} %collective-permute-done.6, f32[16,768]{1,0:T(8,128)S(1)} %get-tuple-element.9, bf16[16,768]{1,0:T(8,128)(2,1)S(1)} %collective-permute-done.5, s32[768]{0:T(1024)S(1)} %copy-done, s32[16]{0:T(128)S(1)} %copy-done.1), kind=kLoop, calls=%fused_computation | loop fusion | flops 98304 | bytes 175168 | tf_op jit(solution)/shard_map/jit(_where)/select_n | solution.py:324
  (1 shorter events, 0.0 us)
Async XLA Ops:
  1.8 8.4 %collective-permute-start.3 = (bf16[2,8,2048]{2,1,0:T(8,128)(2,1)S(1)}, bf16[2,8,2048]{2,1,0:T(8,128)(2,1)S(1)}, u32[]{:S(2)}, u32[]{:S(2)}) collective-permute-start(bf16[2,8,2048]{2,1,0:T(8,128)(2,1)S(1)} %shard_map.82.after.refs_0_), channel_id=1, source_target_pairs={{0,12},{1,15},{2,14},{3,13},{4,8},{5,11},{6,10},{7,9},{8,4},{9,7},... | collective-permute-start | bytes 196616 | tf_op jit(solution)/shard_map/ppermute | solution.py:36
  6.9 6.4 %collective-permute-start.2 = (bf16[2,8,2048]{2,1,0:T(8,128)(2,1)S(1)}, bf16[2,8,2048]{2,1,0:T(8,128)(2,1)S(1)}, u32[]{:S(2)}, u32[]{:S(2)}) collective-permute-start(bf16[2,8,2048]{2,1,0:T(8,128)(2,1)S(1)} %shard_map.82.after.refs_0_), channel_id=1, source_target_pairs={{0,8},{1,11},{2,10},{3,9},{4,12},{5,15},{6,14},{7,13},{8,0},{9,3},... | collective-permute-start | bytes 196616 | tf_op jit(solution)/shard_map/ppermute | solution.py:36
  6.9 6.4 %collective-permute-start.1 = (bf16[2,8,2048]{2,1,0:T(8,128)(2,1)S(1)}, bf16[2,8,2048]{2,1,0:T(8,128)(2,1)S(1)}, u32[]{:S(2)}, u32[]{:S(2)}) collective-permute-start(bf16[2,8,2048]{2,1,0:T(8,128)(2,1)S(1)} %shard_map.82.after.refs_0_), channel_id=1, source_target_pairs={{0,4},{1,7},{2,6},{3,5},{4,0},{5,3},{6,2},{7,1},{8,12},{9,15},{10,... | collective-permute-start | bytes 196616 | tf_op jit(solution)/shard_map/ppermute | solution.py:36
  7.5 5.7 %collective-permute-start = (bf16[2,8,2048]{2,1,0:T(8,128)(2,1)S(1)}, bf16[2,8,2048]{2,1,0:T(8,128)(2,1)S(1)}, u32[]{:S(2)}, u32[]{:S(2)}) collective-permute-start(bf16[2,8,2048]{2,1,0:T(8,128)(2,1)S(1)} %shard_map.82.after.refs_0_), channel_id=1, source_target_pairs={{1,3},{3,1},{5,7},{7,5},{9,11},{11,9},{13,15},{15,13},{17,19},{19,... | collective-permute-start | bytes 196616 | tf_op jit(solution)/shard_map/ppermute | solution.py:36
  10.1 10.0 %copy-start = (s32[768]{0:T(1024)S(1)}, s32[768]{0:T(1024)}, u32[]{:S(2)}) copy-start(s32[768]{0:T(1024)} %param.12) | copy-start | bytes 9220
  10.1 10.0 %copy-start.1 = (s32[16]{0:T(128)S(1)}, s32[16]{0:T(128)}, u32[]{:S(2)}) copy-start(s32[16]{0:T(128)} %param.10) | copy-start | bytes 196
  13.3 1.5 %collective-permute-start.4 = (bf16[4,8,2048]{2,1,0:T(8,128)(2,1)S(1)}, bf16[4,8,2048]{2,1,0:T(8,128)(2,1)S(1)}, u32[]{:S(2)}, u32[]{:S(2)}) collective-permute-start(bf16[4,8,2048]{2,1,0:T(8,128)(2,1)S(1)} %shard_map.84), channel_id=1, source_target_pairs={{0,1},{1,0},{2,3},{3,2},{4,5},{5,4},{6,7},{7,6},{8,9},{9,8},{10,11... | collective-permute-start | bytes 393224 | tf_op jit(solution)/shard_map/ppermute | solution.py:36
  15.9 3.9 %collective-permute-start.5 = (bf16[16,768]{1,0:T(8,128)(2,1)S(1)}, bf16[16,768]{1,0:T(8,128)(2,1)S(1)}, u32[]{:S(2)}, u32[]{:S(2)}) collective-permute-start(bf16[16,768]{1,0:T(8,128)(2,1)S(1)} %get-tuple-element.10), channel_id=1, source_target_pairs={{0,2},{1,3},{2,0},{3,1},{4,6},{5,7},{6,4},{7,5},{8,10},{9,11},{10,... | collective-permute-start | bytes 73736 | tf_op jit(solution)/shard_map/ppermute | solution.py:36
  16.9 3.3 %collective-permute-start.6 = (bf16[16,768]{1,0:T(8,128)(2,1)S(1)}, bf16[16,768]{1,0:T(8,128)(2,1)S(1)}, u32[]{:S(2)}, u32[]{:S(2)}) collective-permute-start(bf16[16,768]{1,0:T(8,128)(2,1)S(1)} %get-tuple-element.11), channel_id=1, source_target_pairs={{0,3},{1,2},{2,1},{3,0},{4,7},{5,6},{6,5},{7,4},{8,11},{9,10},{10,... | collective-permute-start | bytes 73736 | tf_op jit(solution)/shard_map/ppermute | solution.py:36
  17.7 2.4 %collective-permute-start.7 = (bf16[16,768]{1,0:T(8,128)(2,1)S(1)}, bf16[16,768]{1,0:T(8,128)(2,1)S(1)}, u32[]{:S(2)}, u32[]{:S(2)}) collective-permute-start(bf16[16,768]{1,0:T(8,128)(2,1)S(1)} %get-tuple-element.12), channel_id=1, source_target_pairs={{0,1},{1,0},{2,3},{3,2},{4,5},{5,4},{6,7},{7,6},{8,9},{9,8},{10,11... | collective-permute-start | bytes 73736 | tf_op jit(solution)/shard_map/ppermute | solution.py:36

commit v8 on v6

--- a/solution.py
+++ b/solution.py
@@ -76,13 +76,18 @@
     for copy_in in copies_in[:-1]:
         copy_in.wait()
 
-    place = (examples, examples * tokens)
-    example = lax.broadcasted_iota(jnp.int32, place, 0)
+    sets = 2
+    members = examples // sets
+    place = (examples, members * tokens)
+    member = lax.broadcasted_iota(jnp.int32, place, 0) % members
     column = lax.broadcasted_iota(jnp.int32, place, 1)
-    kept = jnp.zeros(place, jnp.bool_)
-    for e in range(examples):
-        kept |= (example == e) & (column >= e * tokens) & (column < e * tokens + counts[e])
-    lane = lax.broadcasted_iota(jnp.int32, (examples * tokens, LANES), 1)
+    kept = []
+    for first in range(0, examples, members):
+        live = jnp.zeros(place, jnp.bool_)
+        for e in range(members):
+            live |= (member == e) & (column >= e * tokens) & (column < e * tokens + counts[first + e])
+        kept.append(live[None])
+    lane = lax.broadcasted_iota(jnp.int32, (members * tokens, LANES), 1)
 
     weights = []
     for turn in range(len(rows)):
@@ -96,7 +101,7 @@
         left = jnp.concatenate(split(left), axis=1).astype(jnp.float32)
         left = jnp.concatenate(
             [
-                jnp.broadcast_to(left[pack * q + p : pack * q + p + 1], (examples, 2 * width))
+                jnp.broadcast_to(left[pack * q + p : pack * q + p + 1], (members, 2 * width))
                 for p in range(pack)
                 for q in range(groups)
             ],
@@ -106,31 +111,38 @@
 
     copies_in[-1].wait()
     for target, (module, left, right) in zip(rows, weights):
-        tokens_in = factors[:, pl.ds(module, 1)].reshape(examples * tokens, width)
-        twice = jnp.concatenate([tokens_in, tokens_in], axis=1)
-        inner = jnp.dot(twice, right, preferred_element_type=jnp.float32)
-        outer = lax.dot_general(
-            left, twice, (((1,), (1,)), ((), ())), preferred_element_type=jnp.float32
-        )
-        outer = outer.reshape(pack * groups, examples, examples * tokens)
-        outer = jnp.where(kept[None], outer, 0.0).reshape(pack * groups * examples, -1)
-
-        total = jnp.zeros((groups * examples, LANES), jnp.float32)
-        for p in range(pack):
-            outer_high, outer_low = split(outer[p * groups * examples : (p + 1) * groups * examples])
-            mine = (lane >= p * features) & (lane < (p + 1) * features)
-            inner_high, inner_low = split(jnp.where(mine, inner, 0.0))
-            both = jnp.dot(
-                outer_high,
-                jnp.concatenate([inner_high, inner_low], axis=1),
-                preferred_element_type=jnp.float32,
-            )
-            total += both[:, :LANES] + both[:, LANES:]
-            total += jnp.dot(outer_low, inner_high, preferred_element_type=jnp.float32)
-        total = total.astype(jnp.bfloat16)
+        totals = []
+        for number, live in enumerate(kept):
+            tokens_in = factors[pl.ds(number * members, members), pl.ds(module, 1)]
+            tokens_in = tokens_in.reshape(members * tokens, width)
+            twice = jnp.concatenate([tokens_in, tokens_in], axis=1)
+            inner = jnp.dot(twice, right, preferred_element_type=jnp.float32)
+            outer = lax.dot_general(
+                left, twice, (((1,), (1,)), ((), ())), preferred_element_type=jnp.float32
+            )
+            outer = jnp.where(live, outer.reshape(-1, examples, members * tokens), 0.0)
+            outer = outer.reshape(pack, groups * members, -1)
+
+            total = jnp.zeros((groups * members, LANES), jnp.float32)
+            for p in range(pack):
+                outer_high, outer_low = split(outer[p])
+                mine = (lane >= p * features) & (lane < (p + 1) * features)
+                inner_high, inner_low = split(jnp.where(mine, inner, 0.0))
+                both = jnp.dot(
+                    outer_high,
+                    jnp.concatenate([inner_high, inner_low], axis=1),
+                    preferred_element_type=jnp.float32,
+                )
+                total += both[:, :LANES] + both[:, LANES:]
+                total += jnp.dot(outer_low, inner_high, preferred_element_type=jnp.float32)
+            totals.append(total)
         for q in range(groups):
-            block = total[q * examples : (q + 1) * examples]
-            target[q // share, :, q % share * LANES : (q % share + 1) * LANES] = block
+            block = jnp.concatenate(
+                [total[q * members : (q + 1) * members] for total in totals], axis=0
+            )
+            target[q // share, :, q % share * LANES : (q % share + 1) * LANES] = block.astype(
+                jnp.bfloat16
+            )
 
 
 def copy_kernel(source, after, target, arrived):

time: 21 us -> 21 us (level)
  no operation moved by 1% of the time
where the time goes in v8:
time: 21 us; the launch traced here: 20.8 us
  starting transfers between devices  9.2 us (44%)
  waiting for transfers between devices  6.11 us (29%)
  Pallas kernels  4.76 us (23%)
  other arithmetic  0.69 us (3%)
    ppermute x8, starting transfers between devices, exchange(): return lax.ppermute(value, names, pairs)  9.2 us
    ppermute x8, waiting for transfers between devices, exchange(): return lax.ppermute(value, names, pairs)  6.11 us
    pallas_call x1, Pallas kernels, body(): pl.pallas_call(copy_kernel, out_shape=pltpu.VMEM((replay_total, depth), j...  1.9 us
    pallas_call x1, Pallas kernels, body(): pl.pallas_call(precondition_kernel, out_shape=[pltpu.VMEM((half_count, ex...  1.76 us
    pallas_call x1, Pallas kernels, body(): pl.pallas_call(functools.partial(score_kernel, sources, counts), out_shap...  1.08 us
    select_n x1, other arithmetic, body(): return jnp.where(self_pairs, jnp.zeros((), jnp.float32), summed_scores)  0.69 us
  transfers between devices with their start and end apart: 8, of which 4 were waited for; matrix products, arithmetic and copies ran while one was open for 0% of the time, Pallas kernels for 9%

profile of v8, /device:TPU:0, one launch (start us, length us, event | category | flops | bytes accessed | tf_op | source)
XLA Modules:
  0.0 20.8 jit_solution(5495783512421332194)
XLA Ops:
  0.0 1.8 %shard_map.82.after.refs_0_ = bf16[2,8,2048]{2,1,0:T(8,128)(2,1)S(1)} custom-call(s32[8]{0:T(128)} %counts_in.1, s32[2]{0:T(128)} %slots_in.1, bf16[8,2,64,128]{3,2,1,0:T(8,128)(2,1)} %factors_in.1, f32[2,64,64]{2,1,0:T(8,128)} %output_inverse_in.1, f32[2,64,64]{2,1,0:T(8,128)} %input_inverse_in.1), custom_call_target="tpu_custom_call" | custom-call | tf_op jit(solution)/shard_map/pallas_call | solution.py:243
  1.8 5.1 %collective-permute-start.3 = (bf16[2,8,2048]{2,1,0:T(8,128)(2,1)S(1)}, bf16[2,8,2048]{2,1,0:T(8,128)(2,1)S(1)}, u32[]{:S(2)}, u32[]{:S(2)}) collective-permute-start(bf16[2,8,2048]{2,1,0:T(8,128)(2,1)S(1)} %shard_map.82.after.refs_0_), channel_id=1, source_target_pairs={{0,12},{1,15},{2,14},{3,13},{4,8},{5,11},{6,10},{7,9},{8,4},{9,7},... | collective-permute-start | bytes 196616 | tf_op jit(solution)/shard_map/ppermute | solution.py:35
  6.9 0.0 collective-permute-start.2
  6.9 0.6 %collective-permute-start.1 = (bf16[2,8,2048]{2,1,0:T(8,128)(2,1)S(1)}, bf16[2,8,2048]{2,1,0:T(8,128)(2,1)S(1)}, u32[]{:S(2)}, u32[]{:S(2)}) collective-permute-start(bf16[2,8,2048]{2,1,0:T(8,128)(2,1)S(1)} %shard_map.82.after.refs_0_), channel_id=1, source_target_pairs={{0,4},{1,7},{2,6},{3,5},{4,0},{5,3},{6,2},{7,1},{8,12},{9,15},{10,... | collective-permute-start | bytes 196616 | tf_op jit(solution)/shard_map/ppermute | solution.py:35
  7.5 0.7 %collective-permute-start = (bf16[2,8,2048]{2,1,0:T(8,128)(2,1)S(1)}, bf16[2,8,2048]{2,1,0:T(8,128)(2,1)S(1)}, u32[]{:S(2)}, u32[]{:S(2)}) collective-permute-start(bf16[2,8,2048]{2,1,0:T(8,128)(2,1)S(1)} %shard_map.82.after.refs_0_), channel_id=1, source_target_pairs={{1,3},{3,1},{5,7},{7,5},{9,11},{11,9},{13,15},{15,13},{17,19},{19,... | collective-permute-start | bytes 196616 | tf_op jit(solution)/shard_map/ppermute | solution.py:35
  8.2 1.9 %shard_map.83.refs_5_.refs_6_ = bf16[768,2048]{1,0:T(8,128)(2,1)S(1)} custom-call(bf16[768,2048]{1,0:T(8,128)(2,1)} %bitcast.1, bf16[2,8,2048]{2,1,0:T(8,128)(2,1)S(1)} %shard_map.82.after.refs_0_), custom_call_target="tpu_custom_call" | custom-call | bytes 6291456 | tf_op jit(solution)/shard_map/pallas_call | solution.py:267
  10.1 0.0 copy-start
  10.1 0.0 copy-start.1
  10.1 0.0 collective-permute-done.3.refs_4_
  10.1 3.1 %collective-permute-done.2.refs_3_ = bf16[2,8,2048]{2,1,0:T(8,128)(2,1)S(1)} collective-permute-done((bf16[2,8,2048]{2,1,0:T(8,128)(2,1)S(1)}, bf16[2,8,2048]{2,1,0:T(8,128)(2,1)S(1)}, u32[]{:S(2)}, u32[]{:S(2)}) %collective-permute-start.2) | collective-permute-done | bytes 65568 | tf_op jit(solution)/shard_map/ppermute | solution.py:35
  13.3 0.0 collective-permute-done.1.refs_2_
  13.3 0.0 collective-permute-done.refs_1_
  13.3 0.6 %collective-permute-start.4 = (bf16[4,8,2048]{2,1,0:T(8,128)(2,1)S(1)}, bf16[4,8,2048]{2,1,0:T(8,128)(2,1)S(1)}, u32[]{:S(2)}, u32[]{:S(2)}) collective-permute-start(bf16[4,8,2048]{2,1,0:T(8,128)(2,1)S(1)} %shard_map.84), channel_id=1, source_target_pairs={{0,1},{1,0},{2,3},{3,2},{4,5},{5,4},{6,7},{7,6},{8,9},{9,8},{10,11... | collective-permute-start | bytes 393224 | tf_op jit(solution)/shard_map/ppermute | solution.py:35
  13.9 1.0 %collective-permute-done.4.refs_5_ = bf16[4,8,2048]{2,1,0:T(8,128)(2,1)S(1)} collective-permute-done((bf16[4,8,2048]{2,1,0:T(8,128)(2,1)S(1)}, bf16[4,8,2048]{2,1,0:T(8,128)(2,1)S(1)}, u32[]{:S(2)}, u32[]{:S(2)}) %collective-permute-start.4) | collective-permute-done | bytes 131104 | tf_op jit(solution)/shard_map/ppermute | solution.py:35
  14.8 1.1 %shard_map.85 = (f32[16,768]{1,0:T(8,128)S(1)}, bf16[16,768]{1,0:T(8,128)(2,1)S(1)}, bf16[16,768]{1,0:T(8,128)(2,1)S(1)}, bf16[16,768]{1,0:T(8,128)(2,1)S(1)}) custom-call(bf16[2,8,2048]{2,1,0:T(8,128)(2,1)S(1)} %shard_map.82.after.refs_0_, bf16[2,8,2048]{2,1,0:T(8,128)(2,1)S(1)} %collective-permute-done.refs_1_, ...), custom_call_target="tpu_custom_call" | custom-call | flops 201326592 | bytes 3604480 | tf_op jit(solution)/shard_map/pallas_call | solution.py:303
  15.9 0.9 %collective-permute-start.5 = (bf16[16,768]{1,0:T(8,128)(2,1)S(1)}, bf16[16,768]{1,0:T(8,128)(2,1)S(1)}, u32[]{:S(2)}, u32[]{:S(2)}) collective-permute-start(bf16[16,768]{1,0:T(8,128)(2,1)S(1)} %get-tuple-element.10), channel_id=1, source_target_pairs={{0,2},{1,3},{2,0},{3,1},{4,6},{5,7},{6,4},{7,5},{8,10},{9,11},{10,... | collective-permute-start | bytes 73736 | tf_op jit(solution)/shard_map/ppermute | solution.py:35
  16.9 0.9 %collective-permute-start.6 = (bf16[16,768]{1,0:T(8,128)(2,1)S(1)}, bf16[16,768]{1,0:T(8,128)(2,1)S(1)}, u32[]{:S(2)}, u32[]{:S(2)}) collective-permute-start(bf16[16,768]{1,0:T(8,128)(2,1)S(1)} %get-tuple-element.11), channel_id=1, source_target_pairs={{0,3},{1,2},{2,1},{3,0},{4,7},{5,6},{6,5},{7,4},{8,11},{9,10},{10,... | collective-permute-start | bytes 73736 | tf_op jit(solution)/shard_map/ppermute | solution.py:35
  17.7 0.4 %collective-permute-start.7 = (bf16[16,768]{1,0:T(8,128)(2,1)S(1)}, bf16[16,768]{1,0:T(8,128)(2,1)S(1)}, u32[]{:S(2)}, u32[]{:S(2)}) collective-permute-start(bf16[16,768]{1,0:T(8,128)(2,1)S(1)} %get-tuple-element.12), channel_id=1, source_target_pairs={{0,1},{1,0},{2,3},{3,2},{4,5},{5,4},{6,7},{7,6},{8,9},{9,8},{10,11... | collective-permute-start | bytes 73736 | tf_op jit(solution)/shard_map/ppermute | solution.py:35
  18.2 1.7 %collective-permute-done.5 = bf16[16,768]{1,0:T(8,128)(2,1)S(1)} collective-permute-done((bf16[16,768]{1,0:T(8,128)(2,1)S(1)}, bf16[16,768]{1,0:T(8,128)(2,1)S(1)}, u32[]{:S(2)}, u32[]{:S(2)}) %collective-permute-start.5) | collective-permute-done | bytes 24608 | tf_op jit(solution)/shard_map/ppermute | solution.py:35
  19.8 0.3 %collective-permute-done.6 = bf16[16,768]{1,0:T(8,128)(2,1)S(1)} collective-permute-done((bf16[16,768]{1,0:T(8,128)(2,1)S(1)}, bf16[16,768]{1,0:T(8,128)(2,1)S(1)}, u32[]{:S(2)}, u32[]{:S(2)}) %collective-permute-start.6) | collective-permute-done | bytes 24608 | tf_op jit(solution)/shard_map/ppermute | solution.py:35
  20.1 0.0 collective-permute-done.7
  20.1 0.0 copy-done
  20.1 0.0 copy-done.1
  20.1 0.7 %add_select_fusion = f32[16,768]{1,0:T(8,128)} fusion(bf16[16,768]{1,0:T(8,128)(2,1)S(1)} %collective-permute-done.7, bf16[16,768]{1,0:T(8,128)(2,1)S(1)} %collective-permute-done.6, f32[16,768]{1,0:T(8,128)S(1)} %get-tuple-element.9, bf16[16,768]{1,0:T(8,128)(2,1)S(1)} %collective-permute-done.5, s32[768]{0:T(1024)S(1)} %copy-done, s32[16]{0:T(128)S(1)} %copy-done.1), kind=kLoop, calls=%fused_computation | loop fusion | flops 98304 | bytes 175168 | tf_op jit(solution)/shard_map/jit(_where)/select_n | solution.py:328
  (1 shorter events, 0.0 us)
Async XLA Ops:
  1.8 8.4 %collective-permute-start.3 = (bf16[2,8,2048]{2,1,0:T(8,128)(2,1)S(1)}, bf16[2,8,2048]{2,1,0:T(8,128)(2,1)S(1)}, u32[]{:S(2)}, u32[]{:S(2)}) collective-permute-start(bf16[2,8,2048]{2,1,0:T(8,128)(2,1)S(1)} %shard_map.82.after.refs_0_), channel_id=1, source_target_pairs={{0,12},{1,15},{2,14},{3,13},{4,8},{5,11},{6,10},{7,9},{8,4},{9,7},... | collective-permute-start | bytes 196616 | tf_op jit(solution)/shard_map/ppermute | solution.py:35
  6.9 6.4 %collective-permute-start.2 = (bf16[2,8,2048]{2,1,0:T(8,128)(2,1)S(1)}, bf16[2,8,2048]{2,1,0:T(8,128)(2,1)S(1)}, u32[]{:S(2)}, u32[]{:S(2)}) collective-permute-start(bf16[2,8,2048]{2,1,0:T(8,128)(2,1)S(1)} %shard_map.82.after.refs_0_), channel_id=1, source_target_pairs={{0,8},{1,11},{2,10},{3,9},{4,12},{5,15},{6,14},{7,13},{8,0},{9,3},... | collective-permute-start | bytes 196616 | tf_op jit(solution)/shard_map/ppermute | solution.py:35
  6.9 6.4 %collective-permute-start.1 = (bf16[2,8,2048]{2,1,0:T(8,128)(2,1)S(1)}, bf16[2,8,2048]{2,1,0:T(8,128)(2,1)S(1)}, u32[]{:S(2)}, u32[]{:S(2)}) collective-permute-start(bf16[2,8,2048]{2,1,0:T(8,128)(2,1)S(1)} %shard_map.82.after.refs_0_), channel_id=1, source_target_pairs={{0,4},{1,7},{2,6},{3,5},{4,0},{5,3},{6,2},{7,1},{8,12},{9,15},{10,... | collective-permute-start | bytes 196616 | tf_op jit(solution)/shard_map/ppermute | solution.py:35
  7.5 5.7 %collective-permute-start = (bf16[2,8,2048]{2,1,0:T(8,128)(2,1)S(1)}, bf16[2,8,2048]{2,1,0:T(8,128)(2,1)S(1)}, u32[]{:S(2)}, u32[]{:S(2)}) collective-permute-start(bf16[2,8,2048]{2,1,0:T(8,128)(2,1)S(1)} %shard_map.82.after.refs_0_), channel_id=1, source_target_pairs={{1,3},{3,1},{5,7},{7,5},{9,11},{11,9},{13,15},{15,13},{17,19},{19,... | collective-permute-start | bytes 196616 | tf_op jit(solution)/shard_map/ppermute | solution.py:35
  10.1 10.0 %copy-start = (s32[768]{0:T(1024)S(1)}, s32[768]{0:T(1024)}, u32[]{:S(2)}) copy-start(s32[768]{0:T(1024)} %param.12) | copy-start | bytes 9220
  10.1 10.0 %copy-start.1 = (s32[16]{0:T(128)S(1)}, s32[16]{0:T(128)}, u32[]{:S(2)}) copy-start(s32[16]{0:T(128)} %param.10) | copy-start | bytes 196
  13.3 1.5 %collective-permute-start.4 = (bf16[4,8,2048]{2,1,0:T(8,128)(2,1)S(1)}, bf16[4,8,2048]{2,1,0:T(8,128)(2,1)S(1)}, u32[]{:S(2)}, u32[]{:S(2)}) collective-permute-start(bf16[4,8,2048]{2,1,0:T(8,128)(2,1)S(1)} %shard_map.84), channel_id=1, source_target_pairs={{0,1},{1,0},{2,3},{3,2},{4,5},{5,4},{6,7},{7,6},{8,9},{9,8},{10,11... | collective-permute-start | bytes 393224 | tf_op jit(solution)/shard_map/ppermute | solution.py:35
  15.9 3.9 %collective-permute-start.5 = (bf16[16,768]{1,0:T(8,128)(2,1)S(1)}, bf16[16,768]{1,0:T(8,128)(2,1)S(1)}, u32[]{:S(2)}, u32[]{:S(2)}) collective-permute-start(bf16[16,768]{1,0:T(8,128)(2,1)S(1)} %get-tuple-element.10), channel_id=1, source_target_pairs={{0,2},{1,3},{2,0},{3,1},{4,6},{5,7},{6,4},{7,5},{8,10},{9,11},{10,... | collective-permute-start | bytes 73736 | tf_op jit(solution)/shard_map/ppermute | solution.py:35
  16.9 3.3 %collective-permute-start.6 = (bf16[16,768]{1,0:T(8,128)(2,1)S(1)}, bf16[16,768]{1,0:T(8,128)(2,1)S(1)}, u32[]{:S(2)}, u32[]{:S(2)}) collective-permute-start(bf16[16,768]{1,0:T(8,128)(2,1)S(1)} %get-tuple-element.11), channel_id=1, source_target_pairs={{0,3},{1,2},{2,1},{3,0},{4,7},{5,6},{6,5},{7,4},{8,11},{9,10},{10,... | collective-permute-start | bytes 73736 | tf_op jit(solution)/shard_map/ppermute | solution.py:35
  17.7 2.4 %collective-permute-start.7 = (bf16[16,768]{1,0:T(8,128)(2,1)S(1)}, bf16[16,768]{1,0:T(8,128)(2,1)S(1)}, u32[]{:S(2)}, u32[]{:S(2)}) collective-permute-start(bf16[16,768]{1,0:T(8,128)(2,1)S(1)} %get-tuple-element.12), channel_id=1, source_target_pairs={{0,1},{1,0},{2,3},{3,2},{4,5},{5,4},{6,7},{7,6},{8,9},{9,8},{10,11... | collective-permute-start | bytes 73736 | tf_op jit(solution)/shard_map/ppermute | solution.py:35

commit v9 on v6

--- a/solution.py
+++ b/solution.py
@@ -27,12 +27,17 @@
     pairs = []
     for place in itertools.product(*[range(count) for count in counts]):
         source = target = 0
-        for spot, count, step in zip(place, counts, steps(place[-1])):
+        for spot, count, step in zip(place, counts, steps(*place)):
             source = source * count + spot
             target = target * count + partner(spot, step, count)
         if target != source:
             pairs.append((source, target))
     return lax.ppermute(value, names, pairs)
+
+
+def turn_order(count, odd):
+    order = list(range(count - 1, 0, -1))
+    return order + [0] if odd else order[-1:] + order[:-1] + [0]
 
 
 def split(value):
@@ -150,7 +155,9 @@
 
 
 def score_kernel(sources, holders, *refs):
-    replay_count, module_count, half_count = holders
+    _, replay_count, module_count, half_count = holders
+    even, odd = (turn_order(replay_count, kind) for kind in range(2))
+    odd_group = lax.axis_index("groups") % 2
     own_count = len(sources) // half_count
     kept, own, passed = refs[0], refs[1 : 1 + own_count], refs[1 + own_count : own_count + half_count]
     replay_rows, *chunks, joined, partials = refs[own_count + half_count :]
@@ -173,7 +180,8 @@
         ).astype(jnp.bfloat16)
 
     def place_of(number):
-        replay_step, turn, half_step = sources[number]
+        number, turn, half_step = sources[number]
+        replay_step = jnp.where(odd_group == 1, odd[number], even[number])
         handler = origin(half_place, half_step, half_count)
         module_step = turn * half_count + handler
         return origin(replay_place, replay_step, replay_count) * module_count + origin(
@@ -244,14 +252,24 @@
         compiler_params=pltpu.CompilerParams(vmem_limit_bytes=16 * 2**20),
     )(*[pltpu.with_memory_space_constraint(operand, pltpu.HBM) for operand in operands])
 
-    axes = ("replay", "module", "half")
-    counts = (replay_count, module_count, half_count)
+    axes = ("groups", "replay", "module", "half")
+    counts = (lax.axis_size("groups"), replay_count, module_count, half_count)
+    orders = [turn_order(replay_count, odd) for odd in range(2)]
     gathered = {}
-    for replay_step in range(replay_count):
+    for number in range(replay_count - 1, -1, -1):
         for turn in range(turns):
-            gathered[replay_step, turn, 0] = exchange(
-                outgoing[turn], axes, counts, lambda half: (replay_step, turn * half_count + half, 0)
+            gathered[number, turn, 0] = exchange(
+                outgoing[turn],
+                axes,
+                counts,
+                lambda group, replay, module, half: (
+                    0,
+                    orders[group % 2][number],
+                    turn * half_count + half,
+                    0,
+                ),
             )
+
     replay_rows = pl.pallas_call(
         copy_kernel,
         out_shape=pltpu.VMEM((replay_total, depth), jnp.bfloat16),
@@ -276,13 +294,13 @@
         compiler_params=pltpu.CompilerParams(vmem_limit_bytes=24 * 2**20),
     )(outgoing[0], *own, replay_rows)
     passed = [
-        exchange(pack, ("half",), (half_count,), lambda half: (half_step,))
+        exchange(pack, axes[3:], counts[3:], lambda half: (half_step,))
         for half_step, pack in enumerate(packs, 1)
     ]
     sources = [
-        (replay_step, turn, half_step)
+        (number, turn, half_step)
         for half_step in range(half_count)
-        for replay_step, turn, _ in gathered
+        for number, turn, _ in gathered
     ]
 
     rows = blocks * examples
@@ -309,7 +327,10 @@
     summed_scores = chunks[0]
     for step in sorted(range(1, holders), key=lambda step: (step < half_count, step)):
         term = exchange(
-            chunks[step], axes[1:], counts[1:], lambda half: (step // half_count, step % half_count)
+            chunks[step],
+            axes[2:],
+            counts[2:],
+            lambda module, half: (step // half_count, step % half_count),
         )
         summed_scores = summed_scores + term.astype(jnp.float32)
     self_pairs = new_ids[:, None] == replay_ids[None, :]

time: 21 us -> 22.3 us (1.062)
  waiting for transfers between devices: 6.1 us -> 7.87 us
  starting transfers between devices: 9.19 us -> 8.7 us
    ppermute x8, waiting for transfers between devices: 6.1 us -> 7.87 us  [exchange(): return lax.ppermute(value, names, pairs)]
    ppermute x8, starting transfers between devices: 9.19 us -> 8.7 us  [exchange(): return lax.ppermute(value, names, pairs)]
  transfers between devices with their start and end apart: 8 -> 8, of which waited for: 4 -> 5; matrix products, arithmetic and copies ran while one was open for 0% -> 0% of each run, Pallas kernels for 9% -> 9%
where the time goes in v9:
time: 22.3 us; the launch traced here: 22.1 us
  starting transfers between devices  8.7 us (39%)
  waiting for transfers between devices  7.87 us (35%)
  Pallas kernels  4.77 us (21%)
  other arithmetic  0.69 us (3%)
    ppermute x8, starting transfers between devices, exchange(): return lax.ppermute(value, names, pairs)  8.7 us
    ppermute x8, waiting for transfers between devices, exchange(): return lax.ppermute(value, names, pairs)  7.87 us
    pallas_call x1, Pallas kernels, body(): pl.pallas_call(copy_kernel, out_shape=pltpu.VMEM((replay_total, depth), j...  1.9 us
    pallas_call x1, Pallas kernels, body(): pl.pallas_call(precondition_kernel, out_shape=[pltpu.VMEM((half_count, ex...  1.77 us
    pallas_call x1, Pallas kernels, body(): pl.pallas_call(functools.partial(score_kernel, sources, counts), out_shap...  1.09 us
    select_n x1, other arithmetic, body(): return jnp.where(self_pairs, jnp.zeros((), jnp.float32), summed_scores)  0.69 us
  transfers between devices with their start and end apart: 8, of which 5 were waited for; matrix products, arithmetic and copies ran while one was open for 0% of the time, Pallas kernels for 9%

profile of v9, /device:TPU:0, one launch (start us, length us, event | category | flops | bytes accessed | tf_op | source)
XLA Modules:
  0.0 22.1 jit_solution(17602504624540303215)
XLA Ops:
  0.0 1.8 %shard_map.82.after.refs_0_ = bf16[2,8,2048]{2,1,0:T(8,128)(2,1)S(1)} custom-call(s32[8]{0:T(128)} %counts_in.1, s32[2]{0:T(128)} %slots_in.1, bf16[8,2,64,128]{3,2,1,0:T(8,128)(2,1)} %factors_in.1, f32[2,64,64]{2,1,0:T(8,128)} %output_inverse_in.1, f32[2,64,64]{2,1,0:T(8,128)} %input_inverse_in.1), custom_call_target="tpu_custom_call" | custom-call | tf_op jit(solution)/shard_map/pallas_call | solution.py:239
  1.8 3.1 %collective-permute-start.3 = (bf16[2,8,2048]{2,1,0:T(8,128)(2,1)S(1)}, bf16[2,8,2048]{2,1,0:T(8,128)(2,1)S(1)}, u32[]{:S(2)}, u32[]{:S(2)}) collective-permute-start(bf16[2,8,2048]{2,1,0:T(8,128)(2,1)S(1)} %shard_map.82.after.refs_0_), channel_id=1, source_target_pairs={{0,4},{1,7},{2,6},{3,5},{4,0},{5,3},{6,2},{7,1},{8,12},{9,15},{10,... | collective-permute-start | bytes 196616 | tf_op jit(solution)/shard_map/ppermute | solution.py:35
  4.9 2.5 %collective-permute-start.2 = (bf16[2,8,2048]{2,1,0:T(8,128)(2,1)S(1)}, bf16[2,8,2048]{2,1,0:T(8,128)(2,1)S(1)}, u32[]{:S(2)}, u32[]{:S(2)}) collective-permute-start(bf16[2,8,2048]{2,1,0:T(8,128)(2,1)S(1)} %shard_map.82.after.refs_0_), channel_id=1, source_target_pairs={{0,12},{1,15},{2,14},{3,13},{4,8},{5,11},{6,10},{7,9},{8,4},{9,7},... | collective-permute-start | bytes 196616 | tf_op jit(solution)/shard_map/ppermute | solution.py:35
  7.3 0.1 collective-permute-start.1
  7.5 0.7 %collective-permute-start = (bf16[2,8,2048]{2,1,0:T(8,128)(2,1)S(1)}, bf16[2,8,2048]{2,1,0:T(8,128)(2,1)S(1)}, u32[]{:S(2)}, u32[]{:S(2)}) collective-permute-start(bf16[2,8,2048]{2,1,0:T(8,128)(2,1)S(1)} %shard_map.82.after.refs_0_), channel_id=1, source_target_pairs={{1,3},{3,1},{5,7},{7,5},{9,11},{11,9},{13,15},{15,13},{17,19},{19,... | collective-permute-start | bytes 196616 | tf_op jit(solution)/shard_map/ppermute | solution.py:35
  8.1 1.9 %shard_map.83.refs_5_.refs_6_ = bf16[768,2048]{1,0:T(8,128)(2,1)S(1)} custom-call(bf16[768,2048]{1,0:T(8,128)(2,1)} %bitcast.1, bf16[2,8,2048]{2,1,0:T(8,128)(2,1)S(1)} %shard_map.82.after.refs_0_), custom_call_target="tpu_custom_call" | custom-call | bytes 6291456 | tf_op jit(solution)/shard_map/pallas_call | solution.py:273
  10.0 0.0 copy-start
  10.0 0.0 copy-start.1
  10.0 0.0 collective-permute-done.3.refs_4_
  10.1 1.5 %collective-permute-done.2.refs_3_ = bf16[2,8,2048]{2,1,0:T(8,128)(2,1)S(1)} collective-permute-done((bf16[2,8,2048]{2,1,0:T(8,128)(2,1)S(1)}, bf16[2,8,2048]{2,1,0:T(8,128)(2,1)S(1)}, u32[]{:S(2)}, u32[]{:S(2)}) %collective-permute-start.2) | collective-permute-done | bytes 65568 | tf_op jit(solution)/shard_map/ppermute | solution.py:35
  11.6 2.9 %collective-permute-done.1.refs_2_ = bf16[2,8,2048]{2,1,0:T(8,128)(2,1)S(1)} collective-permute-done((bf16[2,8,2048]{2,1,0:T(8,128)(2,1)S(1)}, bf16[2,8,2048]{2,1,0:T(8,128)(2,1)S(1)}, u32[]{:S(2)}, u32[]{:S(2)}) %collective-permute-start.1) | collective-permute-done | bytes 65568 | tf_op jit(solution)/shard_map/ppermute | solution.py:35
  14.5 0.0 collective-permute-done.refs_1_
  14.5 0.2 collective-permute-start.4
  14.7 1.2 %collective-permute-done.4.refs_5_ = bf16[4,8,2048]{2,1,0:T(8,128)(2,1)S(1)} collective-permute-done((bf16[4,8,2048]{2,1,0:T(8,128)(2,1)S(1)}, bf16[4,8,2048]{2,1,0:T(8,128)(2,1)S(1)}, u32[]{:S(2)}, u32[]{:S(2)}) %collective-permute-start.4) | collective-permute-done | bytes 131104 | tf_op jit(solution)/shard_map/ppermute | solution.py:35
  15.9 1.1 %shard_map.85 = (f32[16,768]{1,0:T(8,128)S(1)}, bf16[16,768]{1,0:T(8,128)(2,1)S(1)}, bf16[16,768]{1,0:T(8,128)(2,1)S(1)}, bf16[16,768]{1,0:T(8,128)(2,1)S(1)}) custom-call(bf16[2,8,2048]{2,1,0:T(8,128)(2,1)S(1)} %shard_map.82.after.refs_0_, bf16[2,8,2048]{2,1,0:T(8,128)(2,1)S(1)} %collective-permute-done.refs_1_, ...), custom_call_target="tpu_custom_call" | custom-call | flops 201326592 | bytes 3604480 | tf_op jit(solution)/shard_map/pallas_call | solution.py:309
  17.0 1.1 %collective-permute-start.5 = (bf16[16,768]{1,0:T(8,128)(2,1)S(1)}, bf16[16,768]{1,0:T(8,128)(2,1)S(1)}, u32[]{:S(2)}, u32[]{:S(2)}) collective-permute-start(bf16[16,768]{1,0:T(8,128)(2,1)S(1)} %get-tuple-element.10), channel_id=1, source_target_pairs={{0,2},{1,3},{2,0},{3,1},{4,6},{5,7},{6,4},{7,5},{8,10},{9,11},{10,... | collective-permute-start | bytes 73736 | tf_op jit(solution)/shard_map/ppermute | solution.py:35
  18.1 0.5 %collective-permute-start.6 = (bf16[16,768]{1,0:T(8,128)(2,1)S(1)}, bf16[16,768]{1,0:T(8,128)(2,1)S(1)}, u32[]{:S(2)}, u32[]{:S(2)}) collective-permute-start(bf16[16,768]{1,0:T(8,128)(2,1)S(1)} %get-tuple-element.11), channel_id=1, source_target_pairs={{0,3},{1,2},{2,1},{3,0},{4,7},{5,6},{6,5},{7,4},{8,11},{9,10},{10,... | collective-permute-start | bytes 73736 | tf_op jit(solution)/shard_map/ppermute | solution.py:35
  18.6 0.6 %collective-permute-start.7 = (bf16[16,768]{1,0:T(8,128)(2,1)S(1)}, bf16[16,768]{1,0:T(8,128)(2,1)S(1)}, u32[]{:S(2)}, u32[]{:S(2)}) collective-permute-start(bf16[16,768]{1,0:T(8,128)(2,1)S(1)} %get-tuple-element.12), channel_id=1, source_target_pairs={{0,1},{1,0},{2,3},{3,2},{4,5},{5,4},{6,7},{7,6},{8,9},{9,8},{10,11... | collective-permute-start | bytes 73736 | tf_op jit(solution)/shard_map/ppermute | solution.py:35
  19.2 1.7 %collective-permute-done.5 = bf16[16,768]{1,0:T(8,128)(2,1)S(1)} collective-permute-done((bf16[16,768]{1,0:T(8,128)(2,1)S(1)}, bf16[16,768]{1,0:T(8,128)(2,1)S(1)}, u32[]{:S(2)}, u32[]{:S(2)}) %collective-permute-start.5) | collective-permute-done | bytes 24608 | tf_op jit(solution)/shard_map/ppermute | solution.py:35
  20.9 0.5 %collective-permute-done.6 = bf16[16,768]{1,0:T(8,128)(2,1)S(1)} collective-permute-done((bf16[16,768]{1,0:T(8,128)(2,1)S(1)}, bf16[16,768]{1,0:T(8,128)(2,1)S(1)}, u32[]{:S(2)}, u32[]{:S(2)}) %collective-permute-start.6) | collective-permute-done | bytes 24608 | tf_op jit(solution)/shard_map/ppermute | solution.py:35
  21.4 0.0 collective-permute-done.7
  21.4 0.0 copy-done
  21.4 0.0 copy-done.1
  21.4 0.7 %add_select_fusion = f32[16,768]{1,0:T(8,128)} fusion(bf16[16,768]{1,0:T(8,128)(2,1)S(1)} %collective-permute-done.7, bf16[16,768]{1,0:T(8,128)(2,1)S(1)} %collective-permute-done.6, f32[16,768]{1,0:T(8,128)S(1)} %get-tuple-element.9, bf16[16,768]{1,0:T(8,128)(2,1)S(1)} %collective-permute-done.5, s32[768]{0:T(1024)S(1)} %copy-done, s32[16]{0:T(128)S(1)} %copy-done.1), kind=kLoop, calls=%fused_computation | loop fusion | flops 98304 | bytes 175168 | tf_op jit(solution)/shard_map/jit(_where)/select_n | solution.py:337
  (1 shorter events, 0.0 us)
Async XLA Ops:
  1.8 8.3 %collective-permute-start.3 = (bf16[2,8,2048]{2,1,0:T(8,128)(2,1)S(1)}, bf16[2,8,2048]{2,1,0:T(8,128)(2,1)S(1)}, u32[]{:S(2)}, u32[]{:S(2)}) collective-permute-start(bf16[2,8,2048]{2,1,0:T(8,128)(2,1)S(1)} %shard_map.82.after.refs_0_), channel_id=1, source_target_pairs={{0,4},{1,7},{2,6},{3,5},{4,0},{5,3},{6,2},{7,1},{8,12},{9,15},{10,... | collective-permute-start | bytes 196616 | tf_op jit(solution)/shard_map/ppermute | solution.py:35
  4.9 6.7 %collective-permute-start.2 = (bf16[2,8,2048]{2,1,0:T(8,128)(2,1)S(1)}, bf16[2,8,2048]{2,1,0:T(8,128)(2,1)S(1)}, u32[]{:S(2)}, u32[]{:S(2)}) collective-permute-start(bf16[2,8,2048]{2,1,0:T(8,128)(2,1)S(1)} %shard_map.82.after.refs_0_), channel_id=1, source_target_pairs={{0,12},{1,15},{2,14},{3,13},{4,8},{5,11},{6,10},{7,9},{8,4},{9,7},... | collective-permute-start | bytes 196616 | tf_op jit(solution)/shard_map/ppermute | solution.py:35
  7.3 7.2 %collective-permute-start.1 = (bf16[2,8,2048]{2,1,0:T(8,128)(2,1)S(1)}, bf16[2,8,2048]{2,1,0:T(8,128)(2,1)S(1)}, u32[]{:S(2)}, u32[]{:S(2)}) collective-permute-start(bf16[2,8,2048]{2,1,0:T(8,128)(2,1)S(1)} %shard_map.82.after.refs_0_), channel_id=1, source_target_pairs={{0,8},{1,11},{2,10},{3,9},{4,12},{5,15},{6,14},{7,13},{8,0},{9,3},... | collective-permute-start | bytes 196616 | tf_op jit(solution)/shard_map/ppermute | solution.py:35
  7.5 7.0 %collective-permute-start = (bf16[2,8,2048]{2,1,0:T(8,128)(2,1)S(1)}, bf16[2,8,2048]{2,1,0:T(8,128)(2,1)S(1)}, u32[]{:S(2)}, u32[]{:S(2)}) collective-permute-start(bf16[2,8,2048]{2,1,0:T(8,128)(2,1)S(1)} %shard_map.82.after.refs_0_), channel_id=1, source_target_pairs={{1,3},{3,1},{5,7},{7,5},{9,11},{11,9},{13,15},{15,13},{17,19},{19,... | collective-permute-start | bytes 196616 | tf_op jit(solution)/shard_map/ppermute | solution.py:35
  10.0 11.4 %copy-start = (s32[768]{0:T(1024)S(1)}, s32[768]{0:T(1024)}, u32[]{:S(2)}) copy-start(s32[768]{0:T(1024)} %param.12) | copy-start | bytes 9220
  10.0 11.4 %copy-start.1 = (s32[16]{0:T(128)S(1)}, s32[16]{0:T(128)}, u32[]{:S(2)}) copy-start(s32[16]{0:T(128)} %param.10) | copy-start | bytes 196
  14.5 1.4 %collective-permute-start.4 = (bf16[4,8,2048]{2,1,0:T(8,128)(2,1)S(1)}, bf16[4,8,2048]{2,1,0:T(8,128)(2,1)S(1)}, u32[]{:S(2)}, u32[]{:S(2)}) collective-permute-start(bf16[4,8,2048]{2,1,0:T(8,128)(2,1)S(1)} %shard_map.84), channel_id=1, source_target_pairs={{0,1},{1,0},{2,3},{3,2},{4,5},{5,4},{6,7},{7,6},{8,9},{9,8},{10,11... | collective-permute-start | bytes 393224 | tf_op jit(solution)/shard_map/ppermute | solution.py:35
  17.0 3.9 %collective-permute-start.5 = (bf16[16,768]{1,0:T(8,128)(2,1)S(1)}, bf16[16,768]{1,0:T(8,128)(2,1)S(1)}, u32[]{:S(2)}, u32[]{:S(2)}) collective-permute-start(bf16[16,768]{1,0:T(8,128)(2,1)S(1)} %get-tuple-element.10), channel_id=1, source_target_pairs={{0,2},{1,3},{2,0},{3,1},{4,6},{5,7},{6,4},{7,5},{8,10},{9,11},{10,... | collective-permute-start | bytes 73736 | tf_op jit(solution)/shard_map/ppermute | solution.py:35
  18.1 3.3 %collective-permute-start.6 = (bf16[16,768]{1,0:T(8,128)(2,1)S(1)}, bf16[16,768]{1,0:T(8,128)(2,1)S(1)}, u32[]{:S(2)}, u32[]{:S(2)}) collective-permute-start(bf16[16,768]{1,0:T(8,128)(2,1)S(1)} %get-tuple-element.11), channel_id=1, source_target_pairs={{0,3},{1,2},{2,1},{3,0},{4,7},{5,6},{6,5},{7,4},{8,11},{9,10},{10,... | collective-permute-start | bytes 73736 | tf_op jit(solution)/shard_map/ppermute | solution.py:35
  18.6 2.8 %collective-permute-start.7 = (bf16[16,768]{1,0:T(8,128)(2,1)S(1)}, bf16[16,768]{1,0:T(8,128)(2,1)S(1)}, u32[]{:S(2)}, u32[]{:S(2)}) collective-permute-start(bf16[16,768]{1,0:T(8,128)(2,1)S(1)} %get-tuple-element.12), channel_id=1, source_target_pairs={{0,1},{1,0},{2,3},{3,2},{4,5},{5,4},{6,7},{7,6},{8,9},{9,8},{10,11... | collective-permute-start | bytes 73736 | tf_op jit(solution)/shard_map/ppermute | solution.py:35

commit v10 on v9

--- a/solution.py
+++ b/solution.py
@@ -37,7 +37,7 @@
 
 def turn_order(count, odd):
     order = list(range(count - 1, 0, -1))
-    return order + [0] if odd else order[-1:] + order[:-1] + [0]
+    return order[-1:] + order[:-1] + [0] if odd else order + [0]
 
 
 def split(value):

time: 22.3 us -> 21.1 us (0.946)
  waiting for transfers between devices: 7.87 us -> 6.1 us
  starting transfers between devices: 8.7 us -> 9.19 us
    ppermute x8, waiting for transfers between devices: 7.87 us -> 6.1 us  [exchange(): return lax.ppermute(value, names, pairs)]
    ppermute x8, starting transfers between devices: 8.7 us -> 9.19 us  [exchange(): return lax.ppermute(value, names, pairs)]
  transfers between devices with their start and end apart: 8 -> 8, of which waited for: 5 -> 4; matrix products, arithmetic and copies ran while one was open for 0% -> 0% of each run, Pallas kernels for 9% -> 9%
where the time goes in v10:
time: 21.1 us; the launch traced here: 20.8 us
  starting transfers between devices  9.19 us (44%)
  waiting for transfers between devices  6.1 us (29%)
  Pallas kernels  4.77 us (23%)
  other arithmetic  0.69 us (3%)
    ppermute x8, starting transfers between devices, exchange(): return lax.ppermute(value, names, pairs)  9.19 us
    ppermute x8, waiting for transfers between devices, exchange(): return lax.ppermute(value, names, pairs)  6.1 us
    pallas_call x1, Pallas kernels, body(): pl.pallas_call(copy_kernel, out_shape=pltpu.VMEM((replay_total, depth), j...  1.9 us
    pallas_call x1, Pallas kernels, body(): pl.pallas_call(precondition_kernel, out_shape=[pltpu.VMEM((half_count, ex...  1.77 us
    pallas_call x1, Pallas kernels, body(): pl.pallas_call(functools.partial(score_kernel, sources, counts), out_shap...  1.09 us
    select_n x1, other arithmetic, body(): return jnp.where(self_pairs, jnp.zeros((), jnp.float32), summed_scores)  0.69 us
  transfers between devices with their start and end apart: 8, of which 4 were waited for; matrix products, arithmetic and copies ran while one was open for 0% of the time, Pallas kernels for 9%

profile of v10, /device:TPU:0, one launch (start us, length us, event | category | flops | bytes accessed | tf_op | source)
XLA Modules:
  0.0 20.8 jit_solution(17522164239232107405)
XLA Ops:
  0.0 1.8 %shard_map.82.after.refs_0_ = bf16[2,8,2048]{2,1,0:T(8,128)(2,1)S(1)} custom-call(s32[8]{0:T(128)} %counts_in.1, s32[2]{0:T(128)} %slots_in.1, bf16[8,2,64,128]{3,2,1,0:T(8,128)(2,1)} %factors_in.1, f32[2,64,64]{2,1,0:T(8,128)} %output_inverse_in.1, f32[2,64,64]{2,1,0:T(8,128)} %input_inverse_in.1), custom_call_target="tpu_custom_call" | custom-call | tf_op jit(solution)/shard_map/pallas_call | solution.py:239
  1.8 5.1 %collective-permute-start.3 = (bf16[2,8,2048]{2,1,0:T(8,128)(2,1)S(1)}, bf16[2,8,2048]{2,1,0:T(8,128)(2,1)S(1)}, u32[]{:S(2)}, u32[]{:S(2)}) collective-permute-start(bf16[2,8,2048]{2,1,0:T(8,128)(2,1)S(1)} %shard_map.82.after.refs_0_), channel_id=1, source_target_pairs={{0,12},{1,15},{2,14},{3,13},{4,8},{5,11},{6,10},{7,9},{8,4},{9,7},... | collective-permute-start | bytes 196616 | tf_op jit(solution)/shard_map/ppermute | solution.py:35
  6.9 0.0 collective-permute-start.2
  6.9 0.6 %collective-permute-start.1 = (bf16[2,8,2048]{2,1,0:T(8,128)(2,1)S(1)}, bf16[2,8,2048]{2,1,0:T(8,128)(2,1)S(1)}, u32[]{:S(2)}, u32[]{:S(2)}) collective-permute-start(bf16[2,8,2048]{2,1,0:T(8,128)(2,1)S(1)} %shard_map.82.after.refs_0_), channel_id=1, source_target_pairs={{0,4},{1,7},{2,6},{3,5},{4,0},{5,3},{6,2},{7,1},{8,12},{9,15},{10,... | collective-permute-start | bytes 196616 | tf_op jit(solution)/shard_map/ppermute | solution.py:35
  7.5 0.7 %collective-permute-start = (bf16[2,8,2048]{2,1,0:T(8,128)(2,1)S(1)}, bf16[2,8,2048]{2,1,0:T(8,128)(2,1)S(1)}, u32[]{:S(2)}, u32[]{:S(2)}) collective-permute-start(bf16[2,8,2048]{2,1,0:T(8,128)(2,1)S(1)} %shard_map.82.after.refs_0_), channel_id=1, source_target_pairs={{1,3},{3,1},{5,7},{7,5},{9,11},{11,9},{13,15},{15,13},{17,19},{19,... | collective-permute-start | bytes 196616 | tf_op jit(solution)/shard_map/ppermute | solution.py:35
  8.2 1.9 %shard_map.83.refs_5_.refs_6_ = bf16[768,2048]{1,0:T(8,128)(2,1)S(1)} custom-call(bf16[768,2048]{1,0:T(8,128)(2,1)} %bitcast.1, bf16[2,8,2048]{2,1,0:T(8,128)(2,1)S(1)} %shard_map.82.after.refs_0_), custom_call_target="tpu_custom_call" | custom-call | bytes 6291456 | tf_op jit(solution)/shard_map/pallas_call | solution.py:273
  10.1 0.0 copy-start
  10.1 0.0 copy-start.1
  10.1 0.0 collective-permute-done.3.refs_4_
  10.1 3.1 %collective-permute-done.2.refs_3_ = bf16[2,8,2048]{2,1,0:T(8,128)(2,1)S(1)} collective-permute-done((bf16[2,8,2048]{2,1,0:T(8,128)(2,1)S(1)}, bf16[2,8,2048]{2,1,0:T(8,128)(2,1)S(1)}, u32[]{:S(2)}, u32[]{:S(2)}) %collective-permute-start.2) | collective-permute-done | bytes 65568 | tf_op jit(solution)/shard_map/ppermute | solution.py:35
  13.3 0.0 collective-permute-done.1.refs_2_
  13.3 0.0 collective-permute-done.refs_1_
  13.3 0.6 %collective-permute-start.4 = (bf16[4,8,2048]{2,1,0:T(8,128)(2,1)S(1)}, bf16[4,8,2048]{2,1,0:T(8,128)(2,1)S(1)}, u32[]{:S(2)}, u32[]{:S(2)}) collective-permute-start(bf16[4,8,2048]{2,1,0:T(8,128)(2,1)S(1)} %shard_map.84), channel_id=1, source_target_pairs={{0,1},{1,0},{2,3},{3,2},{4,5},{5,4},{6,7},{7,6},{8,9},{9,8},{10,11... | collective-permute-start | bytes 393224 | tf_op jit(solution)/shard_map/ppermute | solution.py:35
  13.9 1.0 %collective-permute-done.4.refs_5_ = bf16[4,8,2048]{2,1,0:T(8,128)(2,1)S(1)} collective-permute-done((bf16[4,8,2048]{2,1,0:T(8,128)(2,1)S(1)}, bf16[4,8,2048]{2,1,0:T(8,128)(2,1)S(1)}, u32[]{:S(2)}, u32[]{:S(2)}) %collective-permute-start.4) | collective-permute-done | bytes 131104 | tf_op jit(solution)/shard_map/ppermute | solution.py:35
  14.8 1.1 %shard_map.85 = (f32[16,768]{1,0:T(8,128)S(1)}, bf16[16,768]{1,0:T(8,128)(2,1)S(1)}, bf16[16,768]{1,0:T(8,128)(2,1)S(1)}, bf16[16,768]{1,0:T(8,128)(2,1)S(1)}) custom-call(bf16[2,8,2048]{2,1,0:T(8,128)(2,1)S(1)} %shard_map.82.after.refs_0_, bf16[2,8,2048]{2,1,0:T(8,128)(2,1)S(1)} %collective-permute-done.refs_1_, ...), custom_call_target="tpu_custom_call" | custom-call | flops 201326592 | bytes 3604480 | tf_op jit(solution)/shard_map/pallas_call | solution.py:309
  15.9 0.9 %collective-permute-start.5 = (bf16[16,768]{1,0:T(8,128)(2,1)S(1)}, bf16[16,768]{1,0:T(8,128)(2,1)S(1)}, u32[]{:S(2)}, u32[]{:S(2)}) collective-permute-start(bf16[16,768]{1,0:T(8,128)(2,1)S(1)} %get-tuple-element.10), channel_id=1, source_target_pairs={{0,2},{1,3},{2,0},{3,1},{4,6},{5,7},{6,4},{7,5},{8,10},{9,11},{10,... | collective-permute-start | bytes 73736 | tf_op jit(solution)/shard_map/ppermute | solution.py:35
  16.9 0.9 %collective-permute-start.6 = (bf16[16,768]{1,0:T(8,128)(2,1)S(1)}, bf16[16,768]{1,0:T(8,128)(2,1)S(1)}, u32[]{:S(2)}, u32[]{:S(2)}) collective-permute-start(bf16[16,768]{1,0:T(8,128)(2,1)S(1)} %get-tuple-element.11), channel_id=1, source_target_pairs={{0,3},{1,2},{2,1},{3,0},{4,7},{5,6},{6,5},{7,4},{8,11},{9,10},{10,... | collective-permute-start | bytes 73736 | tf_op jit(solution)/shard_map/ppermute | solution.py:35
  17.7 0.4 %collective-permute-start.7 = (bf16[16,768]{1,0:T(8,128)(2,1)S(1)}, bf16[16,768]{1,0:T(8,128)(2,1)S(1)}, u32[]{:S(2)}, u32[]{:S(2)}) collective-permute-start(bf16[16,768]{1,0:T(8,128)(2,1)S(1)} %get-tuple-element.12), channel_id=1, source_target_pairs={{0,1},{1,0},{2,3},{3,2},{4,5},{5,4},{6,7},{7,6},{8,9},{9,8},{10,11... | collective-permute-start | bytes 73736 | tf_op jit(solution)/shard_map/ppermute | solution.py:35
  18.2 1.7 %collective-permute-done.5 = bf16[16,768]{1,0:T(8,128)(2,1)S(1)} collective-permute-done((bf16[16,768]{1,0:T(8,128)(2,1)S(1)}, bf16[16,768]{1,0:T(8,128)(2,1)S(1)}, u32[]{:S(2)}, u32[]{:S(2)}) %collective-permute-start.5) | collective-permute-done | bytes 24608 | tf_op jit(solution)/shard_map/ppermute | solution.py:35
  19.8 0.3 %collective-permute-done.6 = bf16[16,768]{1,0:T(8,128)(2,1)S(1)} collective-permute-done((bf16[16,768]{1,0:T(8,128)(2,1)S(1)}, bf16[16,768]{1,0:T(8,128)(2,1)S(1)}, u32[]{:S(2)}, u32[]{:S(2)}) %collective-permute-start.6) | collective-permute-done | bytes 24608 | tf_op jit(solution)/shard_map/ppermute | solution.py:35
  20.1 0.0 collective-permute-done.7
  20.1 0.0 copy-done
  20.1 0.0 copy-done.1
  20.1 0.7 %add_select_fusion = f32[16,768]{1,0:T(8,128)} fusion(bf16[16,768]{1,0:T(8,128)(2,1)S(1)} %collective-permute-done.7, bf16[16,768]{1,0:T(8,128)(2,1)S(1)} %collective-permute-done.6, f32[16,768]{1,0:T(8,128)S(1)} %get-tuple-element.9, bf16[16,768]{1,0:T(8,128)(2,1)S(1)} %collective-permute-done.5, s32[768]{0:T(1024)S(1)} %copy-done, s32[16]{0:T(128)S(1)} %copy-done.1), kind=kLoop, calls=%fused_computation | loop fusion | flops 98304 | bytes 175168 | tf_op jit(solution)/shard_map/jit(_where)/select_n | solution.py:337
  (1 shorter events, 0.0 us)
Async XLA Ops:
  1.8 8.3 %collective-permute-start.3 = (bf16[2,8,2048]{2,1,0:T(8,128)(2,1)S(1)}, bf16[2,8,2048]{2,1,0:T(8,128)(2,1)S(1)}, u32[]{:S(2)}, u32[]{:S(2)}) collective-permute-start(bf16[2,8,2048]{2,1,0:T(8,128)(2,1)S(1)} %shard_map.82.after.refs_0_), channel_id=1, source_target_pairs={{0,12},{1,15},{2,14},{3,13},{4,8},{5,11},{6,10},{7,9},{8,4},{9,7},... | collective-permute-start | bytes 196616 | tf_op jit(solution)/shard_map/ppermute | solution.py:35
  6.9 6.4 %collective-permute-start.2 = (bf16[2,8,2048]{2,1,0:T(8,128)(2,1)S(1)}, bf16[2,8,2048]{2,1,0:T(8,128)(2,1)S(1)}, u32[]{:S(2)}, u32[]{:S(2)}) collective-permute-start(bf16[2,8,2048]{2,1,0:T(8,128)(2,1)S(1)} %shard_map.82.after.refs_0_), channel_id=1, source_target_pairs={{0,8},{1,11},{2,10},{3,9},{4,12},{5,15},{6,14},{7,13},{8,0},{9,3},... | collective-permute-start | bytes 196616 | tf_op jit(solution)/shard_map/ppermute | solution.py:35
  6.9 6.4 %collective-permute-start.1 = (bf16[2,8,2048]{2,1,0:T(8,128)(2,1)S(1)}, bf16[2,8,2048]{2,1,0:T(8,128)(2,1)S(1)}, u32[]{:S(2)}, u32[]{:S(2)}) collective-permute-start(bf16[2,8,2048]{2,1,0:T(8,128)(2,1)S(1)} %shard_map.82.after.refs_0_), channel_id=1, source_target_pairs={{0,4},{1,7},{2,6},{3,5},{4,0},{5,3},{6,2},{7,1},{8,12},{9,15},{10,... | collective-permute-start | bytes 196616 | tf_op jit(solution)/shard_map/ppermute | solution.py:35
  7.5 5.7 %collective-permute-start = (bf16[2,8,2048]{2,1,0:T(8,128)(2,1)S(1)}, bf16[2,8,2048]{2,1,0:T(8,128)(2,1)S(1)}, u32[]{:S(2)}, u32[]{:S(2)}) collective-permute-start(bf16[2,8,2048]{2,1,0:T(8,128)(2,1)S(1)} %shard_map.82.after.refs_0_), channel_id=1, source_target_pairs={{1,3},{3,1},{5,7},{7,5},{9,11},{11,9},{13,15},{15,13},{17,19},{19,... | collective-permute-start | bytes 196616 | tf_op jit(solution)/shard_map/ppermute | solution.py:35
  10.1 10.0 %copy-start = (s32[768]{0:T(1024)S(1)}, s32[768]{0:T(1024)}, u32[]{:S(2)}) copy-start(s32[768]{0:T(1024)} %param.12) | copy-start | bytes 9220
  10.1 10.0 %copy-start.1 = (s32[16]{0:T(128)S(1)}, s32[16]{0:T(128)}, u32[]{:S(2)}) copy-start(s32[16]{0:T(128)} %param.10) | copy-start | bytes 196
  13.3 1.5 %collective-permute-start.4 = (bf16[4,8,2048]{2,1,0:T(8,128)(2,1)S(1)}, bf16[4,8,2048]{2,1,0:T(8,128)(2,1)S(1)}, u32[]{:S(2)}, u32[]{:S(2)}) collective-permute-start(bf16[4,8,2048]{2,1,0:T(8,128)(2,1)S(1)} %shard_map.84), channel_id=1, source_target_pairs={{0,1},{1,0},{2,3},{3,2},{4,5},{5,4},{6,7},{7,6},{8,9},{9,8},{10,11... | collective-permute-start | bytes 393224 | tf_op jit(solution)/shard_map/ppermute | solution.py:35
  15.9 3.9 %collective-permute-start.5 = (bf16[16,768]{1,0:T(8,128)(2,1)S(1)}, bf16[16,768]{1,0:T(8,128)(2,1)S(1)}, u32[]{:S(2)}, u32[]{:S(2)}) collective-permute-start(bf16[16,768]{1,0:T(8,128)(2,1)S(1)} %get-tuple-element.10), channel_id=1, source_target_pairs={{0,2},{1,3},{2,0},{3,1},{4,6},{5,7},{6,4},{7,5},{8,10},{9,11},{10,... | collective-permute-start | bytes 73736 | tf_op jit(solution)/shard_map/ppermute | solution.py:35
  16.9 3.3 %collective-permute-start.6 = (bf16[16,768]{1,0:T(8,128)(2,1)S(1)}, bf16[16,768]{1,0:T(8,128)(2,1)S(1)}, u32[]{:S(2)}, u32[]{:S(2)}) collective-permute-start(bf16[16,768]{1,0:T(8,128)(2,1)S(1)} %get-tuple-element.11), channel_id=1, source_target_pairs={{0,3},{1,2},{2,1},{3,0},{4,7},{5,6},{6,5},{7,4},{8,11},{9,10},{10,... | collective-permute-start | bytes 73736 | tf_op jit(solution)/shard_map/ppermute | solution.py:35
  17.7 2.4 %collective-permute-start.7 = (bf16[16,768]{1,0:T(8,128)(2,1)S(1)}, bf16[16,768]{1,0:T(8,128)(2,1)S(1)}, u32[]{:S(2)}, u32[]{:S(2)}) collective-permute-start(bf16[16,768]{1,0:T(8,128)(2,1)S(1)} %get-tuple-element.12), channel_id=1, source_target_pairs={{0,1},{1,0},{2,3},{3,2},{4,5},{5,4},{6,7},{7,6},{8,9},{9,8},{10,11... | collective-permute-start | bytes 73736 | tf_op jit(solution)/shard_map/ppermute | solution.py:35

commit v11 on v8

--- a/solution.py
+++ b/solution.py
@@ -123,18 +123,18 @@
             outer = jnp.where(live, outer.reshape(-1, examples, members * tokens), 0.0)
             outer = outer.reshape(pack, groups * members, -1)
 
-            total = jnp.zeros((groups * members, LANES), jnp.float32)
+            outers, inners = [], []
             for p in range(pack):
                 outer_high, outer_low = split(outer[p])
                 mine = (lane >= p * features) & (lane < (p + 1) * features)
                 inner_high, inner_low = split(jnp.where(mine, inner, 0.0))
-                both = jnp.dot(
-                    outer_high,
-                    jnp.concatenate([inner_high, inner_low], axis=1),
-                    preferred_element_type=jnp.float32,
-                )
-                total += both[:, :LANES] + both[:, LANES:]
-                total += jnp.dot(outer_low, inner_high, preferred_element_type=jnp.float32)
+                outers += [outer_high, outer_low, outer_high]
+                inners += [inner_high, inner_high, inner_low]
+            total = jnp.dot(
+                jnp.concatenate(outers, axis=1),
+                jnp.concatenate(inners, axis=0),
+                preferred_element_type=jnp.float32,
+            )
             totals.append(total)
         for q in range(groups):
             block = jnp.concatenate(

time: 21 us -> 21.1 us (level)
  no operation moved by 1% of the time
where the time goes in v11:
time: 21.1 us; the launch traced here: 20.9 us
  starting transfers between devices  9.19 us (44%)
  waiting for transfers between devices  6.11 us (29%)
  Pallas kernels  4.85 us (23%)
  other arithmetic  0.69 us (3%)
    ppermute x8, starting transfers between devices, exchange(): return lax.ppermute(value, names, pairs)  9.19 us
    ppermute x8, waiting for transfers between devices, exchange(): return lax.ppermute(value, names, pairs)  6.11 us
    pallas_call x1, Pallas kernels, body(): pl.pallas_call(copy_kernel, out_shape=pltpu.VMEM((replay_total, depth), j...  1.9 us
    pallas_call x1, Pallas kernels, body(): pl.pallas_call(precondition_kernel, out_shape=[pltpu.VMEM((half_count, ex...  1.85 us
    pallas_call x1, Pallas kernels, body(): pl.pallas_call(functools.partial(score_kernel, sources, counts), out_shap...  1.09 us
    select_n x1, other arithmetic, body(): return jnp.where(self_pairs, jnp.zeros((), jnp.float32), summed_scores)  0.69 us
  transfers between devices with their start and end apart: 8, of which 4 were waited for; matrix products, arithmetic and copies ran while one was open for 0% of the time, Pallas kernels for 9%

profile of v11, /device:TPU:0, one launch (start us, length us, event | category | flops | bytes accessed | tf_op | source)
XLA Modules:
  0.0 20.9 jit_solution(6626770934177178190)
XLA Ops:
  0.0 1.9 %shard_map.82.after.refs_0_ = bf16[2,8,2048]{2,1,0:T(8,128)(2,1)S(1)} custom-call(s32[8]{0:T(128)} %counts_in.1, s32[2]{0:T(128)} %slots_in.1, bf16[8,2,64,128]{3,2,1,0:T(8,128)(2,1)} %factors_in.1, f32[2,64,64]{2,1,0:T(8,128)} %output_inverse_in.1, f32[2,64,64]{2,1,0:T(8,128)} %input_inverse_in.1), custom_call_target="tpu_custom_call" | custom-call | tf_op jit(solution)/shard_map/pallas_call | solution.py:243
  1.9 5.1 %collective-permute-start.3 = (bf16[2,8,2048]{2,1,0:T(8,128)(2,1)S(1)}, bf16[2,8,2048]{2,1,0:T(8,128)(2,1)S(1)}, u32[]{:S(2)}, u32[]{:S(2)}) collective-permute-start(bf16[2,8,2048]{2,1,0:T(8,128)(2,1)S(1)} %shard_map.82.after.refs_0_), channel_id=1, source_target_pairs={{0,12},{1,15},{2,14},{3,13},{4,8},{5,11},{6,10},{7,9},{8,4},{9,7},... | collective-permute-start | bytes 196616 | tf_op jit(solution)/shard_map/ppermute | solution.py:35
  7.0 0.0 collective-permute-start.2
  7.0 0.6 %collective-permute-start.1 = (bf16[2,8,2048]{2,1,0:T(8,128)(2,1)S(1)}, bf16[2,8,2048]{2,1,0:T(8,128)(2,1)S(1)}, u32[]{:S(2)}, u32[]{:S(2)}) collective-permute-start(bf16[2,8,2048]{2,1,0:T(8,128)(2,1)S(1)} %shard_map.82.after.refs_0_), channel_id=1, source_target_pairs={{0,4},{1,7},{2,6},{3,5},{4,0},{5,3},{6,2},{7,1},{8,12},{9,15},{10,... | collective-permute-start | bytes 196616 | tf_op jit(solution)/shard_map/ppermute | solution.py:35
  7.6 0.7 %collective-permute-start = (bf16[2,8,2048]{2,1,0:T(8,128)(2,1)S(1)}, bf16[2,8,2048]{2,1,0:T(8,128)(2,1)S(1)}, u32[]{:S(2)}, u32[]{:S(2)}) collective-permute-start(bf16[2,8,2048]{2,1,0:T(8,128)(2,1)S(1)} %shard_map.82.after.refs_0_), channel_id=1, source_target_pairs={{1,3},{3,1},{5,7},{7,5},{9,11},{11,9},{13,15},{15,13},{17,19},{19,... | collective-permute-start | bytes 196616 | tf_op jit(solution)/shard_map/ppermute | solution.py:35
  8.3 1.9 %shard_map.83.refs_5_.refs_6_ = bf16[768,2048]{1,0:T(8,128)(2,1)S(1)} custom-call(bf16[768,2048]{1,0:T(8,128)(2,1)} %bitcast.1, bf16[2,8,2048]{2,1,0:T(8,128)(2,1)S(1)} %shard_map.82.after.refs_0_), custom_call_target="tpu_custom_call" | custom-call | bytes 6291456 | tf_op jit(solution)/shard_map/pallas_call | solution.py:267
  10.2 0.0 copy-start
  10.2 0.0 copy-start.1
  10.2 0.0 collective-permute-done.3.refs_4_
  10.2 3.1 %collective-permute-done.2.refs_3_ = bf16[2,8,2048]{2,1,0:T(8,128)(2,1)S(1)} collective-permute-done((bf16[2,8,2048]{2,1,0:T(8,128)(2,1)S(1)}, bf16[2,8,2048]{2,1,0:T(8,128)(2,1)S(1)}, u32[]{:S(2)}, u32[]{:S(2)}) %collective-permute-start.2) | collective-permute-done | bytes 65568 | tf_op jit(solution)/shard_map/ppermute | solution.py:35
  13.4 0.0 collective-permute-done.1.refs_2_
  13.4 0.0 collective-permute-done.refs_1_
  13.4 0.6 %collective-permute-start.4 = (bf16[4,8,2048]{2,1,0:T(8,128)(2,1)S(1)}, bf16[4,8,2048]{2,1,0:T(8,128)(2,1)S(1)}, u32[]{:S(2)}, u32[]{:S(2)}) collective-permute-start(bf16[4,8,2048]{2,1,0:T(8,128)(2,1)S(1)} %shard_map.84), channel_id=1, source_target_pairs={{0,1},{1,0},{2,3},{3,2},{4,5},{5,4},{6,7},{7,6},{8,9},{9,8},{10,11... | collective-permute-start | bytes 393224 | tf_op jit(solution)/shard_map/ppermute | solution.py:35
  13.9 1.0 %collective-permute-done.4.refs_5_ = bf16[4,8,2048]{2,1,0:T(8,128)(2,1)S(1)} collective-permute-done((bf16[4,8,2048]{2,1,0:T(8,128)(2,1)S(1)}, bf16[4,8,2048]{2,1,0:T(8,128)(2,1)S(1)}, u32[]{:S(2)}, u32[]{:S(2)}) %collective-permute-start.4) | collective-permute-done | bytes 131104 | tf_op jit(solution)/shard_map/ppermute | solution.py:35
  14.9 1.1 %shard_map.85 = (f32[16,768]{1,0:T(8,128)S(1)}, bf16[16,768]{1,0:T(8,128)(2,1)S(1)}, bf16[16,768]{1,0:T(8,128)(2,1)S(1)}, bf16[16,768]{1,0:T(8,128)(2,1)S(1)}) custom-call(bf16[2,8,2048]{2,1,0:T(8,128)(2,1)S(1)} %shard_map.82.after.refs_0_, bf16[2,8,2048]{2,1,0:T(8,128)(2,1)S(1)} %collective-permute-done.refs_1_, ...), custom_call_target="tpu_custom_call" | custom-call | flops 201326592 | bytes 3604480 | tf_op jit(solution)/shard_map/pallas_call | solution.py:303
  16.0 0.9 %collective-permute-start.5 = (bf16[16,768]{1,0:T(8,128)(2,1)S(1)}, bf16[16,768]{1,0:T(8,128)(2,1)S(1)}, u32[]{:S(2)}, u32[]{:S(2)}) collective-permute-start(bf16[16,768]{1,0:T(8,128)(2,1)S(1)} %get-tuple-element.10), channel_id=1, source_target_pairs={{0,2},{1,3},{2,0},{3,1},{4,6},{5,7},{6,4},{7,5},{8,10},{9,11},{10,... | collective-permute-start | bytes 73736 | tf_op jit(solution)/shard_map/ppermute | solution.py:35
  17.0 0.9 %collective-permute-start.6 = (bf16[16,768]{1,0:T(8,128)(2,1)S(1)}, bf16[16,768]{1,0:T(8,128)(2,1)S(1)}, u32[]{:S(2)}, u32[]{:S(2)}) collective-permute-start(bf16[16,768]{1,0:T(8,128)(2,1)S(1)} %get-tuple-element.11), channel_id=1, source_target_pairs={{0,3},{1,2},{2,1},{3,0},{4,7},{5,6},{6,5},{7,4},{8,11},{9,10},{10,... | collective-permute-start | bytes 73736 | tf_op jit(solution)/shard_map/ppermute | solution.py:35
  17.8 0.4 %collective-permute-start.7 = (bf16[16,768]{1,0:T(8,128)(2,1)S(1)}, bf16[16,768]{1,0:T(8,128)(2,1)S(1)}, u32[]{:S(2)}, u32[]{:S(2)}) collective-permute-start(bf16[16,768]{1,0:T(8,128)(2,1)S(1)} %get-tuple-element.12), channel_id=1, source_target_pairs={{0,1},{1,0},{2,3},{3,2},{4,5},{5,4},{6,7},{7,6},{8,9},{9,8},{10,11... | collective-permute-start | bytes 73736 | tf_op jit(solution)/shard_map/ppermute | solution.py:35
  18.2 1.7 %collective-permute-done.5 = bf16[16,768]{1,0:T(8,128)(2,1)S(1)} collective-permute-done((bf16[16,768]{1,0:T(8,128)(2,1)S(1)}, bf16[16,768]{1,0:T(8,128)(2,1)S(1)}, u32[]{:S(2)}, u32[]{:S(2)}) %collective-permute-start.5) | collective-permute-done | bytes 24608 | tf_op jit(solution)/shard_map/ppermute | solution.py:35
  19.9 0.3 %collective-permute-done.6 = bf16[16,768]{1,0:T(8,128)(2,1)S(1)} collective-permute-done((bf16[16,768]{1,0:T(8,128)(2,1)S(1)}, bf16[16,768]{1,0:T(8,128)(2,1)S(1)}, u32[]{:S(2)}, u32[]{:S(2)}) %collective-permute-start.6) | collective-permute-done | bytes 24608 | tf_op jit(solution)/shard_map/ppermute | solution.py:35
  20.2 0.0 collective-permute-done.7
  20.2 0.0 copy-done
  20.2 0.0 copy-done.1
  20.2 0.7 %add_select_fusion = f32[16,768]{1,0:T(8,128)} fusion(bf16[16,768]{1,0:T(8,128)(2,1)S(1)} %collective-permute-done.7, bf16[16,768]{1,0:T(8,128)(2,1)S(1)} %collective-permute-done.6, f32[16,768]{1,0:T(8,128)S(1)} %get-tuple-element.9, bf16[16,768]{1,0:T(8,128)(2,1)S(1)} %collective-permute-done.5, s32[768]{0:T(1024)S(1)} %copy-done, s32[16]{0:T(128)S(1)} %copy-done.1), kind=kLoop, calls=%fused_computation | loop fusion | flops 98304 | bytes 175168 | tf_op jit(solution)/shard_map/jit(_where)/select_n | solution.py:328
  (1 shorter events, 0.0 us)
Async XLA Ops:
  1.9 8.4 %collective-permute-start.3 = (bf16[2,8,2048]{2,1,0:T(8,128)(2,1)S(1)}, bf16[2,8,2048]{2,1,0:T(8,128)(2,1)S(1)}, u32[]{:S(2)}, u32[]{:S(2)}) collective-permute-start(bf16[2,8,2048]{2,1,0:T(8,128)(2,1)S(1)} %shard_map.82.after.refs_0_), channel_id=1, source_target_pairs={{0,12},{1,15},{2,14},{3,13},{4,8},{5,11},{6,10},{7,9},{8,4},{9,7},... | collective-permute-start | bytes 196616 | tf_op jit(solution)/shard_map/ppermute | solution.py:35
  7.0 6.4 %collective-permute-start.2 = (bf16[2,8,2048]{2,1,0:T(8,128)(2,1)S(1)}, bf16[2,8,2048]{2,1,0:T(8,128)(2,1)S(1)}, u32[]{:S(2)}, u32[]{:S(2)}) collective-permute-start(bf16[2,8,2048]{2,1,0:T(8,128)(2,1)S(1)} %shard_map.82.after.refs_0_), channel_id=1, source_target_pairs={{0,8},{1,11},{2,10},{3,9},{4,12},{5,15},{6,14},{7,13},{8,0},{9,3},... | collective-permute-start | bytes 196616 | tf_op jit(solution)/shard_map/ppermute | solution.py:35
  7.0 6.4 %collective-permute-start.1 = (bf16[2,8,2048]{2,1,0:T(8,128)(2,1)S(1)}, bf16[2,8,2048]{2,1,0:T(8,128)(2,1)S(1)}, u32[]{:S(2)}, u32[]{:S(2)}) collective-permute-start(bf16[2,8,2048]{2,1,0:T(8,128)(2,1)S(1)} %shard_map.82.after.refs_0_), channel_id=1, source_target_pairs={{0,4},{1,7},{2,6},{3,5},{4,0},{5,3},{6,2},{7,1},{8,12},{9,15},{10,... | collective-permute-start | bytes 196616 | tf_op jit(solution)/shard_map/ppermute | solution.py:35
  7.6 5.7 %collective-permute-start = (bf16[2,8,2048]{2,1,0:T(8,128)(2,1)S(1)}, bf16[2,8,2048]{2,1,0:T(8,128)(2,1)S(1)}, u32[]{:S(2)}, u32[]{:S(2)}) collective-permute-start(bf16[2,8,2048]{2,1,0:T(8,128)(2,1)S(1)} %shard_map.82.after.refs_0_), channel_id=1, source_target_pairs={{1,3},{3,1},{5,7},{7,5},{9,11},{11,9},{13,15},{15,13},{17,19},{19,... | collective-permute-start | bytes 196616 | tf_op jit(solution)/shard_map/ppermute | solution.py:35
  10.2 10.0 %copy-start = (s32[768]{0:T(1024)S(1)}, s32[768]{0:T(1024)}, u32[]{:S(2)}) copy-start(s32[768]{0:T(1024)} %param.12) | copy-start | bytes 9220
  10.2 10.0 %copy-start.1 = (s32[16]{0:T(128)S(1)}, s32[16]{0:T(128)}, u32[]{:S(2)}) copy-start(s32[16]{0:T(128)} %param.10) | copy-start | bytes 196
  13.4 1.5 %collective-permute-start.4 = (bf16[4,8,2048]{2,1,0:T(8,128)(2,1)S(1)}, bf16[4,8,2048]{2,1,0:T(8,128)(2,1)S(1)}, u32[]{:S(2)}, u32[]{:S(2)}) collective-permute-start(bf16[4,8,2048]{2,1,0:T(8,128)(2,1)S(1)} %shard_map.84), channel_id=1, source_target_pairs={{0,1},{1,0},{2,3},{3,2},{4,5},{5,4},{6,7},{7,6},{8,9},{9,8},{10,11... | collective-permute-start | bytes 393224 | tf_op jit(solution)/shard_map/ppermute | solution.py:35
  16.0 3.9 %collective-permute-start.5 = (bf16[16,768]{1,0:T(8,128)(2,1)S(1)}, bf16[16,768]{1,0:T(8,128)(2,1)S(1)}, u32[]{:S(2)}, u32[]{:S(2)}) collective-permute-start(bf16[16,768]{1,0:T(8,128)(2,1)S(1)} %get-tuple-element.10), channel_id=1, source_target_pairs={{0,2},{1,3},{2,0},{3,1},{4,6},{5,7},{6,4},{7,5},{8,10},{9,11},{10,... | collective-permute-start | bytes 73736 | tf_op jit(solution)/shard_map/ppermute | solution.py:35
  17.0 3.3 %collective-permute-start.6 = (bf16[16,768]{1,0:T(8,128)(2,1)S(1)}, bf16[16,768]{1,0:T(8,128)(2,1)S(1)}, u32[]{:S(2)}, u32[]{:S(2)}) collective-permute-start(bf16[16,768]{1,0:T(8,128)(2,1)S(1)} %get-tuple-element.11), channel_id=1, source_target_pairs={{0,3},{1,2},{2,1},{3,0},{4,7},{5,6},{6,5},{7,4},{8,11},{9,10},{10,... | collective-permute-start | bytes 73736 | tf_op jit(solution)/shard_map/ppermute | solution.py:35
  17.8 2.4 %collective-permute-start.7 = (bf16[16,768]{1,0:T(8,128)(2,1)S(1)}, bf16[16,768]{1,0:T(8,128)(2,1)S(1)}, u32[]{:S(2)}, u32[]{:S(2)}) collective-permute-start(bf16[16,768]{1,0:T(8,128)(2,1)S(1)} %get-tuple-element.12), channel_id=1, source_target_pairs={{0,1},{1,0},{2,3},{3,2},{4,5},{5,4},{6,7},{7,6},{8,9},{9,8},{10,11... | collective-permute-start | bytes 73736 | tf_op jit(solution)/shard_map/ppermute | solution.py:35

commit v12 on v6

--- a/solution.py
+++ b/solution.py
@@ -149,20 +149,9 @@
             pack[number] = block[needed]
 
 
-def score_kernel(sources, holders, *refs):
-    replay_count, module_count, half_count = holders
-    own_count = len(sources) // half_count
-    kept, own, passed = refs[0], refs[1 : 1 + own_count], refs[1 + own_count : own_count + half_count]
-    replay_rows, *chunks, joined, partials = refs[own_count + half_count :]
-    examples = own[0].shape[-2]
-    replay_place = lax.axis_index("replay")
-    module_place = lax.axis_index("module")
-    half_place = lax.axis_index("half")
-
+def multiply(blocks, replay_rows, joined, store):
+    examples = blocks[0].shape[0]
     per_group = joined.shape[1] // examples
-    blocks = [block[half_place] for block in own]
-    blocks[0] = jnp.where(half_place == 0, kept[half_place], blocks[0])
-    blocks += [pack[number] for pack in passed for number in range(own_count)]
     for group in range(joined.shape[0]):
         joined[group] = jnp.concatenate(
             [
@@ -171,6 +160,37 @@
             ],
             axis=0,
         ).astype(jnp.bfloat16)
+    for group in range(joined.shape[0]):
+        product = lax.dot_general(
+            joined[group],
+            replay_rows[...],
+            (((1,), (1,)), ((), ())),
+            preferred_element_type=jnp.float32,
+        )
+        for number in range(per_group):
+            store(group * per_group + number, product[number * examples : (number + 1) * examples])
+
+
+def own_kernel(kept, *refs):
+    own, (replay_rows, products, joined) = refs[:-3], refs[-3:]
+    half_place = lax.axis_index("half")
+    blocks = [block[half_place] for block in own]
+    blocks[0] = jnp.where(half_place == 0, kept[half_place], blocks[0])
+
+    def store(number, rows):
+        products[number] = rows
+
+    multiply(blocks, replay_rows, joined, store)
+
+
+def score_kernel(sources, holders, products, *refs):
+    replay_count, module_count, half_count = holders
+    own_count = products.shape[0]
+    passed = refs[: half_count - 1]
+    replay_rows, *chunks, joined, partials = refs[half_count - 1 :]
+    replay_place = lax.axis_index("replay")
+    module_place = lax.axis_index("module")
+    half_place = lax.axis_index("half")
 
     def place_of(number):
         replay_step, turn, half_step = sources[number]
@@ -180,17 +200,13 @@
             module_place, module_step, module_count
         )
 
-    for group in range(joined.shape[0]):
-        product = lax.dot_general(
-            joined[group],
-            replay_rows[...],
-            (((1,), (1,)), ((), ())),
-            preferred_element_type=jnp.float32,
-        )
-        for number in range(per_group):
-            partials[place_of(group * per_group + number)] = product[
-                number * examples : (number + 1) * examples
-            ]
+    def store(number, rows):
+        partials[place_of(own_count + number)] = rows
+
+    for number in range(own_count):
+        partials[place_of(number)] = products[number]
+    blocks = [pack[number] for pack in passed for number in range(own_count)]
+    multiply(blocks, replay_rows, joined, store)
 
     share = len(sources) // (module_count * half_count)
     for step, chunk in enumerate(chunks):
@@ -285,26 +301,42 @@
         for replay_step, turn, _ in gathered
     ]
 
+    def scratch(rows):
+        group_rows = min(rows, 64)
+        return pltpu.VMEM((rows // group_rows, group_rows, depth), jnp.bfloat16)
+
+    def cost(rows):
+        return pl.CostEstimate(
+            flops=2 * rows * replay_total * depth,
+            bytes_accessed=2 * (rows + replay_total) * depth + 4 * rows * replay_total,
+            transcendentals=0,
+        )
+
     rows = blocks * examples
-    group_rows = min(rows, 64)
+    own_rows = len(own) * examples
+    products = pl.pallas_call(
+        own_kernel,
+        out_shape=pltpu.VMEM((len(own), examples, replay_total), jnp.float32),
+        in_specs=[vmem] * (2 + len(own)),
+        out_specs=vmem,
+        scratch_shapes=[scratch(own_rows)],
+        compiler_params=pltpu.CompilerParams(vmem_limit_bytes=24 * 2**20),
+        cost_estimate=cost(own_rows),
+    )(outgoing[0], *own, replay_rows)
     shape = (rows // holders, replay_total)
     chunks = pl.pallas_call(
         functools.partial(score_kernel, sources, counts),
         out_shape=[pltpu.VMEM(shape, jnp.float32)]
         + [pltpu.VMEM(shape, jnp.bfloat16)] * (holders - 1),
-        in_specs=[vmem] * (1 + len(own) + half_count),
+        in_specs=[vmem] * (1 + half_count),
         out_specs=[vmem] * holders,
         scratch_shapes=[
-            pltpu.VMEM((rows // group_rows, group_rows, depth), jnp.bfloat16),
+            scratch(rows - own_rows),
             pltpu.VMEM((blocks, examples, replay_total), jnp.float32),
         ],
         compiler_params=pltpu.CompilerParams(vmem_limit_bytes=24 * 2**20),
-        cost_estimate=pl.CostEstimate(
-            flops=2 * rows * replay_total * depth,
-            bytes_accessed=2 * (rows + replay_total) * depth + 4 * rows * replay_total,
-            transcendentals=0,
-        ),
-    )(outgoing[0], *own, *passed, replay_rows)
+        cost_estimate=cost(rows - own_rows),
+    )(products, *passed, replay_rows)
 
     summed_scores = chunks[0]
     for step in sorted(range(1, holders), key=lambda step: (step < half_count, step)):

time: 21 us -> 21.1 us (level)
  Pallas kernels: 4.77 us -> 5.74 us
  waiting for transfers between devices: 6.1 us -> 5.19 us
    pallas_call x0 -> x1, Pallas kernels: none -> 1.01 us  [body(): pl.pallas_call(own_kernel, out_shape=pltpu.VMEM((len(own), examples, repl...]
    ppermute x8, waiting for transfers between devices: 6.1 us -> 5.19 us  [exchange(): return lax.ppermute(value, names, pairs)]
  transfers between devices with their start and end apart: 8 -> 8, of which waited for: 4 -> 3; matrix products, arithmetic and copies ran while one was open for 0% -> 0% of each run, Pallas kernels for 9% -> 14%
where the time goes in v12:
time: 21.1 us; the launch traced here: 20.9 us
  starting transfers between devices  9.17 us (43%)
  Pallas kernels  5.74 us (27%)
  waiting for transfers between devices  5.19 us (25%)
  other arithmetic  0.69 us (3%)
    ppermute x8, starting transfers between devices, exchange(): return lax.ppermute(value, names, pairs)  9.17 us
    ppermute x8, waiting for transfers between devices, exchange(): return lax.ppermute(value, names, pairs)  5.19 us
    pallas_call x1, Pallas kernels, body(): pl.pallas_call(copy_kernel, out_shape=pltpu.VMEM((replay_total, depth), j...  1.9 us
    pallas_call x1, Pallas kernels, body(): pl.pallas_call(precondition_kernel, out_shape=[pltpu.VMEM((half_count, ex...  1.77 us
    pallas_call x1, Pallas kernels, body(): pl.pallas_call(functools.partial(score_kernel, sources, counts), out_shap...  1.05 us
    pallas_call x1, Pallas kernels, body(): pl.pallas_call(own_kernel, out_shape=pltpu.VMEM((len(own), examples, repl...  1.01 us
    select_n x1, other arithmetic, body(): return jnp.where(self_pairs, jnp.zeros((), jnp.float32), summed_scores)  0.69 us
  transfers between devices with their start and end apart: 8, of which 3 were waited for; matrix products, arithmetic and copies ran while one was open for 0% of the time, Pallas kernels for 14%

profile of v12, /device:TPU:0, one launch (start us, length us, event | category | flops | bytes accessed | tf_op | source)
XLA Modules:
  0.0 20.9 jit_solution(449482348358298310)
XLA Ops:
  0.0 1.8 %shard_map.82.after.kept.refs_0_ = bf16[2,8,2048]{2,1,0:T(8,128)(2,1)S(1)} custom-call(s32[8]{0:T(128)} %counts_in.1, s32[2]{0:T(128)} %slots_in.1, bf16[8,2,64,128]{3,2,1,0:T(8,128)(2,1)} %factors_in.1, f32[2,64,64]{2,1,0:T(8,128)} %output_inverse_in.1, f32[2,64,64]{2,1,0:T(8,128)} %input_inverse_in.1), custom_call_target="tpu_custom_call" | custom-call | tf_op jit(solution)/shard_map/pallas_call | solution.py:247
  1.8 5.1 %collective-permute-start.3 = (bf16[2,8,2048]{2,1,0:T(8,128)(2,1)S(1)}, bf16[2,8,2048]{2,1,0:T(8,128)(2,1)S(1)}, u32[]{:S(2)}, u32[]{:S(2)}) collective-permute-start(bf16[2,8,2048]{2,1,0:T(8,128)(2,1)S(1)} %shard_map.82.after.kept.refs_0_), channel_id=1, source_target_pairs={{0,12},{1,15},{2,14},{3,13},{4,8},{5,11},{6,10},{7,9},{8,4},{9,7},... | collective-permute-start | bytes 196616 | tf_op jit(solution)/shard_map/ppermute | solution.py:35
  6.9 0.0 collective-permute-start.2
  6.9 0.6 %collective-permute-start.1 = (bf16[2,8,2048]{2,1,0:T(8,128)(2,1)S(1)}, bf16[2,8,2048]{2,1,0:T(8,128)(2,1)S(1)}, u32[]{:S(2)}, u32[]{:S(2)}) collective-permute-start(bf16[2,8,2048]{2,1,0:T(8,128)(2,1)S(1)} %shard_map.82.after.kept.refs_0_), channel_id=1, source_target_pairs={{0,4},{1,7},{2,6},{3,5},{4,0},{5,3},{6,2},{7,1},{8,12},{9,15},{10,... | collective-permute-start | bytes 196616 | tf_op jit(solution)/shard_map/ppermute | solution.py:35
  7.5 0.7 %collective-permute-start = (bf16[2,8,2048]{2,1,0:T(8,128)(2,1)S(1)}, bf16[2,8,2048]{2,1,0:T(8,128)(2,1)S(1)}, u32[]{:S(2)}, u32[]{:S(2)}) collective-permute-start(bf16[2,8,2048]{2,1,0:T(8,128)(2,1)S(1)} %shard_map.82.after.kept.refs_0_), channel_id=1, source_target_pairs={{1,3},{3,1},{5,7},{7,5},{9,11},{11,9},{13,15},{15,13},{17,19},{19,... | collective-permute-start | bytes 196616 | tf_op jit(solution)/shard_map/ppermute | solution.py:35
  8.2 1.9 %shard_map.83.refs_4_.refs_5_.refs_1_ = bf16[768,2048]{1,0:T(8,128)(2,1)S(1)} custom-call(bf16[768,2048]{1,0:T(8,128)(2,1)} %bitcast.1, bf16[2,8,2048]{2,1,0:T(8,128)(2,1)S(1)} %shard_map.82.after.kept.refs_0_), custom_call_target="tpu_custom_call" | custom-call | bytes 6291456 | tf_op jit(solution)/shard_map/pallas_call | solution.py:271
  10.1 0.0 collective-permute-done.3.refs_3_.refs_4_
  10.1 3.2 %collective-permute-done.2.refs_2_.refs_3_ = bf16[2,8,2048]{2,1,0:T(8,128)(2,1)S(1)} collective-permute-done((bf16[2,8,2048]{2,1,0:T(8,128)(2,1)S(1)}, bf16[2,8,2048]{2,1,0:T(8,128)(2,1)S(1)}, u32[]{:S(2)}, u32[]{:S(2)}) %collective-permute-start.2) | collective-permute-done | bytes 65568 | tf_op jit(solution)/shard_map/ppermute | solution.py:35
  13.3 0.0 collective-permute-done.1.refs_1_.refs_2_
  13.3 0.0 collective-permute-done.refs_0_.refs_1_
  13.3 0.0 copy-start
  13.3 0.0 copy-start.1
  13.3 0.6 %collective-permute-start.4 = (bf16[4,8,2048]{2,1,0:T(8,128)(2,1)S(1)}, bf16[4,8,2048]{2,1,0:T(8,128)(2,1)S(1)}, u32[]{:S(2)}, u32[]{:S(2)}) collective-permute-start(bf16[4,8,2048]{2,1,0:T(8,128)(2,1)S(1)} %shard_map.85), channel_id=1, source_target_pairs={{0,1},{1,0},{2,3},{3,2},{4,5},{5,4},{6,7},{7,6},{8,9},{9,8},{10,11... | collective-permute-start | bytes 393224 | tf_op jit(solution)/shard_map/ppermute | solution.py:35
  13.9 1.0 %shard_map.84.products = f32[4,8,768]{2,1,0:T(8,128)S(1)} custom-call(bf16[2,8,2048]{2,1,0:T(8,128)(2,1)S(1)} %shard_map.82.after.kept.refs_0_, bf16[2,8,2048]{2,1,0:T(8,128)(2,1)S(1)} %collective-permute-done.refs_0_.refs_1_, bf16[2,8,2048]{2,1,0:T(8,128)(2,1)S(1)} %collective-permute-done.1.refs_1_.refs_2_, ...), custom_call_target="tpu_custom_call" | custom-call | flops 100663296 | bytes 3375104 | tf_op jit(solution)/shard_map/pallas_call | solution.py:317
  14.9 0.0 collective-permute-done.4.refs_0_
  14.9 1.0 %shard_map.86 = (f32[16,768]{1,0:T(8,128)S(1)}, bf16[16,768]{1,0:T(8,128)(2,1)S(1)}, bf16[16,768]{1,0:T(8,128)(2,1)S(1)}, bf16[16,768]{1,0:T(8,128)(2,1)S(1)}) custom-call(f32[4,8,768]{2,1,0:T(8,128)S(1)} %shard_map.84.products, bf16[4,8,2048]{2,1,0:T(8,128)(2,1)S(1)} %collective-permute-done.4.refs_0_, bf16[768,2048]{1,0:T(8,128)(2,1)S(1)} %shard_map.83.refs_4_.refs_5_.refs_1_), custom_call_target="tpu_custom_call" | custom-call | flops 100663296 | bytes 3375104 | tf_op jit(solution)/shard_map/pallas_call | solution.py:327
  16.0 0.9 %collective-permute-start.5 = (bf16[16,768]{1,0:T(8,128)(2,1)S(1)}, bf16[16,768]{1,0:T(8,128)(2,1)S(1)}, u32[]{:S(2)}, u32[]{:S(2)}) collective-permute-start(bf16[16,768]{1,0:T(8,128)(2,1)S(1)} %get-tuple-element.10), channel_id=1, source_target_pairs={{0,2},{1,3},{2,0},{3,1},{4,6},{5,7},{6,4},{7,5},{8,10},{9,11},{10,... | collective-permute-start | bytes 73736 | tf_op jit(solution)/shard_map/ppermute | solution.py:35
  16.9 0.8 %collective-permute-start.6 = (bf16[16,768]{1,0:T(8,128)(2,1)S(1)}, bf16[16,768]{1,0:T(8,128)(2,1)S(1)}, u32[]{:S(2)}, u32[]{:S(2)}) collective-permute-start(bf16[16,768]{1,0:T(8,128)(2,1)S(1)} %get-tuple-element.11), channel_id=1, source_target_pairs={{0,3},{1,2},{2,1},{3,0},{4,7},{5,6},{6,5},{7,4},{8,11},{9,10},{10,... | collective-permute-start | bytes 73736 | tf_op jit(solution)/shard_map/ppermute | solution.py:35
  17.7 0.5 %collective-permute-start.7 = (bf16[16,768]{1,0:T(8,128)(2,1)S(1)}, bf16[16,768]{1,0:T(8,128)(2,1)S(1)}, u32[]{:S(2)}, u32[]{:S(2)}) collective-permute-start(bf16[16,768]{1,0:T(8,128)(2,1)S(1)} %get-tuple-element.12), channel_id=1, source_target_pairs={{0,1},{1,0},{2,3},{3,2},{4,5},{5,4},{6,7},{7,6},{8,9},{9,8},{10,11... | collective-permute-start | bytes 73736 | tf_op jit(solution)/shard_map/ppermute | solution.py:35
  18.2 1.7 %collective-permute-done.5 = bf16[16,768]{1,0:T(8,128)(2,1)S(1)} collective-permute-done((bf16[16,768]{1,0:T(8,128)(2,1)S(1)}, bf16[16,768]{1,0:T(8,128)(2,1)S(1)}, u32[]{:S(2)}, u32[]{:S(2)}) %collective-permute-start.5) | collective-permute-done | bytes 24608 | tf_op jit(solution)/shard_map/ppermute | solution.py:35
  19.9 0.3 %collective-permute-done.6 = bf16[16,768]{1,0:T(8,128)(2,1)S(1)} collective-permute-done((bf16[16,768]{1,0:T(8,128)(2,1)S(1)}, bf16[16,768]{1,0:T(8,128)(2,1)S(1)}, u32[]{:S(2)}, u32[]{:S(2)}) %collective-permute-start.6) | collective-permute-done | bytes 24608 | tf_op jit(solution)/shard_map/ppermute | solution.py:35
  20.2 0.0 collective-permute-done.7
  20.2 0.0 copy-done
  20.2 0.0 copy-done.1
  20.2 0.7 %add_select_fusion = f32[16,768]{1,0:T(8,128)} fusion(bf16[16,768]{1,0:T(8,128)(2,1)S(1)} %collective-permute-done.7, bf16[16,768]{1,0:T(8,128)(2,1)S(1)} %collective-permute-done.6, f32[16,768]{1,0:T(8,128)S(1)} %get-tuple-element.9, bf16[16,768]{1,0:T(8,128)(2,1)S(1)} %collective-permute-done.5, s32[768]{0:T(1024)S(1)} %copy-done, s32[16]{0:T(128)S(1)} %copy-done.1), kind=kLoop, calls=%fused_computation | loop fusion | flops 98304 | bytes 175168 | tf_op jit(solution)/shard_map/jit(_where)/select_n | solution.py:348
  (1 shorter events, 0.0 us)
Async XLA Ops:
  1.8 8.3 %collective-permute-start.3 = (bf16[2,8,2048]{2,1,0:T(8,128)(2,1)S(1)}, bf16[2,8,2048]{2,1,0:T(8,128)(2,1)S(1)}, u32[]{:S(2)}, u32[]{:S(2)}) collective-permute-start(bf16[2,8,2048]{2,1,0:T(8,128)(2,1)S(1)} %shard_map.82.after.kept.refs_0_), channel_id=1, source_target_pairs={{0,12},{1,15},{2,14},{3,13},{4,8},{5,11},{6,10},{7,9},{8,4},{9,7},... | collective-permute-start | bytes 196616 | tf_op jit(solution)/shard_map/ppermute | solution.py:35
  6.9 6.4 %collective-permute-start.2 = (bf16[2,8,2048]{2,1,0:T(8,128)(2,1)S(1)}, bf16[2,8,2048]{2,1,0:T(8,128)(2,1)S(1)}, u32[]{:S(2)}, u32[]{:S(2)}) collective-permute-start(bf16[2,8,2048]{2,1,0:T(8,128)(2,1)S(1)} %shard_map.82.after.kept.refs_0_), channel_id=1, source_target_pairs={{0,8},{1,11},{2,10},{3,9},{4,12},{5,15},{6,14},{7,13},{8,0},{9,3},... | collective-permute-start | bytes 196616 | tf_op jit(solution)/shard_map/ppermute | solution.py:35
  6.9 6.4 %collective-permute-start.1 = (bf16[2,8,2048]{2,1,0:T(8,128)(2,1)S(1)}, bf16[2,8,2048]{2,1,0:T(8,128)(2,1)S(1)}, u32[]{:S(2)}, u32[]{:S(2)}) collective-permute-start(bf16[2,8,2048]{2,1,0:T(8,128)(2,1)S(1)} %shard_map.82.after.kept.refs_0_), channel_id=1, source_target_pairs={{0,4},{1,7},{2,6},{3,5},{4,0},{5,3},{6,2},{7,1},{8,12},{9,15},{10,... | collective-permute-start | bytes 196616 | tf_op jit(solution)/shard_map/ppermute | solution.py:35
  7.5 5.7 %collective-permute-start = (bf16[2,8,2048]{2,1,0:T(8,128)(2,1)S(1)}, bf16[2,8,2048]{2,1,0:T(8,128)(2,1)S(1)}, u32[]{:S(2)}, u32[]{:S(2)}) collective-permute-start(bf16[2,8,2048]{2,1,0:T(8,128)(2,1)S(1)} %shard_map.82.after.kept.refs_0_), channel_id=1, source_target_pairs={{1,3},{3,1},{5,7},{7,5},{9,11},{11,9},{13,15},{15,13},{17,19},{19,... | collective-permute-start | bytes 196616 | tf_op jit(solution)/shard_map/ppermute | solution.py:35
  13.3 6.9 %copy-start = (s32[768]{0:T(1024)S(1)}, s32[768]{0:T(1024)}, u32[]{:S(2)}) copy-start(s32[768]{0:T(1024)} %param.12) | copy-start | bytes 9220
  13.3 6.9 %copy-start.1 = (s32[16]{0:T(128)S(1)}, s32[16]{0:T(128)}, u32[]{:S(2)}) copy-start(s32[16]{0:T(128)} %param.10) | copy-start | bytes 196
  13.3 1.6 %collective-permute-start.4 = (bf16[4,8,2048]{2,1,0:T(8,128)(2,1)S(1)}, bf16[4,8,2048]{2,1,0:T(8,128)(2,1)S(1)}, u32[]{:S(2)}, u32[]{:S(2)}) collective-permute-start(bf16[4,8,2048]{2,1,0:T(8,128)(2,1)S(1)} %shard_map.85), channel_id=1, source_target_pairs={{0,1},{1,0},{2,3},{3,2},{4,5},{5,4},{6,7},{7,6},{8,9},{9,8},{10,11... | collective-permute-start | bytes 393224 | tf_op jit(solution)/shard_map/ppermute | solution.py:35
  16.0 3.9 %collective-permute-start.5 = (bf16[16,768]{1,0:T(8,128)(2,1)S(1)}, bf16[16,768]{1,0:T(8,128)(2,1)S(1)}, u32[]{:S(2)}, u32[]{:S(2)}) collective-permute-start(bf16[16,768]{1,0:T(8,128)(2,1)S(1)} %get-tuple-element.10), channel_id=1, source_target_pairs={{0,2},{1,3},{2,0},{3,1},{4,6},{5,7},{6,4},{7,5},{8,10},{9,11},{10,... | collective-permute-start | bytes 73736 | tf_op jit(solution)/shard_map/ppermute | solution.py:35
  16.9 3.3 %collective-permute-start.6 = (bf16[16,768]{1,0:T(8,128)(2,1)S(1)}, bf16[16,768]{1,0:T(8,128)(2,1)S(1)}, u32[]{:S(2)}, u32[]{:S(2)}) collective-permute-start(bf16[16,768]{1,0:T(8,128)(2,1)S(1)} %get-tuple-element.11), channel_id=1, source_target_pairs={{0,3},{1,2},{2,1},{3,0},{4,7},{5,6},{6,5},{7,4},{8,11},{9,10},{10,... | collective-permute-start | bytes 73736 | tf_op jit(solution)/shard_map/ppermute | solution.py:35
  17.7 2.5 %collective-permute-start.7 = (bf16[16,768]{1,0:T(8,128)(2,1)S(1)}, bf16[16,768]{1,0:T(8,128)(2,1)S(1)}, u32[]{:S(2)}, u32[]{:S(2)}) collective-permute-start(bf16[16,768]{1,0:T(8,128)(2,1)S(1)} %get-tuple-element.12), channel_id=1, source_target_pairs={{0,1},{1,0},{2,3},{3,2},{4,5},{5,4},{6,7},{7,6},{8,9},{9,8},{10,11... | collective-permute-start | bytes 73736 | tf_op jit(solution)/shard_map/ppermute | solution.py:35

commit v13 on v7

--- a/solution.py
+++ b/solution.py
@@ -190,11 +190,11 @@
 
     for group in range(joined.shape[0]):
         product = lax.dot_general(
+            replay_rows[...],
             joined[group],
-            replay_rows[...],
             (((1,), (1,)), ((), ())),
             preferred_element_type=jnp.float32,
-        )
+        ).T
         for number in range(per_group):
             partials[place_of(group * per_group + number)] = product[
                 number * examples : (number + 1) * examples

time: 21 us -> 21 us (level)
  no operation moved by 1% of the time
where the time goes in v13:
time: 21 us; the launch traced here: 20.8 us
  starting transfers between devices  9.19 us (44%)
  waiting for transfers between devices  6.1 us (29%)
  Pallas kernels  4.69 us (22%)
  other arithmetic  0.69 us (3%)
    ppermute x8, starting transfers between devices, exchange(): return lax.ppermute(value, names, pairs)  9.19 us
    ppermute x8, waiting for transfers between devices, exchange(): return lax.ppermute(value, names, pairs)  6.1 us
    pallas_call x1, Pallas kernels, body(): pl.pallas_call(copy_kernel, out_shape=pltpu.VMEM((replay_total, depth), j...  1.9 us
    pallas_call x1, Pallas kernels, body(): pl.pallas_call(precondition_kernel, out_shape=[pltpu.VMEM((half_count, ex...  1.75 us
    pallas_call x1, Pallas kernels, body(): pl.pallas_call(functools.partial(score_kernel, sources, counts), out_shap...  1.03 us
    select_n x1, other arithmetic, body(): return jnp.where(self_pairs, jnp.zeros((), jnp.float32), summed_scores)  0.69 us
  transfers between devices with their start and end apart: 8, of which 4 were waited for; matrix products, arithmetic and copies ran while one was open for 0% of the time, Pallas kernels for 9%

profile of v13, /device:TPU:0, one launch (start us, length us, event | category | flops | bytes accessed | tf_op | source)
XLA Modules:
  0.0 20.8 jit_solution(5498975493838133019)
XLA Ops:
  0.0 1.7 %shard_map.82.after.refs_0_ = bf16[2,8,2048]{2,1,0:T(8,128)(2,1)S(1)} custom-call(s32[8]{0:T(128)} %counts_in.1, s32[2]{0:T(128)} %slots_in.1, bf16[8,2,64,128]{3,2,1,0:T(8,128)(2,1)} %factors_in.1, f32[2,64,64]{2,1,0:T(8,128)} %output_inverse_in.1, f32[2,64,64]{2,1,0:T(8,128)} %input_inverse_in.1), custom_call_target="tpu_custom_call" | custom-call | tf_op jit(solution)/shard_map/pallas_call | solution.py:239
  1.8 5.1 %collective-permute-start.3 = (bf16[2,8,2048]{2,1,0:T(8,128)(2,1)S(1)}, bf16[2,8,2048]{2,1,0:T(8,128)(2,1)S(1)}, u32[]{:S(2)}, u32[]{:S(2)}) collective-permute-start(bf16[2,8,2048]{2,1,0:T(8,128)(2,1)S(1)} %shard_map.82.after.refs_0_), channel_id=1, source_target_pairs={{0,12},{1,15},{2,14},{3,13},{4,8},{5,11},{6,10},{7,9},{8,4},{9,7},... | collective-permute-start | bytes 196616 | tf_op jit(solution)/shard_map/ppermute | solution.py:36
  6.9 0.0 collective-permute-start.2
  6.9 0.6 %collective-permute-start.1 = (bf16[2,8,2048]{2,1,0:T(8,128)(2,1)S(1)}, bf16[2,8,2048]{2,1,0:T(8,128)(2,1)S(1)}, u32[]{:S(2)}, u32[]{:S(2)}) collective-permute-start(bf16[2,8,2048]{2,1,0:T(8,128)(2,1)S(1)} %shard_map.82.after.refs_0_), channel_id=1, source_target_pairs={{0,4},{1,7},{2,6},{3,5},{4,0},{5,3},{6,2},{7,1},{8,12},{9,15},{10,... | collective-permute-start | bytes 196616 | tf_op jit(solution)/shard_map/ppermute | solution.py:36
  7.5 0.7 %collective-permute-start = (bf16[2,8,2048]{2,1,0:T(8,128)(2,1)S(1)}, bf16[2,8,2048]{2,1,0:T(8,128)(2,1)S(1)}, u32[]{:S(2)}, u32[]{:S(2)}) collective-permute-start(bf16[2,8,2048]{2,1,0:T(8,128)(2,1)S(1)} %shard_map.82.after.refs_0_), channel_id=1, source_target_pairs={{1,3},{3,1},{5,7},{7,5},{9,11},{11,9},{13,15},{15,13},{17,19},{19,... | collective-permute-start | bytes 196616 | tf_op jit(solution)/shard_map/ppermute | solution.py:36
  8.2 1.9 %shard_map.83.refs_5_.refs_6_ = bf16[768,2048]{1,0:T(8,128)(2,1)S(1)} custom-call(bf16[768,2048]{1,0:T(8,128)(2,1)} %bitcast.1, bf16[2,8,2048]{2,1,0:T(8,128)(2,1)S(1)} %shard_map.82.after.refs_0_), custom_call_target="tpu_custom_call" | custom-call | bytes 6291456 | tf_op jit(solution)/shard_map/pallas_call | solution.py:263
  10.1 0.0 copy-start
  10.1 0.0 copy-start.1
  10.1 0.0 collective-permute-done.3.refs_4_
  10.1 3.1 %collective-permute-done.2.refs_3_ = bf16[2,8,2048]{2,1,0:T(8,128)(2,1)S(1)} collective-permute-done((bf16[2,8,2048]{2,1,0:T(8,128)(2,1)S(1)}, bf16[2,8,2048]{2,1,0:T(8,128)(2,1)S(1)}, u32[]{:S(2)}, u32[]{:S(2)}) %collective-permute-start.2) | collective-permute-done | bytes 65568 | tf_op jit(solution)/shard_map/ppermute | solution.py:36
  13.3 0.0 collective-permute-done.1.refs_2_
  13.3 0.0 collective-permute-done.refs_1_
  13.3 0.6 %collective-permute-start.4 = (bf16[4,8,2048]{2,1,0:T(8,128)(2,1)S(1)}, bf16[4,8,2048]{2,1,0:T(8,128)(2,1)S(1)}, u32[]{:S(2)}, u32[]{:S(2)}) collective-permute-start(bf16[4,8,2048]{2,1,0:T(8,128)(2,1)S(1)} %shard_map.84), channel_id=1, source_target_pairs={{0,1},{1,0},{2,3},{3,2},{4,5},{5,4},{6,7},{7,6},{8,9},{9,8},{10,11... | collective-permute-start | bytes 393224 | tf_op jit(solution)/shard_map/ppermute | solution.py:36
  13.8 1.0 %collective-permute-done.4.refs_5_ = bf16[4,8,2048]{2,1,0:T(8,128)(2,1)S(1)} collective-permute-done((bf16[4,8,2048]{2,1,0:T(8,128)(2,1)S(1)}, bf16[4,8,2048]{2,1,0:T(8,128)(2,1)S(1)}, u32[]{:S(2)}, u32[]{:S(2)}) %collective-permute-start.4) | collective-permute-done | bytes 131104 | tf_op jit(solution)/shard_map/ppermute | solution.py:36
  14.8 1.0 %shard_map.85 = (f32[16,768]{1,0:T(8,128)S(1)}, bf16[16,768]{1,0:T(8,128)(2,1)S(1)}, bf16[16,768]{1,0:T(8,128)(2,1)S(1)}, bf16[16,768]{1,0:T(8,128)(2,1)S(1)}) custom-call(bf16[2,8,2048]{2,1,0:T(8,128)(2,1)S(1)} %shard_map.82.after.refs_0_, bf16[2,8,2048]{2,1,0:T(8,128)(2,1)S(1)} %collective-permute-done.refs_1_, ...), custom_call_target="tpu_custom_call" | custom-call | flops 201326592 | bytes 3604480 | tf_op jit(solution)/shard_map/pallas_call | solution.py:299
  15.9 0.9 %collective-permute-start.5 = (bf16[16,768]{1,0:T(8,128)(2,1)S(1)}, bf16[16,768]{1,0:T(8,128)(2,1)S(1)}, u32[]{:S(2)}, u32[]{:S(2)}) collective-permute-start(bf16[16,768]{1,0:T(8,128)(2,1)S(1)} %get-tuple-element.10), channel_id=1, source_target_pairs={{0,2},{1,3},{2,0},{3,1},{4,6},{5,7},{6,4},{7,5},{8,10},{9,11},{10,... | collective-permute-start | bytes 73736 | tf_op jit(solution)/shard_map/ppermute | solution.py:36
  16.8 0.9 %collective-permute-start.6 = (bf16[16,768]{1,0:T(8,128)(2,1)S(1)}, bf16[16,768]{1,0:T(8,128)(2,1)S(1)}, u32[]{:S(2)}, u32[]{:S(2)}) collective-permute-start(bf16[16,768]{1,0:T(8,128)(2,1)S(1)} %get-tuple-element.11), channel_id=1, source_target_pairs={{0,3},{1,2},{2,1},{3,0},{4,7},{5,6},{6,5},{7,4},{8,11},{9,10},{10,... | collective-permute-start | bytes 73736 | tf_op jit(solution)/shard_map/ppermute | solution.py:36
  17.6 0.4 %collective-permute-start.7 = (bf16[16,768]{1,0:T(8,128)(2,1)S(1)}, bf16[16,768]{1,0:T(8,128)(2,1)S(1)}, u32[]{:S(2)}, u32[]{:S(2)}) collective-permute-start(bf16[16,768]{1,0:T(8,128)(2,1)S(1)} %get-tuple-element.12), channel_id=1, source_target_pairs={{0,1},{1,0},{2,3},{3,2},{4,5},{5,4},{6,7},{7,6},{8,9},{9,8},{10,11... | collective-permute-start | bytes 73736 | tf_op jit(solution)/shard_map/ppermute | solution.py:36
  18.1 1.7 %collective-permute-done.5 = bf16[16,768]{1,0:T(8,128)(2,1)S(1)} collective-permute-done((bf16[16,768]{1,0:T(8,128)(2,1)S(1)}, bf16[16,768]{1,0:T(8,128)(2,1)S(1)}, u32[]{:S(2)}, u32[]{:S(2)}) %collective-permute-start.5) | collective-permute-done | bytes 24608 | tf_op jit(solution)/shard_map/ppermute | solution.py:36
  19.8 0.3 %collective-permute-done.6 = bf16[16,768]{1,0:T(8,128)(2,1)S(1)} collective-permute-done((bf16[16,768]{1,0:T(8,128)(2,1)S(1)}, bf16[16,768]{1,0:T(8,128)(2,1)S(1)}, u32[]{:S(2)}, u32[]{:S(2)}) %collective-permute-start.6) | collective-permute-done | bytes 24608 | tf_op jit(solution)/shard_map/ppermute | solution.py:36
  20.1 0.0 collective-permute-done.7
  20.1 0.0 copy-done
  20.1 0.0 copy-done.1
  20.1 0.7 %add_select_fusion = f32[16,768]{1,0:T(8,128)} fusion(bf16[16,768]{1,0:T(8,128)(2,1)S(1)} %collective-permute-done.7, bf16[16,768]{1,0:T(8,128)(2,1)S(1)} %collective-permute-done.6, f32[16,768]{1,0:T(8,128)S(1)} %get-tuple-element.9, bf16[16,768]{1,0:T(8,128)(2,1)S(1)} %collective-permute-done.5, s32[768]{0:T(1024)S(1)} %copy-done, s32[16]{0:T(128)S(1)} %copy-done.1), kind=kLoop, calls=%fused_computation | loop fusion | flops 98304 | bytes 175168 | tf_op jit(solution)/shard_map/jit(_where)/select_n | solution.py:324
  (1 shorter events, 0.0 us)
Async XLA Ops:
  1.8 8.4 %collective-permute-start.3 = (bf16[2,8,2048]{2,1,0:T(8,128)(2,1)S(1)}, bf16[2,8,2048]{2,1,0:T(8,128)(2,1)S(1)}, u32[]{:S(2)}, u32[]{:S(2)}) collective-permute-start(bf16[2,8,2048]{2,1,0:T(8,128)(2,1)S(1)} %shard_map.82.after.refs_0_), channel_id=1, source_target_pairs={{0,12},{1,15},{2,14},{3,13},{4,8},{5,11},{6,10},{7,9},{8,4},{9,7},... | collective-permute-start | bytes 196616 | tf_op jit(solution)/shard_map/ppermute | solution.py:36
  6.9 6.4 %collective-permute-start.2 = (bf16[2,8,2048]{2,1,0:T(8,128)(2,1)S(1)}, bf16[2,8,2048]{2,1,0:T(8,128)(2,1)S(1)}, u32[]{:S(2)}, u32[]{:S(2)}) collective-permute-start(bf16[2,8,2048]{2,1,0:T(8,128)(2,1)S(1)} %shard_map.82.after.refs_0_), channel_id=1, source_target_pairs={{0,8},{1,11},{2,10},{3,9},{4,12},{5,15},{6,14},{7,13},{8,0},{9,3},... | collective-permute-start | bytes 196616 | tf_op jit(solution)/shard_map/ppermute | solution.py:36
  6.9 6.4 %collective-permute-start.1 = (bf16[2,8,2048]{2,1,0:T(8,128)(2,1)S(1)}, bf16[2,8,2048]{2,1,0:T(8,128)(2,1)S(1)}, u32[]{:S(2)}, u32[]{:S(2)}) collective-permute-start(bf16[2,8,2048]{2,1,0:T(8,128)(2,1)S(1)} %shard_map.82.after.refs_0_), channel_id=1, source_target_pairs={{0,4},{1,7},{2,6},{3,5},{4,0},{5,3},{6,2},{7,1},{8,12},{9,15},{10,... | collective-permute-start | bytes 196616 | tf_op jit(solution)/shard_map/ppermute | solution.py:36
  7.5 5.7 %collective-permute-start = (bf16[2,8,2048]{2,1,0:T(8,128)(2,1)S(1)}, bf16[2,8,2048]{2,1,0:T(8,128)(2,1)S(1)}, u32[]{:S(2)}, u32[]{:S(2)}) collective-permute-start(bf16[2,8,2048]{2,1,0:T(8,128)(2,1)S(1)} %shard_map.82.after.refs_0_), channel_id=1, source_target_pairs={{1,3},{3,1},{5,7},{7,5},{9,11},{11,9},{13,15},{15,13},{17,19},{19,... | collective-permute-start | bytes 196616 | tf_op jit(solution)/shard_map/ppermute | solution.py:36
  10.1 10.0 %copy-start = (s32[768]{0:T(1024)S(1)}, s32[768]{0:T(1024)}, u32[]{:S(2)}) copy-start(s32[768]{0:T(1024)} %param.12) | copy-start | bytes 9220
  10.1 10.0 %copy-start.1 = (s32[16]{0:T(128)S(1)}, s32[16]{0:T(128)}, u32[]{:S(2)}) copy-start(s32[16]{0:T(128)} %param.10) | copy-start | bytes 196
  13.3 1.5 %collective-permute-start.4 = (bf16[4,8,2048]{2,1,0:T(8,128)(2,1)S(1)}, bf16[4,8,2048]{2,1,0:T(8,128)(2,1)S(1)}, u32[]{:S(2)}, u32[]{:S(2)}) collective-permute-start(bf16[4,8,2048]{2,1,0:T(8,128)(2,1)S(1)} %shard_map.84), channel_id=1, source_target_pairs={{0,1},{1,0},{2,3},{3,2},{4,5},{5,4},{6,7},{7,6},{8,9},{9,8},{10,11... | collective-permute-start | bytes 393224 | tf_op jit(solution)/shard_map/ppermute | solution.py:36
  15.9 3.9 %collective-permute-start.5 = (bf16[16,768]{1,0:T(8,128)(2,1)S(1)}, bf16[16,768]{1,0:T(8,128)(2,1)S(1)}, u32[]{:S(2)}, u32[]{:S(2)}) collective-permute-start(bf16[16,768]{1,0:T(8,128)(2,1)S(1)} %get-tuple-element.10), channel_id=1, source_target_pairs={{0,2},{1,3},{2,0},{3,1},{4,6},{5,7},{6,4},{7,5},{8,10},{9,11},{10,... | collective-permute-start | bytes 73736 | tf_op jit(solution)/shard_map/ppermute | solution.py:36
  16.8 3.3 %collective-permute-start.6 = (bf16[16,768]{1,0:T(8,128)(2,1)S(1)}, bf16[16,768]{1,0:T(8,128)(2,1)S(1)}, u32[]{:S(2)}, u32[]{:S(2)}) collective-permute-start(bf16[16,768]{1,0:T(8,128)(2,1)S(1)} %get-tuple-element.11), channel_id=1, source_target_pairs={{0,3},{1,2},{2,1},{3,0},{4,7},{5,6},{6,5},{7,4},{8,11},{9,10},{10,... | collective-permute-start | bytes 73736 | tf_op jit(solution)/shard_map/ppermute | solution.py:36
  17.6 2.4 %collective-permute-start.7 = (bf16[16,768]{1,0:T(8,128)(2,1)S(1)}, bf16[16,768]{1,0:T(8,128)(2,1)S(1)}, u32[]{:S(2)}, u32[]{:S(2)}) collective-permute-start(bf16[16,768]{1,0:T(8,128)(2,1)S(1)} %get-tuple-element.12), channel_id=1, source_target_pairs={{0,1},{1,0},{2,3},{3,2},{4,5},{5,4},{6,7},{7,6},{8,9},{9,8},{10,11... | collective-permute-start | bytes 73736 | tf_op jit(solution)/shard_map/ppermute | solution.py:36

commit v14 on v13

--- a/solution.py
+++ b/solution.py
@@ -255,7 +255,7 @@
     axes = ("replay", "module", "half")
     counts = (replay_count, module_count, half_count)
     gathered = {}
-    for replay_step in range(replay_count):
+    for replay_step in sorted(range(replay_count), key=lambda step: (step.bit_length(), -step)):
         for turn in range(turns):
             gathered[replay_step, turn, 0] = exchange(
                 outgoing[turn], axes, counts, lambda half: (replay_step, turn * half_count + half, 0)

time: 21 us -> 21.2 us (level)
  waiting for transfers between devices: 6.1 us -> 6.94 us
  starting transfers between devices: 9.19 us -> 8.61 us
    ppermute x8, waiting for transfers between devices: 6.1 us -> 6.94 us  [exchange(): return lax.ppermute(value, names, pairs)]
    ppermute x8, starting transfers between devices: 9.19 us -> 8.61 us  [exchange(): return lax.ppermute(value, names, pairs)]
  transfers between devices with their start and end apart: 8 -> 8, of which waited for: 4 -> 6; matrix products, arithmetic and copies ran while one was open for 0% -> 0% of each run, Pallas kernels for 9% -> 9%
where the time goes in v14:
time: 21.2 us; the launch traced here: 21 us
  starting transfers between devices  8.61 us (41%)
  waiting for transfers between devices  6.94 us (33%)
  Pallas kernels  4.69 us (22%)
  other arithmetic  0.69 us (3%)
    ppermute x8, starting transfers between devices, exchange(): return lax.ppermute(value, names, pairs)  8.61 us
    ppermute x8, waiting for transfers between devices, exchange(): return lax.ppermute(value, names, pairs)  6.94 us
    pallas_call x1, Pallas kernels, body(): pl.pallas_call(copy_kernel, out_shape=pltpu.VMEM((replay_total, depth), j...  1.9 us
    pallas_call x1, Pallas kernels, body(): pl.pallas_call(precondition_kernel, out_shape=[pltpu.VMEM((half_count, ex...  1.75 us
    pallas_call x1, Pallas kernels, body(): pl.pallas_call(functools.partial(score_kernel, sources, counts), out_shap...  1.03 us
    select_n x1, other arithmetic, body(): return jnp.where(self_pairs, jnp.zeros((), jnp.float32), summed_scores)  0.69 us
  transfers between devices with their start and end apart: 8, of which 6 were waited for; matrix products, arithmetic and copies ran while one was open for 0% of the time, Pallas kernels for 9%

profile of v14, /device:TPU:0, one launch (start us, length us, event | category | flops | bytes accessed | tf_op | source)
XLA Modules:
  0.0 21.0 jit_solution(1204928366927776116)
XLA Ops:
  0.0 1.7 %shard_map.82.after.refs_0_ = bf16[2,8,2048]{2,1,0:T(8,128)(2,1)S(1)} custom-call(s32[8]{0:T(128)} %counts_in.1, s32[2]{0:T(128)} %slots_in.1, bf16[8,2,64,128]{3,2,1,0:T(8,128)(2,1)} %factors_in.1, f32[2,64,64]{2,1,0:T(8,128)} %output_inverse_in.1, f32[2,64,64]{2,1,0:T(8,128)} %input_inverse_in.1), custom_call_target="tpu_custom_call" | custom-call | tf_op jit(solution)/shard_map/pallas_call | solution.py:239
  1.8 4.1 %collective-permute-start.3 = (bf16[2,8,2048]{2,1,0:T(8,128)(2,1)S(1)}, bf16[2,8,2048]{2,1,0:T(8,128)(2,1)S(1)}, u32[]{:S(2)}, u32[]{:S(2)}) collective-permute-start(bf16[2,8,2048]{2,1,0:T(8,128)(2,1)S(1)} %shard_map.82.after.refs_0_), channel_id=1, source_target_pairs={{0,8},{1,11},{2,10},{3,9},{4,12},{5,15},{6,14},{7,13},{8,0},{9,3},... | collective-permute-start | bytes 196616 | tf_op jit(solution)/shard_map/ppermute | solution.py:36
  5.9 1.3 %collective-permute-start.2 = (bf16[2,8,2048]{2,1,0:T(8,128)(2,1)S(1)}, bf16[2,8,2048]{2,1,0:T(8,128)(2,1)S(1)}, u32[]{:S(2)}, u32[]{:S(2)}) collective-permute-start(bf16[2,8,2048]{2,1,0:T(8,128)(2,1)S(1)} %shard_map.82.after.refs_0_), channel_id=1, source_target_pairs={{0,12},{1,15},{2,14},{3,13},{4,8},{5,11},{6,10},{7,9},{8,4},{9,7},... | collective-permute-start | bytes 196616 | tf_op jit(solution)/shard_map/ppermute | solution.py:36
  7.2 0.2 %collective-permute-start.1 = (bf16[2,8,2048]{2,1,0:T(8,128)(2,1)S(1)}, bf16[2,8,2048]{2,1,0:T(8,128)(2,1)S(1)}, u32[]{:S(2)}, u32[]{:S(2)}) collective-permute-start(bf16[2,8,2048]{2,1,0:T(8,128)(2,1)S(1)} %shard_map.82.after.refs_0_), channel_id=1, source_target_pairs={{0,4},{1,7},{2,6},{3,5},{4,0},{5,3},{6,2},{7,1},{8,12},{9,15},{10,... | collective-permute-start | bytes 196616 | tf_op jit(solution)/shard_map/ppermute | solution.py:36
  7.4 0.7 %collective-permute-start = (bf16[2,8,2048]{2,1,0:T(8,128)(2,1)S(1)}, bf16[2,8,2048]{2,1,0:T(8,128)(2,1)S(1)}, u32[]{:S(2)}, u32[]{:S(2)}) collective-permute-start(bf16[2,8,2048]{2,1,0:T(8,128)(2,1)S(1)} %shard_map.82.after.refs_0_), channel_id=1, source_target_pairs={{1,3},{3,1},{5,7},{7,5},{9,11},{11,9},{13,15},{15,13},{17,19},{19,... | collective-permute-start | bytes 196616 | tf_op jit(solution)/shard_map/ppermute | solution.py:36
  8.1 1.9 %shard_map.83.refs_5_.refs_6_ = bf16[768,2048]{1,0:T(8,128)(2,1)S(1)} custom-call(bf16[768,2048]{1,0:T(8,128)(2,1)} %bitcast.1, bf16[2,8,2048]{2,1,0:T(8,128)(2,1)S(1)} %shard_map.82.after.refs_0_), custom_call_target="tpu_custom_call" | custom-call | bytes 6291456 | tf_op jit(solution)/shard_map/pallas_call | solution.py:263
  10.0 0.0 copy-start
  10.0 0.0 copy-start.1
  10.0 0.1 collective-permute-done.3.refs_4_
  10.1 2.2 %collective-permute-done.2.refs_3_ = bf16[2,8,2048]{2,1,0:T(8,128)(2,1)S(1)} collective-permute-done((bf16[2,8,2048]{2,1,0:T(8,128)(2,1)S(1)}, bf16[2,8,2048]{2,1,0:T(8,128)(2,1)S(1)}, u32[]{:S(2)}, u32[]{:S(2)}) %collective-permute-start.2) | collective-permute-done | bytes 65568 | tf_op jit(solution)/shard_map/ppermute | solution.py:36
  12.3 1.1 %collective-permute-done.1.refs_2_ = bf16[2,8,2048]{2,1,0:T(8,128)(2,1)S(1)} collective-permute-done((bf16[2,8,2048]{2,1,0:T(8,128)(2,1)S(1)}, bf16[2,8,2048]{2,1,0:T(8,128)(2,1)S(1)}, u32[]{:S(2)}, u32[]{:S(2)}) %collective-permute-start.1) | collective-permute-done | bytes 65568 | tf_op jit(solution)/shard_map/ppermute | solution.py:36
  13.4 0.0 collective-permute-done.refs_1_
  13.5 0.1 collective-permute-start.4
  13.5 1.3 %collective-permute-done.4.refs_5_ = bf16[4,8,2048]{2,1,0:T(8,128)(2,1)S(1)} collective-permute-done((bf16[4,8,2048]{2,1,0:T(8,128)(2,1)S(1)}, bf16[4,8,2048]{2,1,0:T(8,128)(2,1)S(1)}, u32[]{:S(2)}, u32[]{:S(2)}) %collective-permute-start.4) | collective-permute-done | bytes 131104 | tf_op jit(solution)/shard_map/ppermute | solution.py:36
  14.9 1.0 %shard_map.85 = (f32[16,768]{1,0:T(8,128)S(1)}, bf16[16,768]{1,0:T(8,128)(2,1)S(1)}, bf16[16,768]{1,0:T(8,128)(2,1)S(1)}, bf16[16,768]{1,0:T(8,128)(2,1)S(1)}) custom-call(bf16[2,8,2048]{2,1,0:T(8,128)(2,1)S(1)} %shard_map.82.after.refs_0_, bf16[2,8,2048]{2,1,0:T(8,128)(2,1)S(1)} %collective-permute-done.refs_1_, ...), custom_call_target="tpu_custom_call" | custom-call | flops 201326592 | bytes 3604480 | tf_op jit(solution)/shard_map/pallas_call | solution.py:299
  15.9 1.1 %collective-permute-start.5 = (bf16[16,768]{1,0:T(8,128)(2,1)S(1)}, bf16[16,768]{1,0:T(8,128)(2,1)S(1)}, u32[]{:S(2)}, u32[]{:S(2)}) collective-permute-start(bf16[16,768]{1,0:T(8,128)(2,1)S(1)} %get-tuple-element.10), channel_id=1, source_target_pairs={{0,2},{1,3},{2,0},{3,1},{4,6},{5,7},{6,4},{7,5},{8,10},{9,11},{10,... | collective-permute-start | bytes 73736 | tf_op jit(solution)/shard_map/ppermute | solution.py:36
  17.0 0.4 %collective-permute-start.6 = (bf16[16,768]{1,0:T(8,128)(2,1)S(1)}, bf16[16,768]{1,0:T(8,128)(2,1)S(1)}, u32[]{:S(2)}, u32[]{:S(2)}) collective-permute-start(bf16[16,768]{1,0:T(8,128)(2,1)S(1)} %get-tuple-element.11), channel_id=1, source_target_pairs={{0,3},{1,2},{2,1},{3,0},{4,7},{5,6},{6,5},{7,4},{8,11},{9,10},{10,... | collective-permute-start | bytes 73736 | tf_op jit(solution)/shard_map/ppermute | solution.py:36
  17.5 0.6 %collective-permute-start.7 = (bf16[16,768]{1,0:T(8,128)(2,1)S(1)}, bf16[16,768]{1,0:T(8,128)(2,1)S(1)}, u32[]{:S(2)}, u32[]{:S(2)}) collective-permute-start(bf16[16,768]{1,0:T(8,128)(2,1)S(1)} %get-tuple-element.12), channel_id=1, source_target_pairs={{0,1},{1,0},{2,3},{3,2},{4,5},{5,4},{6,7},{7,6},{8,9},{9,8},{10,11... | collective-permute-start | bytes 73736 | tf_op jit(solution)/shard_map/ppermute | solution.py:36
  18.1 1.7 %collective-permute-done.5 = bf16[16,768]{1,0:T(8,128)(2,1)S(1)} collective-permute-done((bf16[16,768]{1,0:T(8,128)(2,1)S(1)}, bf16[16,768]{1,0:T(8,128)(2,1)S(1)}, u32[]{:S(2)}, u32[]{:S(2)}) %collective-permute-start.5) | collective-permute-done | bytes 24608 | tf_op jit(solution)/shard_map/ppermute | solution.py:36
  19.8 0.5 %collective-permute-done.6 = bf16[16,768]{1,0:T(8,128)(2,1)S(1)} collective-permute-done((bf16[16,768]{1,0:T(8,128)(2,1)S(1)}, bf16[16,768]{1,0:T(8,128)(2,1)S(1)}, u32[]{:S(2)}, u32[]{:S(2)}) %collective-permute-start.6) | collective-permute-done | bytes 24608 | tf_op jit(solution)/shard_map/ppermute | solution.py:36
  20.3 0.0 collective-permute-done.7
  20.3 0.0 copy-done
  20.3 0.0 copy-done.1
  20.3 0.7 %add_select_fusion = f32[16,768]{1,0:T(8,128)} fusion(bf16[16,768]{1,0:T(8,128)(2,1)S(1)} %collective-permute-done.7, bf16[16,768]{1,0:T(8,128)(2,1)S(1)} %collective-permute-done.6, f32[16,768]{1,0:T(8,128)S(1)} %get-tuple-element.9, bf16[16,768]{1,0:T(8,128)(2,1)S(1)} %collective-permute-done.5, s32[768]{0:T(1024)S(1)} %copy-done, s32[16]{0:T(128)S(1)} %copy-done.1), kind=kLoop, calls=%fused_computation | loop fusion | flops 98304 | bytes 175168 | tf_op jit(solution)/shard_map/jit(_where)/select_n | solution.py:324
  (1 shorter events, 0.0 us)
Async XLA Ops:
  1.8 8.3 %collective-permute-start.3 = (bf16[2,8,2048]{2,1,0:T(8,128)(2,1)S(1)}, bf16[2,8,2048]{2,1,0:T(8,128)(2,1)S(1)}, u32[]{:S(2)}, u32[]{:S(2)}) collective-permute-start(bf16[2,8,2048]{2,1,0:T(8,128)(2,1)S(1)} %shard_map.82.after.refs_0_), channel_id=1, source_target_pairs={{0,8},{1,11},{2,10},{3,9},{4,12},{5,15},{6,14},{7,13},{8,0},{9,3},... | collective-permute-start | bytes 196616 | tf_op jit(solution)/shard_map/ppermute | solution.py:36
  5.9 6.5 %collective-permute-start.2 = (bf16[2,8,2048]{2,1,0:T(8,128)(2,1)S(1)}, bf16[2,8,2048]{2,1,0:T(8,128)(2,1)S(1)}, u32[]{:S(2)}, u32[]{:S(2)}) collective-permute-start(bf16[2,8,2048]{2,1,0:T(8,128)(2,1)S(1)} %shard_map.82.after.refs_0_), channel_id=1, source_target_pairs={{0,12},{1,15},{2,14},{3,13},{4,8},{5,11},{6,10},{7,9},{8,4},{9,7},... | collective-permute-start | bytes 196616 | tf_op jit(solution)/shard_map/ppermute | solution.py:36
  7.2 6.2 %collective-permute-start.1 = (bf16[2,8,2048]{2,1,0:T(8,128)(2,1)S(1)}, bf16[2,8,2048]{2,1,0:T(8,128)(2,1)S(1)}, u32[]{:S(2)}, u32[]{:S(2)}) collective-permute-start(bf16[2,8,2048]{2,1,0:T(8,128)(2,1)S(1)} %shard_map.82.after.refs_0_), channel_id=1, source_target_pairs={{0,4},{1,7},{2,6},{3,5},{4,0},{5,3},{6,2},{7,1},{8,12},{9,15},{10,... | collective-permute-start | bytes 196616 | tf_op jit(solution)/shard_map/ppermute | solution.py:36
  7.4 6.0 %collective-permute-start = (bf16[2,8,2048]{2,1,0:T(8,128)(2,1)S(1)}, bf16[2,8,2048]{2,1,0:T(8,128)(2,1)S(1)}, u32[]{:S(2)}, u32[]{:S(2)}) collective-permute-start(bf16[2,8,2048]{2,1,0:T(8,128)(2,1)S(1)} %shard_map.82.after.refs_0_), channel_id=1, source_target_pairs={{1,3},{3,1},{5,7},{7,5},{9,11},{11,9},{13,15},{15,13},{17,19},{19,... | collective-permute-start | bytes 196616 | tf_op jit(solution)/shard_map/ppermute | solution.py:36
  10.0 10.3 %copy-start = (s32[768]{0:T(1024)S(1)}, s32[768]{0:T(1024)}, u32[]{:S(2)}) copy-start(s32[768]{0:T(1024)} %param.12) | copy-start | bytes 9220
  10.0 10.3 %copy-start.1 = (s32[16]{0:T(128)S(1)}, s32[16]{0:T(128)}, u32[]{:S(2)}) copy-start(s32[16]{0:T(128)} %param.10) | copy-start | bytes 196
  13.5 1.4 %collective-permute-start.4 = (bf16[4,8,2048]{2,1,0:T(8,128)(2,1)S(1)}, bf16[4,8,2048]{2,1,0:T(8,128)(2,1)S(1)}, u32[]{:S(2)}, u32[]{:S(2)}) collective-permute-start(bf16[4,8,2048]{2,1,0:T(8,128)(2,1)S(1)} %shard_map.84), channel_id=1, source_target_pairs={{0,1},{1,0},{2,3},{3,2},{4,5},{5,4},{6,7},{7,6},{8,9},{9,8},{10,11... | collective-permute-start | bytes 393224 | tf_op jit(solution)/shard_map/ppermute | solution.py:36
  15.9 3.9 %collective-permute-start.5 = (bf16[16,768]{1,0:T(8,128)(2,1)S(1)}, bf16[16,768]{1,0:T(8,128)(2,1)S(1)}, u32[]{:S(2)}, u32[]{:S(2)}) collective-permute-start(bf16[16,768]{1,0:T(8,128)(2,1)S(1)} %get-tuple-element.10), channel_id=1, source_target_pairs={{0,2},{1,3},{2,0},{3,1},{4,6},{5,7},{6,4},{7,5},{8,10},{9,11},{10,... | collective-permute-start | bytes 73736 | tf_op jit(solution)/shard_map/ppermute | solution.py:36
  17.0 3.3 %collective-permute-start.6 = (bf16[16,768]{1,0:T(8,128)(2,1)S(1)}, bf16[16,768]{1,0:T(8,128)(2,1)S(1)}, u32[]{:S(2)}, u32[]{:S(2)}) collective-permute-start(bf16[16,768]{1,0:T(8,128)(2,1)S(1)} %get-tuple-element.11), channel_id=1, source_target_pairs={{0,3},{1,2},{2,1},{3,0},{4,7},{5,6},{6,5},{7,4},{8,11},{9,10},{10,... | collective-permute-start | bytes 73736 | tf_op jit(solution)/shard_map/ppermute | solution.py:36
  17.5 2.8 %collective-permute-start.7 = (bf16[16,768]{1,0:T(8,128)(2,1)S(1)}, bf16[16,768]{1,0:T(8,128)(2,1)S(1)}, u32[]{:S(2)}, u32[]{:S(2)}) collective-permute-start(bf16[16,768]{1,0:T(8,128)(2,1)S(1)} %get-tuple-element.12), channel_id=1, source_target_pairs={{0,1},{1,0},{2,3},{3,2},{4,5},{5,4},{6,7},{7,6},{8,9},{9,8},{10,11... | collective-permute-start | bytes 73736 | tf_op jit(solution)/shard_map/ppermute | solution.py:36

commit v15 on v14

--- a/solution.py
+++ b/solution.py
@@ -34,6 +34,11 @@
         if target != source:
             pairs.append((source, target))
     return lax.ppermute(value, names, pairs)
+
+
+def turn_order(count, half):
+    order = list(range(count))
+    return order[:-2] + order[:-3:-1] if half % 2 and count > 2 else order
 
 
 def split(value):
@@ -181,8 +186,10 @@
         ).astype(jnp.bfloat16)
 
     def place_of(number):
-        replay_step, turn, half_step = sources[number]
+        number, turn, half_step = sources[number]
         handler = origin(half_place, half_step, half_count)
+        even, odd = (turn_order(replay_count, half)[number] for half in range(2))
+        replay_step = jnp.where(handler % 2 == 1, odd, even)
         module_step = turn * half_count + handler
         return origin(replay_place, replay_step, replay_count) * module_count + origin(
             module_place, module_step, module_count
@@ -255,10 +262,13 @@
     axes = ("replay", "module", "half")
     counts = (replay_count, module_count, half_count)
     gathered = {}
-    for replay_step in sorted(range(replay_count), key=lambda step: (step.bit_length(), -step)):
+    for number in range(replay_count):
         for turn in range(turns):
-            gathered[replay_step, turn, 0] = exchange(
-                outgoing[turn], axes, counts, lambda half: (replay_step, turn * half_count + half, 0)
+            gathered[number, turn, 0] = exchange(
+                outgoing[turn],
+                axes,
+                counts,
+                lambda half: (turn_order(replay_count, half)[number], turn * half_count + half, 0),
             )
     replay_rows = pl.pallas_call(
         copy_kernel,
@@ -288,9 +298,9 @@
         for half_step, pack in enumerate(packs, 1)
     ]
     sources = [
-        (replay_step, turn, half_step)
+        (number, turn, half_step)
         for half_step in range(half_count)
-        for replay_step, turn, _ in gathered
+        for number, turn, _ in gathered
     ]
 
     rows = blocks * examples

time: 21.2 us -> 21.1 us (level)
  waiting for transfers between devices: 6.94 us -> 6.68 us
    ppermute x8, waiting for transfers between devices: 6.94 us -> 6.68 us  [exchange(): return lax.ppermute(value, names, pairs)]
  transfers between devices with their start and end apart: 8 -> 8, of which waited for: 6 -> 4; matrix products, arithmetic and copies ran while one was open for 0% -> 0% of each run, Pallas kernels for 9% -> 9%
where the time goes in v15:
time: 21.1 us; the launch traced here: 20.9 us
  starting transfers between devices  8.79 us (42%)
  waiting for transfers between devices  6.68 us (32%)
  Pallas kernels  4.69 us (22%)
  other arithmetic  0.69 us (3%)
    ppermute x8, starting transfers between devices, exchange(): return lax.ppermute(value, names, pairs)  8.79 us
    ppermute x8, waiting for transfers between devices, exchange(): return lax.ppermute(value, names, pairs)  6.68 us
    pallas_call x1, Pallas kernels, body(): pl.pallas_call(copy_kernel, out_shape=pltpu.VMEM((replay_total, depth), j...  1.9 us
    pallas_call x1, Pallas kernels, body(): pl.pallas_call(precondition_kernel, out_shape=[pltpu.VMEM((half_count, ex...  1.75 us
    pallas_call x1, Pallas kernels, body(): pl.pallas_call(functools.partial(score_kernel, sources, counts), out_shap...  1.03 us
    select_n x1, other arithmetic, body(): return jnp.where(self_pairs, jnp.zeros((), jnp.float32), summed_scores)  0.69 us
  transfers between devices with their start and end apart: 8, of which 4 were waited for; matrix products, arithmetic and copies ran while one was open for 0% of the time, Pallas kernels for 9%

profile of v15, /device:TPU:0, one launch (start us, length us, event | category | flops | bytes accessed | tf_op | source)
XLA Modules:
  0.0 20.9 jit_solution(11726529756114538548)
XLA Ops:
  0.0 1.7 %shard_map.82.after.refs_0_ = bf16[2,8,2048]{2,1,0:T(8,128)(2,1)S(1)} custom-call(s32[8]{0:T(128)} %counts_in.1, s32[2]{0:T(128)} %slots_in.1, bf16[8,2,64,128]{3,2,1,0:T(8,128)(2,1)} %factors_in.1, f32[2,64,64]{2,1,0:T(8,128)} %output_inverse_in.1, f32[2,64,64]{2,1,0:T(8,128)} %input_inverse_in.1), custom_call_target="tpu_custom_call" | custom-call | tf_op jit(solution)/shard_map/pallas_call | solution.py:246
  1.8 5.1 %collective-permute-start.3 = (bf16[2,8,2048]{2,1,0:T(8,128)(2,1)S(1)}, bf16[2,8,2048]{2,1,0:T(8,128)(2,1)S(1)}, u32[]{:S(2)}, u32[]{:S(2)}) collective-permute-start(bf16[2,8,2048]{2,1,0:T(8,128)(2,1)S(1)} %shard_map.82.after.refs_0_), channel_id=1, source_target_pairs={{0,12},{1,11},{2,14},{3,9},{4,8},{5,15},{6,10},{7,13},{8,4},{9,3},... | collective-permute-start | bytes 196616 | tf_op jit(solution)/shard_map/ppermute | solution.py:36
  6.9 0.0 collective-permute-start.2
  6.9 0.6 %collective-permute-start.1 = (bf16[2,8,2048]{2,1,0:T(8,128)(2,1)S(1)}, bf16[2,8,2048]{2,1,0:T(8,128)(2,1)S(1)}, u32[]{:S(2)}, u32[]{:S(2)}) collective-permute-start(bf16[2,8,2048]{2,1,0:T(8,128)(2,1)S(1)} %shard_map.82.after.refs_0_), channel_id=1, source_target_pairs={{0,4},{1,7},{2,6},{3,5},{4,0},{5,3},{6,2},{7,1},{8,12},{9,15},{10,... | collective-permute-start | bytes 196616 | tf_op jit(solution)/shard_map/ppermute | solution.py:36
  7.5 0.7 %collective-permute-start = (bf16[2,8,2048]{2,1,0:T(8,128)(2,1)S(1)}, bf16[2,8,2048]{2,1,0:T(8,128)(2,1)S(1)}, u32[]{:S(2)}, u32[]{:S(2)}) collective-permute-start(bf16[2,8,2048]{2,1,0:T(8,128)(2,1)S(1)} %shard_map.82.after.refs_0_), channel_id=1, source_target_pairs={{1,3},{3,1},{5,7},{7,5},{9,11},{11,9},{13,15},{15,13},{17,19},{19,... | collective-permute-start | bytes 196616 | tf_op jit(solution)/shard_map/ppermute | solution.py:36
  8.2 1.9 %shard_map.83.refs_5_.refs_6_ = bf16[768,2048]{1,0:T(8,128)(2,1)S(1)} custom-call(bf16[768,2048]{1,0:T(8,128)(2,1)} %bitcast.1, bf16[2,8,2048]{2,1,0:T(8,128)(2,1)S(1)} %shard_map.82.after.refs_0_), custom_call_target="tpu_custom_call" | custom-call | bytes 6291456 | tf_op jit(solution)/shard_map/pallas_call | solution.py:273
  10.1 0.0 copy-start
  10.1 0.0 copy-start.1
  10.1 0.0 collective-permute-done.3.refs_4_
  10.1 3.0 %collective-permute-done.2.refs_3_ = bf16[2,8,2048]{2,1,0:T(8,128)(2,1)S(1)} collective-permute-done((bf16[2,8,2048]{2,1,0:T(8,128)(2,1)S(1)}, bf16[2,8,2048]{2,1,0:T(8,128)(2,1)S(1)}, u32[]{:S(2)}, u32[]{:S(2)}) %collective-permute-start.2) | collective-permute-done | bytes 65568 | tf_op jit(solution)/shard_map/ppermute | solution.py:36
  13.1 0.0 collective-permute-done.1.refs_2_
  13.1 0.0 collective-permute-done.refs_1_
  13.2 0.2 collective-permute-start.4
  13.3 1.2 %collective-permute-done.4.refs_5_ = bf16[4,8,2048]{2,1,0:T(8,128)(2,1)S(1)} collective-permute-done((bf16[4,8,2048]{2,1,0:T(8,128)(2,1)S(1)}, bf16[4,8,2048]{2,1,0:T(8,128)(2,1)S(1)}, u32[]{:S(2)}, u32[]{:S(2)}) %collective-permute-start.4) | collective-permute-done | bytes 131104 | tf_op jit(solution)/shard_map/ppermute | solution.py:36
  14.6 1.0 %shard_map.85 = (f32[16,768]{1,0:T(8,128)S(1)}, bf16[16,768]{1,0:T(8,128)(2,1)S(1)}, bf16[16,768]{1,0:T(8,128)(2,1)S(1)}, bf16[16,768]{1,0:T(8,128)(2,1)S(1)}) custom-call(bf16[2,8,2048]{2,1,0:T(8,128)(2,1)S(1)} %shard_map.82.after.refs_0_, bf16[2,8,2048]{2,1,0:T(8,128)(2,1)S(1)} %collective-permute-done.refs_1_, ...), custom_call_target="tpu_custom_call" | custom-call | flops 201326592 | bytes 3604480 | tf_op jit(solution)/shard_map/pallas_call | solution.py:309
  15.6 1.2 %collective-permute-start.5 = (bf16[16,768]{1,0:T(8,128)(2,1)S(1)}, bf16[16,768]{1,0:T(8,128)(2,1)S(1)}, u32[]{:S(2)}, u32[]{:S(2)}) collective-permute-start(bf16[16,768]{1,0:T(8,128)(2,1)S(1)} %get-tuple-element.10), channel_id=1, source_target_pairs={{0,2},{1,3},{2,0},{3,1},{4,6},{5,7},{6,4},{7,5},{8,10},{9,11},{10,... | collective-permute-start | bytes 73736 | tf_op jit(solution)/shard_map/ppermute | solution.py:36
  16.8 0.3 %collective-permute-start.6 = (bf16[16,768]{1,0:T(8,128)(2,1)S(1)}, bf16[16,768]{1,0:T(8,128)(2,1)S(1)}, u32[]{:S(2)}, u32[]{:S(2)}) collective-permute-start(bf16[16,768]{1,0:T(8,128)(2,1)S(1)} %get-tuple-element.11), channel_id=1, source_target_pairs={{0,3},{1,2},{2,1},{3,0},{4,7},{5,6},{6,5},{7,4},{8,11},{9,10},{10,... | collective-permute-start | bytes 73736 | tf_op jit(solution)/shard_map/ppermute | solution.py:36
  17.2 0.6 %collective-permute-start.7 = (bf16[16,768]{1,0:T(8,128)(2,1)S(1)}, bf16[16,768]{1,0:T(8,128)(2,1)S(1)}, u32[]{:S(2)}, u32[]{:S(2)}) collective-permute-start(bf16[16,768]{1,0:T(8,128)(2,1)S(1)} %get-tuple-element.12), channel_id=1, source_target_pairs={{0,1},{1,0},{2,3},{3,2},{4,5},{5,4},{6,7},{7,6},{8,9},{9,8},{10,11... | collective-permute-start | bytes 73736 | tf_op jit(solution)/shard_map/ppermute | solution.py:36
  17.8 1.7 %collective-permute-done.5 = bf16[16,768]{1,0:T(8,128)(2,1)S(1)} collective-permute-done((bf16[16,768]{1,0:T(8,128)(2,1)S(1)}, bf16[16,768]{1,0:T(8,128)(2,1)S(1)}, u32[]{:S(2)}, u32[]{:S(2)}) %collective-permute-start.5) | collective-permute-done | bytes 24608 | tf_op jit(solution)/shard_map/ppermute | solution.py:36
  19.5 0.7 %collective-permute-done.6 = bf16[16,768]{1,0:T(8,128)(2,1)S(1)} collective-permute-done((bf16[16,768]{1,0:T(8,128)(2,1)S(1)}, bf16[16,768]{1,0:T(8,128)(2,1)S(1)}, u32[]{:S(2)}, u32[]{:S(2)}) %collective-permute-start.6) | collective-permute-done | bytes 24608 | tf_op jit(solution)/shard_map/ppermute | solution.py:36
  20.2 0.0 collective-permute-done.7
  20.2 0.0 copy-done
  20.2 0.0 copy-done.1
  20.2 0.7 %add_select_fusion = f32[16,768]{1,0:T(8,128)} fusion(bf16[16,768]{1,0:T(8,128)(2,1)S(1)} %collective-permute-done.7, bf16[16,768]{1,0:T(8,128)(2,1)S(1)} %collective-permute-done.6, f32[16,768]{1,0:T(8,128)S(1)} %get-tuple-element.9, bf16[16,768]{1,0:T(8,128)(2,1)S(1)} %collective-permute-done.5, s32[768]{0:T(1024)S(1)} %copy-done, s32[16]{0:T(128)S(1)} %copy-done.1), kind=kLoop, calls=%fused_computation | loop fusion | flops 98304 | bytes 175168 | tf_op jit(solution)/shard_map/jit(_where)/select_n | solution.py:334
  (1 shorter events, 0.0 us)
Async XLA Ops:
  1.8 8.4 %collective-permute-start.3 = (bf16[2,8,2048]{2,1,0:T(8,128)(2,1)S(1)}, bf16[2,8,2048]{2,1,0:T(8,128)(2,1)S(1)}, u32[]{:S(2)}, u32[]{:S(2)}) collective-permute-start(bf16[2,8,2048]{2,1,0:T(8,128)(2,1)S(1)} %shard_map.82.after.refs_0_), channel_id=1, source_target_pairs={{0,12},{1,11},{2,14},{3,9},{4,8},{5,15},{6,10},{7,13},{8,4},{9,3},... | collective-permute-start | bytes 196616 | tf_op jit(solution)/shard_map/ppermute | solution.py:36
  6.9 6.3 %collective-permute-start.2 = (bf16[2,8,2048]{2,1,0:T(8,128)(2,1)S(1)}, bf16[2,8,2048]{2,1,0:T(8,128)(2,1)S(1)}, u32[]{:S(2)}, u32[]{:S(2)}) collective-permute-start(bf16[2,8,2048]{2,1,0:T(8,128)(2,1)S(1)} %shard_map.82.after.refs_0_), channel_id=1, source_target_pairs={{0,8},{1,15},{2,10},{3,13},{4,12},{5,11},{6,14},{7,9},{8,0},{9,7},... | collective-permute-start | bytes 196616 | tf_op jit(solution)/shard_map/ppermute | solution.py:36
  6.9 6.3 %collective-permute-start.1 = (bf16[2,8,2048]{2,1,0:T(8,128)(2,1)S(1)}, bf16[2,8,2048]{2,1,0:T(8,128)(2,1)S(1)}, u32[]{:S(2)}, u32[]{:S(2)}) collective-permute-start(bf16[2,8,2048]{2,1,0:T(8,128)(2,1)S(1)} %shard_map.82.after.refs_0_), channel_id=1, source_target_pairs={{0,4},{1,7},{2,6},{3,5},{4,0},{5,3},{6,2},{7,1},{8,12},{9,15},{10,... | collective-permute-start | bytes 196616 | tf_op jit(solution)/shard_map/ppermute | solution.py:36
  7.5 5.6 %collective-permute-start = (bf16[2,8,2048]{2,1,0:T(8,128)(2,1)S(1)}, bf16[2,8,2048]{2,1,0:T(8,128)(2,1)S(1)}, u32[]{:S(2)}, u32[]{:S(2)}) collective-permute-start(bf16[2,8,2048]{2,1,0:T(8,128)(2,1)S(1)} %shard_map.82.after.refs_0_), channel_id=1, source_target_pairs={{1,3},{3,1},{5,7},{7,5},{9,11},{11,9},{13,15},{15,13},{17,19},{19,... | collective-permute-start | bytes 196616 | tf_op jit(solution)/shard_map/ppermute | solution.py:36
  10.1 10.1 %copy-start = (s32[768]{0:T(1024)S(1)}, s32[768]{0:T(1024)}, u32[]{:S(2)}) copy-start(s32[768]{0:T(1024)} %param.12) | copy-start | bytes 9220
  10.1 10.1 %copy-start.1 = (s32[16]{0:T(128)S(1)}, s32[16]{0:T(128)}, u32[]{:S(2)}) copy-start(s32[16]{0:T(128)} %param.10) | copy-start | bytes 196
  13.2 1.4 %collective-permute-start.4 = (bf16[4,8,2048]{2,1,0:T(8,128)(2,1)S(1)}, bf16[4,8,2048]{2,1,0:T(8,128)(2,1)S(1)}, u32[]{:S(2)}, u32[]{:S(2)}) collective-permute-start(bf16[4,8,2048]{2,1,0:T(8,128)(2,1)S(1)} %shard_map.84), channel_id=1, source_target_pairs={{0,1},{1,0},{2,3},{3,2},{4,5},{5,4},{6,7},{7,6},{8,9},{9,8},{10,11... | collective-permute-start | bytes 393224 | tf_op jit(solution)/shard_map/ppermute | solution.py:36
  15.6 3.9 %collective-permute-start.5 = (bf16[16,768]{1,0:T(8,128)(2,1)S(1)}, bf16[16,768]{1,0:T(8,128)(2,1)S(1)}, u32[]{:S(2)}, u32[]{:S(2)}) collective-permute-start(bf16[16,768]{1,0:T(8,128)(2,1)S(1)} %get-tuple-element.10), channel_id=1, source_target_pairs={{0,2},{1,3},{2,0},{3,1},{4,6},{5,7},{6,4},{7,5},{8,10},{9,11},{10,... | collective-permute-start | bytes 73736 | tf_op jit(solution)/shard_map/ppermute | solution.py:36
  16.8 3.4 %collective-permute-start.6 = (bf16[16,768]{1,0:T(8,128)(2,1)S(1)}, bf16[16,768]{1,0:T(8,128)(2,1)S(1)}, u32[]{:S(2)}, u32[]{:S(2)}) collective-permute-start(bf16[16,768]{1,0:T(8,128)(2,1)S(1)} %get-tuple-element.11), channel_id=1, source_target_pairs={{0,3},{1,2},{2,1},{3,0},{4,7},{5,6},{6,5},{7,4},{8,11},{9,10},{10,... | collective-permute-start | bytes 73736 | tf_op jit(solution)/shard_map/ppermute | solution.py:36
  17.2 3.0 %collective-permute-start.7 = (bf16[16,768]{1,0:T(8,128)(2,1)S(1)}, bf16[16,768]{1,0:T(8,128)(2,1)S(1)}, u32[]{:S(2)}, u32[]{:S(2)}) collective-permute-start(bf16[16,768]{1,0:T(8,128)(2,1)S(1)} %get-tuple-element.12), channel_id=1, source_target_pairs={{0,1},{1,0},{2,3},{3,2},{4,5},{5,4},{6,7},{7,6},{8,9},{9,8},{10,11... | collective-permute-start | bytes 73736 | tf_op jit(solution)/shard_map/ppermute | solution.py:36

commit v16 on v13

--- a/solution.py
+++ b/solution.py
@@ -70,8 +70,8 @@
     small = ((slots_in, slots), (counts_in, counts))
     small += cut(input_inverse_in, input_inverse, input_inverse.shape[0])
     small += cut(output_inverse_in, output_inverse, output_inverse.shape[0])
+    late = start_copies(((factors_in, factors),), arrived, len(small))
     early = start_copies(small, arrived, 0)
-    late = start_copies(cut(factors_in, factors, factors.shape[0]), arrived, len(small))
 
     examples, modules, tokens, width = factors.shape
     features = width // 2
@@ -247,7 +247,7 @@
             pltpu.VMEM(new_factors.shape, jnp.bfloat16),
             pltpu.VMEM(output_inverse.shape, jnp.float32),
             pltpu.VMEM(input_inverse.shape, jnp.float32),
-            pltpu.SemaphoreType.DMA((2 + 2 * module_count + examples,)),
+            pltpu.SemaphoreType.DMA((3 + 2 * module_count,)),
         ],
         compiler_params=pltpu.CompilerParams(vmem_limit_bytes=16 * 2**20),
     )(*[pltpu.with_memory_space_constraint(operand, pltpu.HBM) for operand in operands])

time: 21 us -> 20.9 us (level)
  no operation moved by 1% of the time
where the time goes in v16:
time: 20.9 us; the launch traced here: 20.8 us
  starting transfers between devices  9.19 us (44%)
  waiting for transfers between devices  6.11 us (29%)
  Pallas kernels  4.69 us (22%)
  other arithmetic  0.69 us (3%)
    ppermute x8, starting transfers between devices, exchange(): return lax.ppermute(value, names, pairs)  9.19 us
    ppermute x8, waiting for transfers between devices, exchange(): return lax.ppermute(value, names, pairs)  6.11 us
    pallas_call x1, Pallas kernels, body(): pl.pallas_call(copy_kernel, out_shape=pltpu.VMEM((replay_total, depth), j...  1.9 us
    pallas_call x1, Pallas kernels, body(): pl.pallas_call(precondition_kernel, out_shape=[pltpu.VMEM((half_count, ex...  1.75 us
    pallas_call x1, Pallas kernels, body(): pl.pallas_call(functools.partial(score_kernel, sources, counts), out_shap...  1.03 us
    select_n x1, other arithmetic, body(): return jnp.where(self_pairs, jnp.zeros((), jnp.float32), summed_scores)  0.69 us
  transfers between devices with their start and end apart: 8, of which 4 were waited for; matrix products, arithmetic and copies ran while one was open for 0% of the time, Pallas kernels for 9%

profile of v16, /device:TPU:0, one launch (start us, length us, event | category | flops | bytes accessed | tf_op | source)
XLA Modules:
  0.0 20.8 jit_solution(10097121616087316434)
XLA Ops:
  0.0 1.8 %shard_map.82.after.refs_0_ = bf16[2,8,2048]{2,1,0:T(8,128)(2,1)S(1)} custom-call(s32[8]{0:T(128)} %counts_in.1, s32[2]{0:T(128)} %slots_in.1, bf16[8,2,64,128]{3,2,1,0:T(8,128)(2,1)} %factors_in.1, f32[2,64,64]{2,1,0:T(8,128)} %output_inverse_in.1, f32[2,64,64]{2,1,0:T(8,128)} %input_inverse_in.1), custom_call_target="tpu_custom_call" | custom-call | tf_op jit(solution)/shard_map/pallas_call | solution.py:239
  1.8 5.1 %collective-permute-start.3 = (bf16[2,8,2048]{2,1,0:T(8,128)(2,1)S(1)}, bf16[2,8,2048]{2,1,0:T(8,128)(2,1)S(1)}, u32[]{:S(2)}, u32[]{:S(2)}) collective-permute-start(bf16[2,8,2048]{2,1,0:T(8,128)(2,1)S(1)} %shard_map.82.after.refs_0_), channel_id=1, source_target_pairs={{0,12},{1,15},{2,14},{3,13},{4,8},{5,11},{6,10},{7,9},{8,4},{9,7},... | collective-permute-start | bytes 196616 | tf_op jit(solution)/shard_map/ppermute | solution.py:36
  6.9 0.0 collective-permute-start.2
  6.9 0.6 %collective-permute-start.1 = (bf16[2,8,2048]{2,1,0:T(8,128)(2,1)S(1)}, bf16[2,8,2048]{2,1,0:T(8,128)(2,1)S(1)}, u32[]{:S(2)}, u32[]{:S(2)}) collective-permute-start(bf16[2,8,2048]{2,1,0:T(8,128)(2,1)S(1)} %shard_map.82.after.refs_0_), channel_id=1, source_target_pairs={{0,4},{1,7},{2,6},{3,5},{4,0},{5,3},{6,2},{7,1},{8,12},{9,15},{10,... | collective-permute-start | bytes 196616 | tf_op jit(solution)/shard_map/ppermute | solution.py:36
  7.5 0.7 %collective-permute-start = (bf16[2,8,2048]{2,1,0:T(8,128)(2,1)S(1)}, bf16[2,8,2048]{2,1,0:T(8,128)(2,1)S(1)}, u32[]{:S(2)}, u32[]{:S(2)}) collective-permute-start(bf16[2,8,2048]{2,1,0:T(8,128)(2,1)S(1)} %shard_map.82.after.refs_0_), channel_id=1, source_target_pairs={{1,3},{3,1},{5,7},{7,5},{9,11},{11,9},{13,15},{15,13},{17,19},{19,... | collective-permute-start | bytes 196616 | tf_op jit(solution)/shard_map/ppermute | solution.py:36
  8.2 1.9 %shard_map.83.refs_5_.refs_6_ = bf16[768,2048]{1,0:T(8,128)(2,1)S(1)} custom-call(bf16[768,2048]{1,0:T(8,128)(2,1)} %bitcast.1, bf16[2,8,2048]{2,1,0:T(8,128)(2,1)S(1)} %shard_map.82.after.refs_0_), custom_call_target="tpu_custom_call" | custom-call | bytes 6291456 | tf_op jit(solution)/shard_map/pallas_call | solution.py:263
  10.1 0.0 copy-start
  10.1 0.0 copy-start.1
  10.1 0.0 collective-permute-done.3.refs_4_
  10.1 3.1 %collective-permute-done.2.refs_3_ = bf16[2,8,2048]{2,1,0:T(8,128)(2,1)S(1)} collective-permute-done((bf16[2,8,2048]{2,1,0:T(8,128)(2,1)S(1)}, bf16[2,8,2048]{2,1,0:T(8,128)(2,1)S(1)}, u32[]{:S(2)}, u32[]{:S(2)}) %collective-permute-start.2) | collective-permute-done | bytes 65568 | tf_op jit(solution)/shard_map/ppermute | solution.py:36
  13.3 0.0 collective-permute-done.1.refs_2_
  13.3 0.0 collective-permute-done.refs_1_
  13.3 0.6 %collective-permute-start.4 = (bf16[4,8,2048]{2,1,0:T(8,128)(2,1)S(1)}, bf16[4,8,2048]{2,1,0:T(8,128)(2,1)S(1)}, u32[]{:S(2)}, u32[]{:S(2)}) collective-permute-start(bf16[4,8,2048]{2,1,0:T(8,128)(2,1)S(1)} %shard_map.84), channel_id=1, source_target_pairs={{0,1},{1,0},{2,3},{3,2},{4,5},{5,4},{6,7},{7,6},{8,9},{9,8},{10,11... | collective-permute-start | bytes 393224 | tf_op jit(solution)/shard_map/ppermute | solution.py:36
  13.8 1.0 %collective-permute-done.4.refs_5_ = bf16[4,8,2048]{2,1,0:T(8,128)(2,1)S(1)} collective-permute-done((bf16[4,8,2048]{2,1,0:T(8,128)(2,1)S(1)}, bf16[4,8,2048]{2,1,0:T(8,128)(2,1)S(1)}, u32[]{:S(2)}, u32[]{:S(2)}) %collective-permute-start.4) | collective-permute-done | bytes 131104 | tf_op jit(solution)/shard_map/ppermute | solution.py:36
  14.8 1.0 %shard_map.85 = (f32[16,768]{1,0:T(8,128)S(1)}, bf16[16,768]{1,0:T(8,128)(2,1)S(1)}, bf16[16,768]{1,0:T(8,128)(2,1)S(1)}, bf16[16,768]{1,0:T(8,128)(2,1)S(1)}) custom-call(bf16[2,8,2048]{2,1,0:T(8,128)(2,1)S(1)} %shard_map.82.after.refs_0_, bf16[2,8,2048]{2,1,0:T(8,128)(2,1)S(1)} %collective-permute-done.refs_1_, ...), custom_call_target="tpu_custom_call" | custom-call | flops 201326592 | bytes 3604480 | tf_op jit(solution)/shard_map/pallas_call | solution.py:299
  15.9 0.9 %collective-permute-start.5 = (bf16[16,768]{1,0:T(8,128)(2,1)S(1)}, bf16[16,768]{1,0:T(8,128)(2,1)S(1)}, u32[]{:S(2)}, u32[]{:S(2)}) collective-permute-start(bf16[16,768]{1,0:T(8,128)(2,1)S(1)} %get-tuple-element.10), channel_id=1, source_target_pairs={{0,2},{1,3},{2,0},{3,1},{4,6},{5,7},{6,4},{7,5},{8,10},{9,11},{10,... | collective-permute-start | bytes 73736 | tf_op jit(solution)/shard_map/ppermute | solution.py:36
  16.8 0.9 %collective-permute-start.6 = (bf16[16,768]{1,0:T(8,128)(2,1)S(1)}, bf16[16,768]{1,0:T(8,128)(2,1)S(1)}, u32[]{:S(2)}, u32[]{:S(2)}) collective-permute-start(bf16[16,768]{1,0:T(8,128)(2,1)S(1)} %get-tuple-element.11), channel_id=1, source_target_pairs={{0,3},{1,2},{2,1},{3,0},{4,7},{5,6},{6,5},{7,4},{8,11},{9,10},{10,... | collective-permute-start | bytes 73736 | tf_op jit(solution)/shard_map/ppermute | solution.py:36
  17.6 0.4 %collective-permute-start.7 = (bf16[16,768]{1,0:T(8,128)(2,1)S(1)}, bf16[16,768]{1,0:T(8,128)(2,1)S(1)}, u32[]{:S(2)}, u32[]{:S(2)}) collective-permute-start(bf16[16,768]{1,0:T(8,128)(2,1)S(1)} %get-tuple-element.12), channel_id=1, source_target_pairs={{0,1},{1,0},{2,3},{3,2},{4,5},{5,4},{6,7},{7,6},{8,9},{9,8},{10,11... | collective-permute-start | bytes 73736 | tf_op jit(solution)/shard_map/ppermute | solution.py:36
  18.1 1.7 %collective-permute-done.5 = bf16[16,768]{1,0:T(8,128)(2,1)S(1)} collective-permute-done((bf16[16,768]{1,0:T(8,128)(2,1)S(1)}, bf16[16,768]{1,0:T(8,128)(2,1)S(1)}, u32[]{:S(2)}, u32[]{:S(2)}) %collective-permute-start.5) | collective-permute-done | bytes 24608 | tf_op jit(solution)/shard_map/ppermute | solution.py:36
  19.8 0.3 %collective-permute-done.6 = bf16[16,768]{1,0:T(8,128)(2,1)S(1)} collective-permute-done((bf16[16,768]{1,0:T(8,128)(2,1)S(1)}, bf16[16,768]{1,0:T(8,128)(2,1)S(1)}, u32[]{:S(2)}, u32[]{:S(2)}) %collective-permute-start.6) | collective-permute-done | bytes 24608 | tf_op jit(solution)/shard_map/ppermute | solution.py:36
  20.1 0.0 collective-permute-done.7
  20.1 0.0 copy-done
  20.1 0.0 copy-done.1
  20.1 0.7 %add_select_fusion = f32[16,768]{1,0:T(8,128)} fusion(bf16[16,768]{1,0:T(8,128)(2,1)S(1)} %collective-permute-done.7, bf16[16,768]{1,0:T(8,128)(2,1)S(1)} %collective-permute-done.6, f32[16,768]{1,0:T(8,128)S(1)} %get-tuple-element.9, bf16[16,768]{1,0:T(8,128)(2,1)S(1)} %collective-permute-done.5, s32[768]{0:T(1024)S(1)} %copy-done, s32[16]{0:T(128)S(1)} %copy-done.1), kind=kLoop, calls=%fused_computation | loop fusion | flops 98304 | bytes 175168 | tf_op jit(solution)/shard_map/jit(_where)/select_n | solution.py:324
  (1 shorter events, 0.0 us)
Async XLA Ops:
  1.8 8.4 %collective-permute-start.3 = (bf16[2,8,2048]{2,1,0:T(8,128)(2,1)S(1)}, bf16[2,8,2048]{2,1,0:T(8,128)(2,1)S(1)}, u32[]{:S(2)}, u32[]{:S(2)}) collective-permute-start(bf16[2,8,2048]{2,1,0:T(8,128)(2,1)S(1)} %shard_map.82.after.refs_0_), channel_id=1, source_target_pairs={{0,12},{1,15},{2,14},{3,13},{4,8},{5,11},{6,10},{7,9},{8,4},{9,7},... | collective-permute-start | bytes 196616 | tf_op jit(solution)/shard_map/ppermute | solution.py:36
  6.9 6.4 %collective-permute-start.2 = (bf16[2,8,2048]{2,1,0:T(8,128)(2,1)S(1)}, bf16[2,8,2048]{2,1,0:T(8,128)(2,1)S(1)}, u32[]{:S(2)}, u32[]{:S(2)}) collective-permute-start(bf16[2,8,2048]{2,1,0:T(8,128)(2,1)S(1)} %shard_map.82.after.refs_0_), channel_id=1, source_target_pairs={{0,8},{1,11},{2,10},{3,9},{4,12},{5,15},{6,14},{7,13},{8,0},{9,3},... | collective-permute-start | bytes 196616 | tf_op jit(solution)/shard_map/ppermute | solution.py:36
  6.9 6.4 %collective-permute-start.1 = (bf16[2,8,2048]{2,1,0:T(8,128)(2,1)S(1)}, bf16[2,8,2048]{2,1,0:T(8,128)(2,1)S(1)}, u32[]{:S(2)}, u32[]{:S(2)}) collective-permute-start(bf16[2,8,2048]{2,1,0:T(8,128)(2,1)S(1)} %shard_map.82.after.refs_0_), channel_id=1, source_target_pairs={{0,4},{1,7},{2,6},{3,5},{4,0},{5,3},{6,2},{7,1},{8,12},{9,15},{10,... | collective-permute-start | bytes 196616 | tf_op jit(solution)/shard_map/ppermute | solution.py:36
  7.5 5.7 %collective-permute-start = (bf16[2,8,2048]{2,1,0:T(8,128)(2,1)S(1)}, bf16[2,8,2048]{2,1,0:T(8,128)(2,1)S(1)}, u32[]{:S(2)}, u32[]{:S(2)}) collective-permute-start(bf16[2,8,2048]{2,1,0:T(8,128)(2,1)S(1)} %shard_map.82.after.refs_0_), channel_id=1, source_target_pairs={{1,3},{3,1},{5,7},{7,5},{9,11},{11,9},{13,15},{15,13},{17,19},{19,... | collective-permute-start | bytes 196616 | tf_op jit(solution)/shard_map/ppermute | solution.py:36
  10.1 10.0 %copy-start = (s32[768]{0:T(1024)S(1)}, s32[768]{0:T(1024)}, u32[]{:S(2)}) copy-start(s32[768]{0:T(1024)} %param.12) | copy-start | bytes 9220
  10.1 10.0 %copy-start.1 = (s32[16]{0:T(128)S(1)}, s32[16]{0:T(128)}, u32[]{:S(2)}) copy-start(s32[16]{0:T(128)} %param.10) | copy-start | bytes 196
  13.3 1.5 %collective-permute-start.4 = (bf16[4,8,2048]{2,1,0:T(8,128)(2,1)S(1)}, bf16[4,8,2048]{2,1,0:T(8,128)(2,1)S(1)}, u32[]{:S(2)}, u32[]{:S(2)}) collective-permute-start(bf16[4,8,2048]{2,1,0:T(8,128)(2,1)S(1)} %shard_map.84), channel_id=1, source_target_pairs={{0,1},{1,0},{2,3},{3,2},{4,5},{5,4},{6,7},{7,6},{8,9},{9,8},{10,11... | collective-permute-start | bytes 393224 | tf_op jit(solution)/shard_map/ppermute | solution.py:36
  15.9 3.9 %collective-permute-start.5 = (bf16[16,768]{1,0:T(8,128)(2,1)S(1)}, bf16[16,768]{1,0:T(8,128)(2,1)S(1)}, u32[]{:S(2)}, u32[]{:S(2)}) collective-permute-start(bf16[16,768]{1,0:T(8,128)(2,1)S(1)} %get-tuple-element.10), channel_id=1, source_target_pairs={{0,2},{1,3},{2,0},{3,1},{4,6},{5,7},{6,4},{7,5},{8,10},{9,11},{10,... | collective-permute-start | bytes 73736 | tf_op jit(solution)/shard_map/ppermute | solution.py:36
  16.8 3.3 %collective-permute-start.6 = (bf16[16,768]{1,0:T(8,128)(2,1)S(1)}, bf16[16,768]{1,0:T(8,128)(2,1)S(1)}, u32[]{:S(2)}, u32[]{:S(2)}) collective-permute-start(bf16[16,768]{1,0:T(8,128)(2,1)S(1)} %get-tuple-element.11), channel_id=1, source_target_pairs={{0,3},{1,2},{2,1},{3,0},{4,7},{5,6},{6,5},{7,4},{8,11},{9,10},{10,... | collective-permute-start | bytes 73736 | tf_op jit(solution)/shard_map/ppermute | solution.py:36
  17.6 2.4 %collective-permute-start.7 = (bf16[16,768]{1,0:T(8,128)(2,1)S(1)}, bf16[16,768]{1,0:T(8,128)(2,1)S(1)}, u32[]{:S(2)}, u32[]{:S(2)}) collective-permute-start(bf16[16,768]{1,0:T(8,128)(2,1)S(1)} %get-tuple-element.12), channel_id=1, source_target_pairs={{0,1},{1,0},{2,3},{3,2},{4,5},{5,4},{6,7},{7,6},{8,9},{9,8},{10,11... | collective-permute-start | bytes 73736 | tf_op jit(solution)/shard_map/ppermute | solution.py:36

commit v17 on v16

--- a/solution.py
+++ b/solution.py
@@ -174,11 +174,11 @@
     for group in range(joined.shape[0]):
         joined[group] = jnp.concatenate(
             [
-                block.astype(jnp.float32)
+                block
                 for block in blocks[group * per_group : (group + 1) * per_group]
             ],
             axis=0,
-        ).astype(jnp.bfloat16)
+        )
 
     def place_of(number):
         replay_step, turn, half_step = sources[number]

time: 20.9 us -> 20.9 us (level)
  no operation moved by 1% of the time
where the time goes in v17:
time: 20.9 us; the launch traced here: 20.8 us
  starting transfers between devices  9.19 us (44%)
  waiting for transfers between devices  6.1 us (29%)
  Pallas kernels  4.69 us (22%)
  other arithmetic  0.69 us (3%)
    ppermute x8, starting transfers between devices, exchange(): return lax.ppermute(value, names, pairs)  9.19 us
    ppermute x8, waiting for transfers between devices, exchange(): return lax.ppermute(value, names, pairs)  6.1 us
    pallas_call x1, Pallas kernels, body(): pl.pallas_call(copy_kernel, out_shape=pltpu.VMEM((replay_total, depth), j...  1.9 us
    pallas_call x1, Pallas kernels, body(): pl.pallas_call(precondition_kernel, out_shape=[pltpu.VMEM((half_count, ex...  1.75 us
    pallas_call x1, Pallas kernels, body(): pl.pallas_call(functools.partial(score_kernel, sources, counts), out_shap...  1.03 us
    select_n x1, other arithmetic, body(): return jnp.where(self_pairs, jnp.zeros((), jnp.float32), summed_scores)  0.69 us
  transfers between devices with their start and end apart: 8, of which 4 were waited for; matrix products, arithmetic and copies ran while one was open for 0% of the time, Pallas kernels for 9%

profile of v17, /device:TPU:0, one launch (start us, length us, event | category | flops | bytes accessed | tf_op | source)
XLA Modules:
  0.0 20.8 jit_solution(6467459449097476758)
XLA Ops:
  0.0 1.8 %shard_map.82.after.refs_0_ = bf16[2,8,2048]{2,1,0:T(8,128)(2,1)S(1)} custom-call(s32[8]{0:T(128)} %counts_in.1, s32[2]{0:T(128)} %slots_in.1, bf16[8,2,64,128]{3,2,1,0:T(8,128)(2,1)} %factors_in.1, f32[2,64,64]{2,1,0:T(8,128)} %output_inverse_in.1, f32[2,64,64]{2,1,0:T(8,128)} %input_inverse_in.1), custom_call_target="tpu_custom_call" | custom-call | tf_op jit(solution)/shard_map/pallas_call | solution.py:239
  1.8 5.1 %collective-permute-start.3 = (bf16[2,8,2048]{2,1,0:T(8,128)(2,1)S(1)}, bf16[2,8,2048]{2,1,0:T(8,128)(2,1)S(1)}, u32[]{:S(2)}, u32[]{:S(2)}) collective-permute-start(bf16[2,8,2048]{2,1,0:T(8,128)(2,1)S(1)} %shard_map.82.after.refs_0_), channel_id=1, source_target_pairs={{0,12},{1,15},{2,14},{3,13},{4,8},{5,11},{6,10},{7,9},{8,4},{9,7},... | collective-permute-start | bytes 196616 | tf_op jit(solution)/shard_map/ppermute | solution.py:36
  6.9 0.0 collective-permute-start.2
  6.9 0.6 %collective-permute-start.1 = (bf16[2,8,2048]{2,1,0:T(8,128)(2,1)S(1)}, bf16[2,8,2048]{2,1,0:T(8,128)(2,1)S(1)}, u32[]{:S(2)}, u32[]{:S(2)}) collective-permute-start(bf16[2,8,2048]{2,1,0:T(8,128)(2,1)S(1)} %shard_map.82.after.refs_0_), channel_id=1, source_target_pairs={{0,4},{1,7},{2,6},{3,5},{4,0},{5,3},{6,2},{7,1},{8,12},{9,15},{10,... | collective-permute-start | bytes 196616 | tf_op jit(solution)/shard_map/ppermute | solution.py:36
  7.5 0.7 %collective-permute-start = (bf16[2,8,2048]{2,1,0:T(8,128)(2,1)S(1)}, bf16[2,8,2048]{2,1,0:T(8,128)(2,1)S(1)}, u32[]{:S(2)}, u32[]{:S(2)}) collective-permute-start(bf16[2,8,2048]{2,1,0:T(8,128)(2,1)S(1)} %shard_map.82.after.refs_0_), channel_id=1, source_target_pairs={{1,3},{3,1},{5,7},{7,5},{9,11},{11,9},{13,15},{15,13},{17,19},{19,... | collective-permute-start | bytes 196616 | tf_op jit(solution)/shard_map/ppermute | solution.py:36
  8.2 1.9 %shard_map.83.refs_5_.refs_6_ = bf16[768,2048]{1,0:T(8,128)(2,1)S(1)} custom-call(bf16[768,2048]{1,0:T(8,128)(2,1)} %bitcast.1, bf16[2,8,2048]{2,1,0:T(8,128)(2,1)S(1)} %shard_map.82.after.refs_0_), custom_call_target="tpu_custom_call" | custom-call | bytes 6291456 | tf_op jit(solution)/shard_map/pallas_call | solution.py:263
  10.1 0.0 copy-start
  10.1 0.0 copy-start.1
  10.1 0.0 collective-permute-done.3.refs_4_
  10.1 3.1 %collective-permute-done.2.refs_3_ = bf16[2,8,2048]{2,1,0:T(8,128)(2,1)S(1)} collective-permute-done((bf16[2,8,2048]{2,1,0:T(8,128)(2,1)S(1)}, bf16[2,8,2048]{2,1,0:T(8,128)(2,1)S(1)}, u32[]{:S(2)}, u32[]{:S(2)}) %collective-permute-start.2) | collective-permute-done | bytes 65568 | tf_op jit(solution)/shard_map/ppermute | solution.py:36
  13.3 0.0 collective-permute-done.1.refs_2_
  13.3 0.0 collective-permute-done.refs_1_
  13.3 0.6 %collective-permute-start.4 = (bf16[4,8,2048]{2,1,0:T(8,128)(2,1)S(1)}, bf16[4,8,2048]{2,1,0:T(8,128)(2,1)S(1)}, u32[]{:S(2)}, u32[]{:S(2)}) collective-permute-start(bf16[4,8,2048]{2,1,0:T(8,128)(2,1)S(1)} %shard_map.84), channel_id=1, source_target_pairs={{0,1},{1,0},{2,3},{3,2},{4,5},{5,4},{6,7},{7,6},{8,9},{9,8},{10,11... | collective-permute-start | bytes 393224 | tf_op jit(solution)/shard_map/ppermute | solution.py:36
  13.8 1.0 %collective-permute-done.4.refs_5_ = bf16[4,8,2048]{2,1,0:T(8,128)(2,1)S(1)} collective-permute-done((bf16[4,8,2048]{2,1,0:T(8,128)(2,1)S(1)}, bf16[4,8,2048]{2,1,0:T(8,128)(2,1)S(1)}, u32[]{:S(2)}, u32[]{:S(2)}) %collective-permute-start.4) | collective-permute-done | bytes 131104 | tf_op jit(solution)/shard_map/ppermute | solution.py:36
  14.8 1.0 %shard_map.85 = (f32[16,768]{1,0:T(8,128)S(1)}, bf16[16,768]{1,0:T(8,128)(2,1)S(1)}, bf16[16,768]{1,0:T(8,128)(2,1)S(1)}, bf16[16,768]{1,0:T(8,128)(2,1)S(1)}) custom-call(bf16[2,8,2048]{2,1,0:T(8,128)(2,1)S(1)} %shard_map.82.after.refs_0_, bf16[2,8,2048]{2,1,0:T(8,128)(2,1)S(1)} %collective-permute-done.refs_1_, ...), custom_call_target="tpu_custom_call" | custom-call | flops 201326592 | bytes 3604480 | tf_op jit(solution)/shard_map/pallas_call | solution.py:299
  15.9 0.9 %collective-permute-start.5 = (bf16[16,768]{1,0:T(8,128)(2,1)S(1)}, bf16[16,768]{1,0:T(8,128)(2,1)S(1)}, u32[]{:S(2)}, u32[]{:S(2)}) collective-permute-start(bf16[16,768]{1,0:T(8,128)(2,1)S(1)} %get-tuple-element.10), channel_id=1, source_target_pairs={{0,2},{1,3},{2,0},{3,1},{4,6},{5,7},{6,4},{7,5},{8,10},{9,11},{10,... | collective-permute-start | bytes 73736 | tf_op jit(solution)/shard_map/ppermute | solution.py:36
  16.8 0.9 %collective-permute-start.6 = (bf16[16,768]{1,0:T(8,128)(2,1)S(1)}, bf16[16,768]{1,0:T(8,128)(2,1)S(1)}, u32[]{:S(2)}, u32[]{:S(2)}) collective-permute-start(bf16[16,768]{1,0:T(8,128)(2,1)S(1)} %get-tuple-element.11), channel_id=1, source_target_pairs={{0,3},{1,2},{2,1},{3,0},{4,7},{5,6},{6,5},{7,4},{8,11},{9,10},{10,... | collective-permute-start | bytes 73736 | tf_op jit(solution)/shard_map/ppermute | solution.py:36
  17.6 0.4 %collective-permute-start.7 = (bf16[16,768]{1,0:T(8,128)(2,1)S(1)}, bf16[16,768]{1,0:T(8,128)(2,1)S(1)}, u32[]{:S(2)}, u32[]{:S(2)}) collective-permute-start(bf16[16,768]{1,0:T(8,128)(2,1)S(1)} %get-tuple-element.12), channel_id=1, source_target_pairs={{0,1},{1,0},{2,3},{3,2},{4,5},{5,4},{6,7},{7,6},{8,9},{9,8},{10,11... | collective-permute-start | bytes 73736 | tf_op jit(solution)/shard_map/ppermute | solution.py:36
  18.1 1.7 %collective-permute-done.5 = bf16[16,768]{1,0:T(8,128)(2,1)S(1)} collective-permute-done((bf16[16,768]{1,0:T(8,128)(2,1)S(1)}, bf16[16,768]{1,0:T(8,128)(2,1)S(1)}, u32[]{:S(2)}, u32[]{:S(2)}) %collective-permute-start.5) | collective-permute-done | bytes 24608 | tf_op jit(solution)/shard_map/ppermute | solution.py:36
  19.8 0.3 %collective-permute-done.6 = bf16[16,768]{1,0:T(8,128)(2,1)S(1)} collective-permute-done((bf16[16,768]{1,0:T(8,128)(2,1)S(1)}, bf16[16,768]{1,0:T(8,128)(2,1)S(1)}, u32[]{:S(2)}, u32[]{:S(2)}) %collective-permute-start.6) | collective-permute-done | bytes 24608 | tf_op jit(solution)/shard_map/ppermute | solution.py:36
  20.1 0.0 collective-permute-done.7
  20.1 0.0 copy-done
  20.1 0.0 copy-done.1
  20.1 0.7 %add_select_fusion = f32[16,768]{1,0:T(8,128)} fusion(bf16[16,768]{1,0:T(8,128)(2,1)S(1)} %collective-permute-done.7, bf16[16,768]{1,0:T(8,128)(2,1)S(1)} %collective-permute-done.6, f32[16,768]{1,0:T(8,128)S(1)} %get-tuple-element.9, bf16[16,768]{1,0:T(8,128)(2,1)S(1)} %collective-permute-done.5, s32[768]{0:T(1024)S(1)} %copy-done, s32[16]{0:T(128)S(1)} %copy-done.1), kind=kLoop, calls=%fused_computation | loop fusion | flops 98304 | bytes 175168 | tf_op jit(solution)/shard_map/jit(_where)/select_n | solution.py:324
  (1 shorter events, 0.0 us)
Async XLA Ops:
  1.8 8.4 %collective-permute-start.3 = (bf16[2,8,2048]{2,1,0:T(8,128)(2,1)S(1)}, bf16[2,8,2048]{2,1,0:T(8,128)(2,1)S(1)}, u32[]{:S(2)}, u32[]{:S(2)}) collective-permute-start(bf16[2,8,2048]{2,1,0:T(8,128)(2,1)S(1)} %shard_map.82.after.refs_0_), channel_id=1, source_target_pairs={{0,12},{1,15},{2,14},{3,13},{4,8},{5,11},{6,10},{7,9},{8,4},{9,7},... | collective-permute-start | bytes 196616 | tf_op jit(solution)/shard_map/ppermute | solution.py:36
  6.9 6.4 %collective-permute-start.2 = (bf16[2,8,2048]{2,1,0:T(8,128)(2,1)S(1)}, bf16[2,8,2048]{2,1,0:T(8,128)(2,1)S(1)}, u32[]{:S(2)}, u32[]{:S(2)}) collective-permute-start(bf16[2,8,2048]{2,1,0:T(8,128)(2,1)S(1)} %shard_map.82.after.refs_0_), channel_id=1, source_target_pairs={{0,8},{1,11},{2,10},{3,9},{4,12},{5,15},{6,14},{7,13},{8,0},{9,3},... | collective-permute-start | bytes 196616 | tf_op jit(solution)/shard_map/ppermute | solution.py:36
  6.9 6.4 %collective-permute-start.1 = (bf16[2,8,2048]{2,1,0:T(8,128)(2,1)S(1)}, bf16[2,8,2048]{2,1,0:T(8,128)(2,1)S(1)}, u32[]{:S(2)}, u32[]{:S(2)}) collective-permute-start(bf16[2,8,2048]{2,1,0:T(8,128)(2,1)S(1)} %shard_map.82.after.refs_0_), channel_id=1, source_target_pairs={{0,4},{1,7},{2,6},{3,5},{4,0},{5,3},{6,2},{7,1},{8,12},{9,15},{10,... | collective-permute-start | bytes 196616 | tf_op jit(solution)/shard_map/ppermute | solution.py:36
  7.5 5.7 %collective-permute-start = (bf16[2,8,2048]{2,1,0:T(8,128)(2,1)S(1)}, bf16[2,8,2048]{2,1,0:T(8,128)(2,1)S(1)}, u32[]{:S(2)}, u32[]{:S(2)}) collective-permute-start(bf16[2,8,2048]{2,1,0:T(8,128)(2,1)S(1)} %shard_map.82.after.refs_0_), channel_id=1, source_target_pairs={{1,3},{3,1},{5,7},{7,5},{9,11},{11,9},{13,15},{15,13},{17,19},{19,... | collective-permute-start | bytes 196616 | tf_op jit(solution)/shard_map/ppermute | solution.py:36
  10.1 10.0 %copy-start = (s32[768]{0:T(1024)S(1)}, s32[768]{0:T(1024)}, u32[]{:S(2)}) copy-start(s32[768]{0:T(1024)} %param.12) | copy-start | bytes 9220
  10.1 10.0 %copy-start.1 = (s32[16]{0:T(128)S(1)}, s32[16]{0:T(128)}, u32[]{:S(2)}) copy-start(s32[16]{0:T(128)} %param.10) | copy-start | bytes 196
  13.3 1.5 %collective-permute-start.4 = (bf16[4,8,2048]{2,1,0:T(8,128)(2,1)S(1)}, bf16[4,8,2048]{2,1,0:T(8,128)(2,1)S(1)}, u32[]{:S(2)}, u32[]{:S(2)}) collective-permute-start(bf16[4,8,2048]{2,1,0:T(8,128)(2,1)S(1)} %shard_map.84), channel_id=1, source_target_pairs={{0,1},{1,0},{2,3},{3,2},{4,5},{5,4},{6,7},{7,6},{8,9},{9,8},{10,11... | collective-permute-start | bytes 393224 | tf_op jit(solution)/shard_map/ppermute | solution.py:36
  15.9 3.9 %collective-permute-start.5 = (bf16[16,768]{1,0:T(8,128)(2,1)S(1)}, bf16[16,768]{1,0:T(8,128)(2,1)S(1)}, u32[]{:S(2)}, u32[]{:S(2)}) collective-permute-start(bf16[16,768]{1,0:T(8,128)(2,1)S(1)} %get-tuple-element.10), channel_id=1, source_target_pairs={{0,2},{1,3},{2,0},{3,1},{4,6},{5,7},{6,4},{7,5},{8,10},{9,11},{10,... | collective-permute-start | bytes 73736 | tf_op jit(solution)/shard_map/ppermute | solution.py:36
  16.8 3.3 %collective-permute-start.6 = (bf16[16,768]{1,0:T(8,128)(2,1)S(1)}, bf16[16,768]{1,0:T(8,128)(2,1)S(1)}, u32[]{:S(2)}, u32[]{:S(2)}) collective-permute-start(bf16[16,768]{1,0:T(8,128)(2,1)S(1)} %get-tuple-element.11), channel_id=1, source_target_pairs={{0,3},{1,2},{2,1},{3,0},{4,7},{5,6},{6,5},{7,4},{8,11},{9,10},{10,... | collective-permute-start | bytes 73736 | tf_op jit(solution)/shard_map/ppermute | solution.py:36
  17.6 2.4 %collective-permute-start.7 = (bf16[16,768]{1,0:T(8,128)(2,1)S(1)}, bf16[16,768]{1,0:T(8,128)(2,1)S(1)}, u32[]{:S(2)}, u32[]{:S(2)}) collective-permute-start(bf16[16,768]{1,0:T(8,128)(2,1)S(1)} %get-tuple-element.12), channel_id=1, source_target_pairs={{0,1},{1,0},{2,3},{3,2},{4,5},{5,4},{6,7},{7,6},{8,9},{9,8},{10,11... | collective-permute-start | bytes 73736 | tf_op jit(solution)/shard_map/ppermute | solution.py:36
